TPU v7x, 32 devices: a whole 2x2x4 slice. The times are simulated.
32 devices in a mesh: ckpt: 2 (over x), fsdp: 16 (over z, y, core).
Axes of the slice: x: 2, y: 2, z: 4, core: 2. Of those that a mesh axis runs over, the one named last changes fastest.
Arguments:
- tokens: bfloat16 [2, 128, 4096], P('ckpt', 'fsdp'), may hold values from -6 to 6
- gate_weight: bfloat16 [2, 14336, 4096], P('ckpt', 'fsdp'), may hold values from -6 to 6
- up_weight: bfloat16 [2, 14336, 4096], P('ckpt', 'fsdp'), may hold values from -6 to 6
- down_weight: bfloat16 [2, 14336, 4096], P('ckpt', 'fsdp'), may hold values from -0.046875 to 0.046875
- row_code: int32 [2, 2, 4096], P('ckpt'), may hold values from 0 to 2097151
- col_code: int32 [2, 2, 14336], P('ckpt', None, 'fsdp'), may hold values from 0 to 2097151
Outputs:
- merged_gate: bfloat16 [14336, 4096], P('fsdp', 'ckpt')
- merged_up: bfloat16 [14336, 4096], P('fsdp', 'ckpt')
All inputs are finite; a program needn't handle non-finite values.
Results may differ from a plain program's by a relative error of at most 0.028.
Values may be sent and summed in bfloat16 or wider, within the bound.
No kernel may reach another device: no remote copies, remote signals or barrier semaphores. Data moves between devices by JAX's collectives and lax.ppermute only.
A program may use at most 128 MiB of HBM per device.

v0:
```python
import jax
import jax.numpy as jnp
from jax import lax
from jax.sharding import PartitionSpec as P


def odd_bits(value):
    for shift in (16, 8, 4, 2, 1):
        value = jnp.bitwise_xor(value, jnp.right_shift(value, shift))
    return jnp.bitwise_and(value, 1)


def probe(col, row):
    bits = odd_bits(jnp.bitwise_and(col[:, None], row[None, :]))
    return (1 - 2 * bits).astype(jnp.bfloat16)


def cross(left, right):
    return lax.dot_general(
        left, right, (((1,), (1,)), ((), ())), preferred_element_type=jnp.float32
    )


def inner(left, right):
    return lax.dot_general(
        left, right, (((0,), (0,)), ((), ())), preferred_element_type=jnp.float32
    )


def merge_weight(hessian, signs):
    magnitude = jnp.abs(signs.astype(jnp.float32) * hessian)
    return magnitude / (jnp.mean(magnitude, axis=1, keepdims=True) + 1e-06)


def finish(numer, denom):
    return (numer / jnp.maximum(denom, 1.0)).astype(jnp.bfloat16)


def on_device(tokens, gate_weight, up_weight, down_weight, row_code, col_code):
    gate = gate_weight[0]
    upper = up_weight[0]
    down = down_weight[0]
    whole = lax.all_gather(tokens[0], "fsdp", axis=0, tiled=True)
    factor = whole.shape[1] ** (-0.5)
    z_gate = probe(col_code[0, 0], row_code[0, 0])
    z_up = probe(col_code[0, 1], row_code[0, 1])
    a_pre = cross(gate, whole) * factor
    b_pre = cross(upper, whole) * factor
    da_pre = cross(z_gate, whole) * factor
    db_pre = cross(z_up, whole) * factor
    sigma = jax.nn.sigmoid(a_pre)
    act = a_pre * sigma
    slope = sigma * (1.0 + a_pre * (1.0 - sigma))
    curve = sigma * (1.0 - sigma) * (2.0 + a_pre * (1.0 - 2.0 * sigma))
    hidden = (act * b_pre).astype(jnp.bfloat16)
    d_hidden = (slope * da_pre * b_pre + act * db_pre).astype(jnp.bfloat16)
    term_y = inner(hidden, down)
    term_dy = inner(d_hidden, down)
    out_y, out_dy = (
        lax.psum(term_y.astype(jnp.bfloat16), "fsdp").astype(jnp.float32),
        lax.psum(term_dy.astype(jnp.bfloat16), "fsdp").astype(jnp.float32),
    )
    grad_y = out_y.astype(jnp.bfloat16)
    grad_dy = out_dy.astype(jnp.bfloat16)
    grad_h = cross(down, grad_y)
    grad_dh = cross(down, grad_dy)
    dga = (
        grad_dh * b_pre * slope + grad_h * db_pre * slope + grad_h * b_pre * curve * da_pre
    ).astype(jnp.bfloat16)
    dgb = (grad_dh * act + grad_h * slope * da_pre).astype(jnp.bfloat16)
    hz_gate = jnp.dot(dga, whole, preferred_element_type=jnp.float32)
    w_gate = merge_weight(hz_gate, z_gate)
    term_gate = w_gate * gate.astype(jnp.float32)
    hz_up = jnp.dot(dgb, whole, preferred_element_type=jnp.float32)
    w_up = merge_weight(hz_up, z_up)
    term_up = w_up * upper.astype(jnp.float32)
    numer_gate, denom_gate, numer_up, denom_up = (
        lax.psum_scatter(
            term_gate.astype(jnp.bfloat16), "ckpt", scatter_dimension=1, tiled=True
        ).astype(jnp.float32),
        lax.psum_scatter(
            w_gate.astype(jnp.bfloat16), "ckpt", scatter_dimension=1, tiled=True
        ).astype(jnp.float32),
        lax.psum_scatter(
            term_up.astype(jnp.bfloat16), "ckpt", scatter_dimension=1, tiled=True
        ).astype(jnp.float32),
        lax.psum_scatter(w_up.astype(jnp.bfloat16), "ckpt", scatter_dimension=1, tiled=True).astype(
            jnp.float32
        ),
    )
    return (finish(numer_gate, denom_gate), finish(numer_up, denom_up))


def solution(mesh):
    in_specs = (
        P("ckpt", "fsdp", None),
        P("ckpt", "fsdp", None),
        P("ckpt", "fsdp", None),
        P("ckpt", "fsdp", None),
        P("ckpt", None, None),
        P("ckpt", None, "fsdp"),
    )
    out_specs = (P("fsdp", "ckpt"), P("fsdp", "ckpt"))
    return jax.shard_map(
        on_device, mesh=mesh, in_specs=in_specs, out_specs=out_specs, check_vma=False
    )
```

profile of v0, /device:TPU:0, one launch (start us, length us, event | category | flops | bytes accessed | tf_op | source)
XLA Modules:
  0.0 612.7 jit_solution(1149976140707160135)
XLA Ops:
  7.2 0.0 all-gather.3.cloned.1.call-start
  7.2 0.7 all-gather.3.cloned.1.call-update
  7.9 0.0 all-reduce.3.cloned.1.call-start
  7.9 0.8 slice_reduce_fusion
  8.7 0.9 fusion.91
  9.6 41.2 %all-gather.3.cloned.1.call-done = bf16[1,128,4096]{2,1,0:T(8,128)(2,1)} async-done(((bf16[1,8,4096]{2,1,0:T(8,128)(2,1)}), bf16[1,128,4096]{2,1,0:T(8,128)(2,1)}) %all-gather.3.cloned.1.call-update) | async-done | bytes 1048592 | tf_op jit(solution)/shard_map/all_gather | solution.py:43
  50.8 5.5 fusion.46
  56.4 5.6 fusion.49
  62.0 2.3 fusion.31
  64.3 7.7 %fusion.43 = f32[896,128]{1,0:T(8,128)S(1)} fusion(s32[4096]{0:T(1024)S(1)} %bitcast.59, s32[896]{0:T(1024)S(1)} %get-tuple-element.3, bf16[1,128,4096]{2,1,0:T(8,128)(2,1)S(1)} %copy-done.10), kind=kOutput, calls=%fused_computation.47 | convolution fusion | flops 994689024 | bytes 1527296 | tf_op jit(solution)/shard_map/dot_general | solution.py:19
  72.0 7.5 %fusion.40 = f32[896,128]{1,0:T(8,128)S(1)} fusion(s32[4096]{0:T(1024)S(1)} %bitcast.56, s32[896]{0:T(1024)S(1)} %get-tuple-element.2, bf16[1,128,4096]{2,1,0:T(8,128)(2,1)S(1)} %copy-done.10), kind=kOutput, calls=%fused_computation.46 | convolution fusion | flops 994689024 | bytes 1527296 | tf_op jit(solution)/shard_map/dot_general | solution.py:19
  79.6 0.8 copy-done.8
  80.4 2.5 fusion.28
  82.9 0.4 reduce-scatter.9.cloned.1.call-start
  83.3 96.6 %all-reduce.3.cloned.1.call-done = (bf16[128,4096]{1,0:T(8,128)(2,1)}, bf16[128,4096]{1,0:T(8,128)(2,1)}) async-done(((bf16[128,4096]{1,0:T(8,128)(2,1)}, bf16[128,4096]{1,0:T(8,128)(2,1)}), (bf16[128,4096]{1,0:T(8,128)(2,1)}, bf16[128,4096]{1,0:T(8,128)(2,1)})) %all-reduce.3.cloned.1.call-update) | async-done | bytes 2097168 | tf_op jit(solution)/shard_map/psum | solution.py:60
  180.0 5.6 fusion.37
  185.6 2.1 fusion.34
  187.7 9.5 %fusion.9 = (f32[896]{0:T(1024)S(1)}, f32[896,4096]{1,0:T(8,128)S(1)}) fusion(s32[4096]{0:T(1024)S(1)} %bitcast.60, s32[896]{0:T(1024)S(1)} %get-tuple-element.3, bf16[1,128,4096]{2,1,0:T(8,128)(2,1)S(1)} %copy-done.11, f32[896,128]{1,0:T(8,128)S(1)} %copy-done.7, f32[896,128]{1,0:T(8,128)S(1)} %copy-done.3, f32[896,128]{1,0:T(8,128)S(1)} %fusion.37, ...), kind=kOutput, calls=%fused_computation.23 | convolution fusion | flops 1011776640 | bytes 18504704 | tf_op jit(solution)/shard_map/dot_general | solution.py:71
  197.2 13.0 %fusion.11 = (f32[896]{0:T(1024)S(1)}, f32[896,4096]{1,0:T(8,128)}) fusion(s32[4096]{0:T(1024)S(1)} %bitcast.57, s32[896]{0:T(1024)S(1)} %get-tuple-element.2, bf16[1,128,4096]{2,1,0:T(8,128)(2,1)S(1)} %copy-done.11, f32[896,128]{1,0:T(8,128)S(1)} %copy-done.7, f32[896,128]{1,0:T(8,128)S(1)} %fusion.37, f32[896,128]{1,0:T(8,128)S(1)} %fusion.34, ...), kind=kOutput, calls=%fused_computation.25 | convolution fusion | flops 1010744448 | bytes 17587200 | tf_op jit(solution)/shard_map/dot_general | solution.py:74
  210.2 28.3 %multiply_convert_fusion = (bf16[896,4096]{1,0:T(8,128)(2,1)}, bf16[896,4096]{1,0:T(8,128)(2,1)}, bf16[896,4096]{1,0:T(8,128)(2,1)}, bf16[896,4096]{1,0:T(8,128)(2,1)}) fusion(bf16[1,896,4096]{2,1,0:T(8,128)(2,1)} %param.8, f32[896]{0:T(1024)S(1)} %multiply_add_fusion, f32[896,4096]{1,0:T(8,128)} %get-tuple-element.15, s32[4096]{0:T(1024)S(1)} %bitcast.58, ...), kind=kLoop, calls=%fused_computation.16 | loop fusion | flops 168820736 | bytes 73447424 | tf_op jit(solution)/shard_map/convert_element_type | solution.py:85
  238.5 0.0 reduce-scatter.11.cloned.1.call-start
  238.5 0.5 reduce-scatter.11.cloned.1.call-update
  239.1 0.0 reduce-scatter.7.cloned.1.call-start
  239.1 0.5 reduce-scatter.7.cloned.1.call-update
  239.7 0.3 reduce-scatter.5.cloned.1.call-start
  239.9 0.3 reduce-scatter.5.cloned.1.call-update
  240.2 86.3 %reduce-scatter.9.cloned.1.call-done = bf16[896,2048]{1,0:T(8,128)(2,1)} async-done(((bf16[896,4096]{1,0:T(8,128)(2,1)}), bf16[896,2048]{1,0:T(8,128)(2,1)}) %reduce-scatter.9.cloned.1.call-update) | async-done | bytes 3670032 | tf_op jit(solution)/shard_map/reduce_scatter | solution.py:84
  326.6 90.6 %reduce-scatter.11.cloned.1.call-done = bf16[896,2048]{1,0:T(8,128)(2,1)} async-done(((bf16[896,4096]{1,0:T(8,128)(2,1)}), bf16[896,2048]{1,0:T(8,128)(2,1)}) %reduce-scatter.11.cloned.1.call-update) | async-done | bytes 3670032 | tf_op jit(solution)/shard_map/reduce_scatter | solution.py:87
  417.2 7.1 %divide_convert_fusion = bf16[896,2048]{1,0:T(8,128)(2,1)} fusion(bf16[896,2048]{1,0:T(8,128)(2,1)} %reduce-scatter.11.cloned.1.call-done, bf16[896,2048]{1,0:T(8,128)(2,1)} %reduce-scatter.9.cloned.1.call-done), kind=kLoop, calls=%fused_computation.38 | loop fusion | flops 9175040 | bytes 11010048 | tf_op jit(solution)/shard_map/convert_element_type | solution.py:36
  424.3 83.6 %reduce-scatter.7.cloned.1.call-done = bf16[896,2048]{1,0:T(8,128)(2,1)} async-done(((bf16[896,4096]{1,0:T(8,128)(2,1)}), bf16[896,2048]{1,0:T(8,128)(2,1)}) %reduce-scatter.7.cloned.1.call-update) | async-done | bytes 3670032 | tf_op jit(solution)/shard_map/reduce_scatter | solution.py:81
  507.9 90.6 %reduce-scatter.5.cloned.1.call-done = bf16[896,2048]{1,0:T(8,128)(2,1)} async-done(((bf16[896,4096]{1,0:T(8,128)(2,1)}), bf16[896,2048]{1,0:T(8,128)(2,1)}) %reduce-scatter.5.cloned.1.call-update) | async-done | bytes 3670032 | tf_op jit(solution)/shard_map/reduce_scatter | solution.py:78
  598.5 7.1 %divide_convert_fusion.1 = bf16[896,2048]{1,0:T(8,128)(2,1)} fusion(bf16[896,2048]{1,0:T(8,128)(2,1)} %reduce-scatter.7.cloned.1.call-done, bf16[896,2048]{1,0:T(8,128)(2,1)} %reduce-scatter.5.cloned.1.call-done), kind=kLoop, calls=%fused_computation.39 | loop fusion | flops 9175040 | bytes 11010048 | tf_op jit(solution)/shard_map/convert_element_type | solution.py:36
  (32 shorter events, 0.1 us)
Async XLA Ops:
  7.2 43.7 %all-gather.3.cloned.1.call-start = ((), (), s32[]{:S(2)}) async-start(), calls=%async_computation.8 | async-start | bytes 1114112 | tf_op jit(solution)/shard_map/all_gather | solution.py:43
  7.9 172.0 %all-reduce.3.cloned.1.call-start = ((), (), s32[]{:S(2)}) async-start(), calls=%async_computation.9 | async-start | bytes 4194304 | tf_op jit(solution)/shard_map/psum | solution.py:60
  50.8 11.1 %copy-start = (bf16[1,896,4096]{2,1,0:T(8,128)(2,1)S(1)}, bf16[1,896,4096]{2,1,0:T(8,128)(2,1)}, u32[]{:S(2)}) copy-start(bf16[1,896,4096]{2,1,0:T(8,128)(2,1)} %param.9) | copy-start | bytes 22020100
  56.4 23.2 %copy-start.2 = (f32[896,128]{1,0:T(8,128)}, f32[896,128]{1,0:T(8,128)S(1)}, u32[]{:S(2)}) copy-start(f32[896,128]{1,0:T(8,128)S(1)} %fusion.46) | copy-start | bytes 1376260
  56.4 7.9 %copy-start.10 = (bf16[1,128,4096]{2,1,0:T(8,128)(2,1)S(1)}, bf16[1,128,4096]{2,1,0:T(8,128)(2,1)}, u32[]{:S(2)}) copy-start(bf16[1,128,4096]{2,1,0:T(8,128)(2,1)} %all-gather.3.cloned.1.call-done) | copy-start | bytes 3145732
  62.0 17.6 %copy-start.4 = (f32[896,128]{1,0:T(8,128)}, f32[896,128]{1,0:T(8,128)S(1)}, u32[]{:S(2)}) copy-start(f32[896,128]{1,0:T(8,128)S(1)} %fusion.49) | copy-start | bytes 1376260
  72.0 7.6 %copy-start.6 = (f32[896,128]{1,0:T(8,128)}, f32[896,128]{1,0:T(8,128)S(1)}, u32[]{:S(2)}) copy-start(f32[896,128]{1,0:T(8,128)S(1)} %fusion.43) | copy-start | bytes 1376260
  79.6 0.8 copy-start.8
  80.4 105.2 %slice-start = ((s8[7340032]{0:T(1024)(128)(4,1)}), s8[3145728]{0:T(1024)(128)(4,1)S(1)}, s32[]{:S(2)}) async-start(s8[7340032]{0:T(1024)(128)(4,1)} %bitcast.54), calls=%async_computation.10 | async-start | bytes 6291456
  82.9 243.7 %reduce-scatter.9.cloned.1.call-start = ((), (), s32[]{:S(2)}) async-start(), calls=%async_computation.6 | async-start | bytes 11010048 | tf_op jit(solution)/shard_map/reduce_scatter | solution.py:84
  179.9 5.7 copy-start.1
  179.9 5.7 slice-start.1
  179.9 7.8 %copy-start.3 = (f32[896,128]{1,0:T(8,128)S(1)}, f32[896,128]{1,0:T(8,128)}, u32[]{:S(2)}) copy-start(f32[896,128]{1,0:T(8,128)} %copy-done.2) | copy-start | bytes 1376260
  179.9 7.8 %copy-start.5 = (f32[896,128]{1,0:T(8,128)S(1)}, f32[896,128]{1,0:T(8,128)}, u32[]{:S(2)}) copy-start(f32[896,128]{1,0:T(8,128)} %copy-done.4) | copy-start | bytes 1376260
  179.9 7.8 %copy-start.7 = (f32[896,128]{1,0:T(8,128)S(1)}, f32[896,128]{1,0:T(8,128)}, u32[]{:S(2)}) copy-start(f32[896,128]{1,0:T(8,128)} %copy-done.6) | copy-start | bytes 1376260
  179.9 7.8 %copy-start.9 = (f32[896,128]{1,0:T(8,128)S(1)}, f32[896,128]{1,0:T(8,128)}, u32[]{:S(2)}) copy-start(f32[896,128]{1,0:T(8,128)} %copy-done.8) | copy-start | bytes 1376260
  179.9 7.8 %copy-start.11 = (bf16[1,128,4096]{2,1,0:T(8,128)(2,1)S(1)}, bf16[1,128,4096]{2,1,0:T(8,128)(2,1)}, u32[]{:S(2)}) copy-start(bf16[1,128,4096]{2,1,0:T(8,128)(2,1)} %all-gather.3.cloned.1.call-done) | copy-start | bytes 3145732
  238.5 178.7 %reduce-scatter.11.cloned.1.call-start = ((), (), s32[]{:S(2)}) async-start(), calls=%async_computation.7 | async-start | bytes 11010048 | tf_op jit(solution)/shard_map/reduce_scatter | solution.py:87
  239.1 268.8 %reduce-scatter.7.cloned.1.call-start = ((), (), s32[]{:S(2)}) async-start(), calls=%async_computation.5 | async-start | bytes 11010048 | tf_op jit(solution)/shard_map/reduce_scatter | solution.py:81
  239.7 358.9 %reduce-scatter.5.cloned.1.call-start = ((), (), s32[]{:S(2)}) async-start(), calls=%async_computation.4 | async-start | bytes 11010048 | tf_op jit(solution)/shard_map/reduce_scatter | solution.py:78
Sparse Core Ops, SparseCore 0:
  10.2 40.6 all-gather.2
  83.0 96.8 all-reduce.2
  238.6 87.8 reduce-scatter.8
  328.7 88.4 reduce-scatter.10
  419.4 88.4 reduce-scatter.6
  510.0 88.4 reduce-scatter.4
where the time goes:
time: 622 us; the launch traced here: 613 us
  waiting for transfers between devices  491 us (79%)
  matrix products  61.3 us (10%)
  other arithmetic  42.4 us (7%)
  between operations  14.5 us (2%)
    psum x1, waiting for transfers between devices, on_device(): lax.psum(term_y.astype(jnp.bfloat16), 'fsdp').astype(jnp.float32)  96.6 us
    reduce_scatter x1, waiting for transfers between devices, on_device(): lax.psum_scatter(term_gate.astype(jnp.bfloat16), 'ckpt', scatter_dimensio...  90.6 us
    reduce_scatter x1, waiting for transfers between devices, on_device(): lax.psum_scatter(w_up.astype(jnp.bfloat16), 'ckpt', scatter_dimension=1,...  90.6 us
    reduce_scatter x1, waiting for transfers between devices, on_device(): lax.psum_scatter(term_up.astype(jnp.bfloat16), 'ckpt', scatter_dimension=...  86.3 us
    reduce_scatter x1, waiting for transfers between devices, on_device(): lax.psum_scatter(w_gate.astype(jnp.bfloat16), 'ckpt', scatter_dimension=1...  83.6 us
    all_gather x1, waiting for transfers between devices, on_device(): whole = lax.all_gather(tokens[0], 'fsdp', axis=0, tiled=True)  41.2 us
    dot_general x6, matrix products, cross(): lax.dot_general(left, right, (((1,), (1,)), ((), ())), preferred_element_...  34 us
    convert_element_type x1, other arithmetic, on_device(): term_up.astype(jnp.bfloat16)  28.3 us
  transfers between devices with their start and end apart: 6, of which 6 were waited for; matrix products, arithmetic and copies ran while one was open for 1% of the time, Pallas kernels for 0%

commit v1 on v0

v1 whole, which is shorter than its diff:
```python
import functools

import jax
import jax.numpy as jnp
from jax import lax
from jax.experimental import pallas as pl
from jax.experimental.pallas import tpu as pltpu
from jax.sharding import PartitionSpec as P

F32 = jnp.float32
BF16 = jnp.bfloat16
NT = (((1,), (1,)), ((), ()))
NN = (((1,), (0,)), ((), ()))
TN = (((0,), (0,)), ((), ()))


def dot(left, right, dims):
    return lax.dot_general(left, right, dims, preferred_element_type=F32)


def params():
    return pltpu.CompilerParams(
        dimension_semantics=("arbitrary",), vmem_limit_bytes=48 * 1024 * 1024
    )


def rows_of(units):
    return 128 if units % 128 == 0 else units


def tile_of(width):
    return 512 if width % 512 == 0 else width


def hops(n):
    high = list(range(1, n.bit_length() - 1))
    return list(zip(high, high[1:] + high[:1]))


def swap(value, axis, n, even, odd):
    pairs = [(i, i ^ (1 << (odd if i & 1 else even))) for i in range(n)]
    return lax.ppermute(value, axis, pairs)


def side(axis, even, odd):
    me = lax.axis_index(axis)
    return jnp.where(me & 1 == 1, (me >> odd) & 1, (me >> even) & 1)


def add(left, right):
    return (left.astype(F32) + right.astype(F32)).astype(BF16)


def scatter_sum(value, axis, n):
    for even, odd in hops(n):
        half = value.shape[0] // 2
        mine = side(axis, even, odd)
        keep = lax.dynamic_slice_in_dim(value, mine * half, half, 0)
        send = lax.dynamic_slice_in_dim(value, (1 - mine) * half, half, 0)
        value = add(keep, swap(send, axis, n, even, odd))
    return value


def gather(value, axis, n):
    for even, odd in reversed(hops(n)):
        other = swap(value, axis, n, even, odd)
        first = side(axis, even, odd) == 0
        value = jnp.where(
            first, jnp.concatenate([value, other]), jnp.concatenate([other, value])
        )
    return value


def gather_order(n):
    order = []
    for core in (0, 1):
        bits = [pair[core] for pair in reversed(hops(n))]
        for place in range(n // 2):
            order.append(core + sum(((place >> j) & 1) << b for j, b in enumerate(bits)))
    return order


def forward_kernel(factor, steps, core, x, gate, upper, down, row, col, p, q, act, sd,
                   send, keep, hid, whole, sem):
    step = pl.program_id(0)
    tokens, width = x.shape
    units = gate.shape[0]
    copy = pltpu.make_async_copy(down, whole, sem)

    @pl.when(step == 0)
    def _():
        copy.start()

    a = dot(x[...], gate[...], NT) * factor
    b = dot(x[...], upper[...], NT) * factor
    tile = tile_of(width)
    da = jnp.zeros((tokens, units), F32)
    db = jnp.zeros((tokens, units), F32)
    for at in range(0, width, tile):
        part = x[:, at:at + tile]
        signs = []
        for k in (0, 1):
            code = jnp.bitwise_and(col[:, k:k + 1], row[k:k + 1, at:at + tile])
            odd = jnp.bitwise_and(lax.population_count(code), 1)
            signs.append((1 - 2 * odd).astype(F32).astype(BF16))
        da = da + dot(part, signs[0], NT)
        db = db + dot(part, signs[1], NT)
    da = da * factor
    db = db * factor
    sigma = jax.nn.sigmoid(a)
    s = a * sigma
    slope = sigma * (1.0 + a * (1.0 - sigma))
    curve = sigma * (1.0 - sigma) * (2.0 + a * (1.0 - 2.0 * sigma))
    p[...] = b * slope
    q[...] = db * slope + b * curve * da
    act[...] = s
    sd[...] = slope * da
    hidden = s * b
    d_hidden = slope * da * b + s * db
    even = core[0] == 0
    if steps == 1:
        place = slice(None)
    else:
        place = pl.ds(pl.multiple_of(step * units, units), units)
    hid[:tokens, place] = jnp.where(even, d_hidden, hidden).astype(BF16)
    hid[tokens:, place] = jnp.where(even, hidden, d_hidden).astype(BF16)

    @pl.when(step == steps - 1)
    def _():
        copy.wait()
        for at in range(0, width, tile):
            both = dot(hid[...], whole[:, at:at + tile], NN)
            send[:, at:at + tile] = both[:tokens].astype(BF16)
            keep[:, at:at + tile] = both[tokens:].astype(BF16)


def forward(core, x, gate, upper, down, row, col):
    tokens, width = x.shape
    units = gate.shape[0]
    block = rows_of(units)
    steps = units // block
    by_unit = pl.BlockSpec((block, width), lambda i, c: (i, 0))
    by_lane = pl.BlockSpec((tokens, block), lambda i, c: (0, i))
    fixed = pl.BlockSpec((tokens, width), lambda i, c: (0, 0))
    wide = jax.ShapeDtypeStruct((tokens, units), F32)
    out = jax.ShapeDtypeStruct((tokens, width), BF16)
    return pl.pallas_call(
        functools.partial(forward_kernel, width ** (-0.5), steps),
        out_shape=(wide,) * 4 + (out,) * 2,
        grid_spec=pltpu.PrefetchScalarGridSpec(
            num_scalar_prefetch=1,
            grid=(steps,),
            in_specs=[
                fixed,
                by_unit,
                by_unit,
                pl.BlockSpec(memory_space=pl.ANY),
                pl.BlockSpec((2, width), lambda i, c: (0, 0)),
                pl.BlockSpec((block, 2), lambda i, c: (i, 0)),
            ],
            out_specs=[by_lane] * 4 + [fixed] * 2,
            scratch_shapes=[
                pltpu.VMEM((2 * tokens, units), BF16),
                pltpu.VMEM((units, width), BF16),
                pltpu.SemaphoreType.DMA,
            ],
        ),
        compiler_params=params(),
        cost_estimate=pl.CostEstimate(
            flops=12 * tokens * width * units,
            bytes_accessed=6 * units * width,
            transcendentals=tokens * units,
        ),
        name="forward",
    )(core, x, gate, upper, down, row, col)


def backward_kernel(core, mine, other, down, x, p, q, act, sd, grads, scale):
    tokens, width = x.shape
    units = down.shape[0]
    g_mine = dot(mine[...], down[...], NT)
    g_other = dot(other[...], down[...], NT)
    even = core[0] == 0
    gh = jnp.where(even, g_mine, g_other)
    gdh = jnp.where(even, g_other, g_mine)
    both = (
        (gdh * p[...] + gh * q[...]).astype(BF16),
        (gdh * act[...] + gh * sd[...]).astype(BF16),
    )
    tile = tile_of(width)
    lanes = 128 if tile % 128 == 0 else tile
    rows = []
    for k, grad in enumerate(both):
        grads[k * tokens:(k + 1) * tokens, :] = grad
        total = jnp.zeros((units, lanes), F32)
        for at in range(0, width, tile):
            e = jnp.abs(dot(grad, x[:, at:at + tile], TN))
            for low in range(0, tile, lanes):
                total = total + e[:, low:low + lanes]
        mean = jnp.sum(total.T, axis=0, keepdims=True) * (1.0 / width)
        rows.append(1.0 / (mean + 1e-06))
    scale[...] = jnp.concatenate(rows + [jnp.zeros((6, units), F32)], axis=0)


def backward(core, mine, other, down, x, kept):
    tokens, width = x.shape
    units = down.shape[0]
    block = rows_of(units)
    by_lane = pl.BlockSpec((tokens, block), lambda i, c: (0, i))
    fixed = pl.BlockSpec((tokens, width), lambda i, c: (0, 0))
    return pl.pallas_call(
        backward_kernel,
        out_shape=(
            jax.ShapeDtypeStruct((2 * tokens, units), BF16),
            jax.ShapeDtypeStruct((8, units), F32),
        ),
        grid_spec=pltpu.PrefetchScalarGridSpec(
            num_scalar_prefetch=1,
            grid=(units // block,),
            in_specs=[
                fixed,
                fixed,
                pl.BlockSpec((block, width), lambda i, c: (i, 0)),
                fixed,
            ] + [by_lane] * 4,
            out_specs=[
                pl.BlockSpec((2 * tokens, block), lambda i, c: (0, i)),
                pl.BlockSpec((8, block), lambda i, c: (0, i)),
            ],
        ),
        compiler_params=params(),
        cost_estimate=pl.CostEstimate(
            flops=8 * tokens * width * units,
            bytes_accessed=2 * units * width,
            transcendentals=0,
        ),
        name="backward",
    )(core, mine, other, down, x, *kept)


def merge_kernel(which, members, *refs):
    refs = refs[1:]
    weights, refs = refs[:members], refs[members:]
    grads, refs = refs[:members], refs[members:]
    scales, refs = refs[:members], refs[members:]
    tokens = refs[:members]
    out = refs[-1]
    width = out.shape[1]
    tile = tile_of(width)
    columns = [scale[...].T[:, which:which + 1] for scale in scales]
    for at in range(0, width, tile):
        numer = denom = None
        for j in range(members):
            hz = dot(grads[j][...], tokens[j][:, at:at + tile], TN)
            w = jnp.abs(hz) * columns[j]
            term = (w * weights[j][:, at:at + tile].astype(F32)).astype(BF16).astype(F32)
            w = w.astype(BF16).astype(F32)
            numer = term if numer is None else numer + term
            denom = w if denom is None else denom + w
        out[:, at:at + tile] = (numer / jnp.maximum(denom, 1.0)).astype(BF16)


def merge(spot, which, start, weight, received, grads, scales, x, others, so_far):
    members = 1 + len(received)
    units = weight.shape[0]
    tokens, width = others[0].shape
    block = rows_of(units)
    rows = received[0].shape[0]
    first = start // block
    in_specs = [pl.BlockSpec((block, width), lambda i, c: (first + i, c[0]))]
    in_specs += [pl.BlockSpec((block, width), lambda i, c: (i, 0))] * (members - 1)
    in_specs += [pl.BlockSpec((tokens, block), lambda i, c: (which, first + i))] * members
    in_specs += [pl.BlockSpec((8, block), lambda i, c: (0, first + i))] * members
    in_specs += [pl.BlockSpec((tokens, width), lambda i, c: (0, c[0]))]
    in_specs += [pl.BlockSpec((tokens, width), lambda i, c: (0, 0))] * (members - 1)
    args = [spot, weight, *received, *grads, *scales, x, *others]
    aliases = {}
    if so_far is not None:
        aliases = {len(args): 0}
        in_specs.append(pl.BlockSpec(memory_space=pl.ANY))
        args.append(so_far)
    return pl.pallas_call(
        functools.partial(merge_kernel, which, members),
        out_shape=jax.ShapeDtypeStruct((units, width), BF16),
        grid_spec=pltpu.PrefetchScalarGridSpec(
            num_scalar_prefetch=1,
            grid=(rows // block,),
            in_specs=in_specs,
            out_specs=pl.BlockSpec((block, width), lambda i, c: (first + i, 0)),
        ),
        input_output_aliases=aliases,
        compiler_params=params(),
        cost_estimate=pl.CostEstimate(
            flops=2 * members * tokens * width * rows,
            bytes_accessed=2 * (members + 1) * rows * width,
            transcendentals=0,
        ),
        name="merge",
    )(*args)


def pieces(units):
    block = rows_of(units)
    count = units // block
    if count < 4:
        return [(0, 0, units), (1, 0, units)], []
    last = block
    third = block * max(1, count // 3)
    head = units - last - third
    return (
        [(0, 0, units), (1, 0, head)],
        [(1, head, third), (1, head + third, last)],
    )


def on_device(n_ckpt, n_fsdp, tokens, gate_weight, up_weight, down_weight, row_code, col_code):
    weights = (gate_weight[0], up_weight[0])
    down = down_weight[0]
    own = tokens[0]
    units, width = down.shape
    part = width // n_ckpt
    spot = lax.axis_index("ckpt")
    core = (lax.axis_index("fsdp") & 1).astype(jnp.int32).reshape(1)
    at = spot.astype(jnp.int32).reshape(1)

    def across(value, shift):
        return lax.ppermute(
            value, "ckpt", [(i, (i + shift) % n_ckpt) for i in range(n_ckpt)]
        )

    def cut(which, start, rows, shift):
        left = lax.rem(spot + shift, n_ckpt) * part
        return lax.dynamic_slice(weights[which], (start, left), (rows, part))

    shifts = range(1, n_ckpt)
    early, late = pieces(units)
    arrived = {}
    for piece in early:
        arrived[piece] = [across(cut(*piece, s), s) for s in shifts]

    x = gather(own, "fsdp", n_fsdp)
    other = lax.ppermute(x, "fsdp", [(i, i ^ 1) for i in range(n_fsdp)])
    even = core[0] == 0
    x = jnp.where(even, jnp.concatenate([x, other]), jnp.concatenate([other, x]))

    others = []
    order = gather_order(n_fsdp)
    for s in shifts:
        left = lax.rem(spot + s, n_ckpt) * part
        mine = lax.dynamic_slice(own, (0, left), (own.shape[0], part))
        natural = lax.all_gather(across(mine, s), "fsdp", axis=0, tiled=False)
        others.append(jnp.concatenate([natural[i] for i in order]))

    *kept, send, keep = forward(
        core, x, weights[0], weights[1], down, row_code[0], col_code[0].T
    )
    got = lax.ppermute(send, "fsdp", [(i, i ^ 1) for i in range(n_fsdp)])
    total = gather(scatter_sum(add(keep, got), "fsdp", n_fsdp), "fsdp", n_fsdp)
    other = lax.ppermute(total, "fsdp", [(i, i ^ 1) for i in range(n_fsdp)])
    grads, scale = backward(core, total, other, down, x, kept)

    all_grads = [grads] + [across(grads, s) for s in shifts]
    all_scales = [scale] + [across(scale, s) for s in shifts]
    for piece in late:
        blocks, _ = lax.optimization_barrier(([cut(*piece, s) for s in shifts], grads))
        arrived[piece] = [across(block, s) for block, s in zip(blocks, shifts)]

    out = [None, None]
    for which, start, rows in early + late:
        out[which] = merge(
            at, which, start, weights[which], arrived[which, start, rows], all_grads,
            all_scales, x, others, out[which],
        )
    return tuple(out)


def solution(mesh):
    in_specs = (
        P("ckpt", "fsdp", None),
        P("ckpt", "fsdp", None),
        P("ckpt", "fsdp", None),
        P("ckpt", "fsdp", None),
        P("ckpt", None, None),
        P("ckpt", None, "fsdp"),
    )
    out_specs = (P("fsdp", "ckpt"), P("fsdp", "ckpt"))
    return jax.shard_map(
        functools.partial(on_device, mesh.shape["ckpt"], mesh.shape["fsdp"]),
        mesh=mesh, in_specs=in_specs, out_specs=out_specs, check_vma=False,
    )
```

time: 622 us -> 202 us (0.32); the launches traced: 613 us -> 201 us
  waiting for transfers between devices: 491 us -> 92.5 us
  matrix products: 61.3 us -> 0 us
  Pallas kernels: 0 us -> 51.4 us
  other arithmetic: 42.4 us -> 3.37 us
  blocking collectives: 0 us -> 23.6 us
  starting transfers between devices: 0.85 us -> 17.7 us
  between operations: 14.5 us -> 0.95 us
  local copies, waits for them, and re-layouts: 2.5 us -> 11.1 us
    reduce_scatter x4 -> x0, waiting for transfers between devices: 351 us -> none  [the longest x1 90.6 us: on_device(): lax.psum_scatter(term_gate.astype(jnp.bfloat16), 'ckpt', scatter_dimensio...]
    psum x1 -> x0, waiting for transfers between devices: 96.6 us -> none  [on_device(): lax.psum(term_y.astype(jnp.bfloat16), 'fsdp').astype(jnp.float32)]
    ppermute x0 -> x19, waiting for transfers between devices: none -> 92.5 us  [the longest x9 55.4 us: swap(): return lax.ppermute(value, axis, pairs)]
    dot_general x10 -> x0, matrix products: 61.3 us -> none  [the longest x6 34 us: cross(): lax.dot_general(left, right, (((1,), (1,)), ((), ())), preferred_element_...]
    pallas_call x0 -> x6, Pallas kernels: none -> 51.4 us  [the longest x4 23.4 us: merge(): pl.pallas_call(functools.partial(merge_kernel, which, members), out_shape...]
    convert_element_type x3 -> x4, other arithmetic: 42.4 us -> 0.48 us  [add(): return (left.astype(F32) + right.astype(F32)).astype(BF16)]
    all_gather x1 -> x0, waiting for transfers between devices: 41.2 us -> none  [on_device(): whole = lax.all_gather(tokens[0], 'fsdp', axis=0, tiled=True)]
    all_gather x0 -> x1, blocking collectives: none -> 23.6 us  [on_device(): natural = lax.all_gather(across(mine, s), 'fsdp', axis=0, tiled=False)]
  transfers between devices with their start and end apart: 6 -> 19, of which waited for: 6 -> 10; matrix products, arithmetic and copies ran while one was open for 1% -> 7% of each run, Pallas kernels for 0% -> 24%
where the time goes in v1:
time: 202 us; the launch traced here: 201 us
  waiting for transfers between devices  92.5 us (46%)
  Pallas kernels  51.4 us (25%)
  blocking collectives  23.6 us (12%)
  starting transfers between devices  17.7 us (9%)
  local copies, waits for them, and re-layouts  11.1 us (5%)
  other arithmetic  3.37 us (2%)
    ppermute x9, waiting for transfers between devices, swap(): return lax.ppermute(value, axis, pairs)  55.4 us
    ppermute x7, waiting for transfers between devices, across(): lax.ppermute(value, 'ckpt', [(i, (i + shift) % n_ckpt) for i in range(n_c...  34.5 us
    all_gather x1, blocking collectives, on_device(): natural = lax.all_gather(across(mine, s), 'fsdp', axis=0, tiled=False)  23.6 us
    pallas_call x4, Pallas kernels, merge(): pl.pallas_call(functools.partial(merge_kernel, which, members), out_shape...  23.4 us
    pallas_call x1, Pallas kernels, forward(): pl.pallas_call(functools.partial(forward_kernel, width ** (-0.5), steps),...  15.9 us
    pallas_call x1, Pallas kernels, backward(): pl.pallas_call(backward_kernel, out_shape=(jax.ShapeDtypeStruct((2 * toke...  12.1 us
    dynamic_slice x4, local copies, waits for them, and re-layouts, cut(): return lax.dynamic_slice(weights[which], (start, left), (rows, part))  9.96 us
    ppermute x7, starting transfers between devices, across(): lax.ppermute(value, 'ckpt', [(i, (i + shift) % n_ckpt) for i in range(n_c...  8.8 us
  transfers between devices with their start and end apart: 19, of which 10 were waited for; matrix products, arithmetic and copies ran while one was open for 7% of the time, Pallas kernels for 24%

profile of v1, /device:TPU:0, one launch (start us, length us, event | category | flops | bytes accessed | tf_op | source)
XLA Modules:
  0.0 200.6 jit_solution(4728773358712075269)
XLA Ops:
  0.6 4.1 %collective-permute-start.1 = (bf16[8,4096]{1,0:T(8,128)(2,1)}, bf16[8,4096]{1,0:T(8,128)(2,1)S(1)}, u32[]{:S(2)}, u32[]{:S(2)}) collective-permute-start(bf16[8,4096]{1,0:T(8,128)(2,1)} %bitcast.30), channel_id=1, source_target_pairs={{0,8},{1,3},{2,10},{3,1},{4,12},{5,7},{6,14},{7,5},{8,0},{9,11},{1... | collective-permute-start | bytes 196616 | tf_op jit(solution)/shard_map/ppermute | solution.py:42
  4.7 2.5 %collective-permute-done.1 = bf16[8,4096]{1,0:T(8,128)(2,1)S(1)} collective-permute-done((bf16[8,4096]{1,0:T(8,128)(2,1)}, bf16[8,4096]{1,0:T(8,128)(2,1)S(1)}, u32[]{:S(2)}, u32[]{:S(2)}) %collective-permute-start.1) | collective-permute-done | bytes 65568 | tf_op jit(solution)/shard_map/ppermute | solution.py:42
  7.2 0.9 maximum_select_fusion.6
  8.1 2.0 collective-permute-start.2
  10.1 0.8 dynamic-slice_bitcast_fusion.4
  10.9 1.5 collective-permute-start.15
  12.4 1.1 collective-permute-done.2
  13.5 2.0 collective-permute-start.3
  15.4 3.2 %dynamic-slice_bitcast_fusion.1 = bf16[512,2048]{1,0:T(8,128)(2,1)} fusion(bf16[1,896,4096]{2,1,0:T(8,128)(2,1)} %param.8, s32[]{:T(128)S(6)} %select_n.91), kind=kLoop, calls=%fused_computation.1 | loop fusion | bytes 4194308 | tf_op jit(solution)/shard_map/dynamic_slice | solution.py:333
  18.6 1.5 collective-permute-start.18
  20.3 4.4 %dynamic-slice_bitcast_fusion = bf16[896,2048]{1,0:T(8,128)(2,1)} fusion(bf16[1,896,4096]{2,1,0:T(8,128)(2,1)} %param.7, s32[]{:T(128)S(6)} %select_n.91), kind=kLoop, calls=%fused_computation | loop fusion | bytes 7340036 | tf_op jit(solution)/shard_map/dynamic_slice | solution.py:333
  24.6 1.7 collective-permute-start
  26.5 1.1 dynamic-slice_bitcast_fusion.3
  27.7 1.3 dynamic-slice_bitcast_fusion.2
  29.0 1.5 maximum_select_fusion.x.refs_7_
  30.5 15.9 %forward.1 = (f32[128,896]{1,0:T(8,128)S(1)}, f32[128,896]{1,0:T(8,128)S(1)}, f32[128,896]{1,0:T(8,128)S(1)}, f32[128,896]{1,0:T(8,128)S(1)}, bf16[128,4096]{1,0...) custom-call(s32[1]{0:T(128)} %bitcast.3.core, bf16[128,4096]{1,0:T(8,128)(2,1)S(1)} %maximum_select_fusion.x.refs_7_, ...), custom_call_target="tpu_custom_call" | custom-call | flops 5637144576 | bytes 22020096 | tf_op jit(solution)/shard_map/forward/pallas_call | solution.py:147
  46.7 23.6 %all-gather = bf16[128,2048]{1,0:T(8,128)(2,1)S(1)} all-gather(bf16[8,2048]{1,0:T(8,128)(2,1)S(1)} %collective-permute-done.15), channel_id=2, replica_groups=mesh['ckpt'=2,'fsdp'=16] {'fsdp'}, dimensions={0}, use_global_device_ids=true | all-gather | bytes 557056 | tf_op jit(solution)/shard_map/all_gather | solution.py:351
  70.7 9.1 %collective-permute-done.6 = bf16[64,4096]{1,0:T(8,128)(2,1)S(1)} collective-permute-done((bf16[64,4096]{1,0:T(8,128)(2,1)S(1)}, bf16[64,4096]{1,0:T(8,128)(2,1)S(1)}, u32[]{:S(2)}, u32[]{:S(2)}) %collective-permute-start.6) | collective-permute-done | bytes 524320 | tf_op jit(solution)/shard_map/ppermute | solution.py:42
  80.1 9.0 %collective-permute-done.7 = bf16[32,4096]{1,0:T(8,128)(2,1)S(1)} collective-permute-done((bf16[32,4096]{1,0:T(8,128)(2,1)S(1)}, bf16[32,4096]{1,0:T(8,128)(2,1)S(1)}, u32[]{:S(2)}, u32[]{:S(2)}) %collective-permute-start.7) | collective-permute-done | bytes 262176 | tf_op jit(solution)/shard_map/ppermute | solution.py:42
  89.3 6.3 %collective-permute-done.8 = bf16[16,4096]{1,0:T(8,128)(2,1)S(1)} collective-permute-done((bf16[16,4096]{1,0:T(8,128)(2,1)S(1)}, bf16[16,4096]{1,0:T(8,128)(2,1)S(1)}, u32[]{:S(2)}, u32[]{:S(2)}) %collective-permute-start.8) | collective-permute-done | bytes 131104 | tf_op jit(solution)/shard_map/ppermute | solution.py:42
  95.6 9.5 %collective-permute-done.9 = bf16[16,4096]{1,0:T(8,128)(2,1)S(1)} collective-permute-done((bf16[16,4096]{1,0:T(8,128)(2,1)S(1)}, bf16[16,4096]{1,0:T(8,128)(2,1)S(1)}, u32[]{:S(2)}, u32[]{:S(2)}) %collective-permute-start.9) | collective-permute-done | bytes 131104 | tf_op jit(solution)/shard_map/ppermute | solution.py:42
  105.3 8.9 %collective-permute-done.10 = bf16[32,4096]{1,0:T(8,128)(2,1)S(1)} collective-permute-done((bf16[32,4096]{1,0:T(8,128)(2,1)S(1)}, bf16[32,4096]{1,0:T(8,128)(2,1)S(1)}, u32[]{:S(2)}, u32[]{:S(2)}) %collective-permute-start.10) | collective-permute-done | bytes 262176 | tf_op jit(solution)/shard_map/ppermute | solution.py:42
  114.4 9.1 %collective-permute-done.11 = bf16[64,4096]{1,0:T(8,128)(2,1)S(1)} collective-permute-done((bf16[64,4096]{1,0:T(8,128)(2,1)S(1)}, bf16[64,4096]{1,0:T(8,128)(2,1)S(1)}, u32[]{:S(2)}, u32[]{:S(2)}) %collective-permute-start.11) | collective-permute-done | bytes 524320 | tf_op jit(solution)/shard_map/ppermute | solution.py:42
  123.8 2.6 %collective-permute-done.12.other = bf16[128,4096]{1,0:T(8,128)(2,1)S(1)} collective-permute-done((bf16[128,4096]{1,0:T(8,128)(2,1)S(1)}, bf16[128,4096]{1,0:T(8,128)(2,1)S(1)}, u32[]{:S(2)}, u32[]{:S(2)}) %collective-permute-start.12) | collective-permute-done | bytes 1048608 | tf_op jit(solution)/shard_map/ppermute | solution.py:359
  126.4 12.1 %backward.1 = (bf16[256,896]{1,0:T(8,128)(2,1)S(1)}, f32[8,896]{1,0:T(8,128)S(1)}) custom-call(s32[1]{0:T(128)} %bitcast.3.core, bf16[128,4096]{1,0:T(8,128)(2,1)S(1)} %maximum_select_fusion.1.mine, bf16[128,4096]{1,0:T(8,128)(2,1)S(1)} %collective-permute-done.12.other, bf16[896,4096]{1,0:T(8,128)(2,1)} %bitcast.29, ...), custom_call_target="tpu_custom_call" | custom-call | flops 3758096384 | bytes 7340032 | tf_op jit(solution)/shard_map/backward/pallas_call | solution.py:211
  139.1 1.5 collective-permute-start.13
  141.1 1.5 collective-permute-start.16
  142.7 34.5 %collective-permute-done.14.refs_6_ = f32[8,896]{1,0:T(8,128)S(1)} collective-permute-done((f32[8,896]{1,0:T(8,128)S(1)}, f32[8,896]{1,0:T(8,128)S(1)}, u32[]{:S(2)}, u32[]{:S(2)}) %collective-permute-start.14) | collective-permute-done | bytes 28704 | tf_op jit(solution)/shard_map/ppermute | solution.py:327
  177.1 6.2 %merge.5.refs_9_ = bf16[896,2048]{1,0:T(8,128)(2,1)} custom-call(s32[1]{0:T(128)} %bitcast.refs_0_, bf16[896,4096]{1,0:T(8,128)(2,1)} %bitcast.23, bf16[512,2048]{1,0:T(8,128)(2,1)S(1)} %collective-permute-done.18.refs_2_, bf16[256,896]{1,0:T(8,128)(2,1)S(1)} %get-tuple-element.18.refs_3_, bf16[256,896]{1,0:T(8,128)(2,1)S(1)} %collective-permute-done.13.refs_4_, ...), custom_call_target="tpu_custom_call" | custom-call | flops 536870912 | bytes 6291456 | tf_op jit(solution)/shard_map/merge/pallas_call | solution.py:282
  183.4 10.4 %merge.4 = bf16[896,2048]{1,0:T(8,128)(2,1)} custom-call(s32[1]{0:T(128)} %bitcast.refs_0_, bf16[896,4096]{1,0:T(8,128)(2,1)} %bitcast.27, bf16[896,2048]{1,0:T(8,128)(2,1)} %collective-permute-done.refs_2_, bf16[256,896]{1,0:T(8,128)(2,1)S(1)} %get-tuple-element.18.refs_3_, bf16[256,896]{1,0:T(8,128)(2,1)S(1)} %collective-permute-done.13.refs_4_, ...), custom_call_target="tpu_custom_call" | custom-call | flops 939524096 | bytes 11010048 | tf_op jit(solution)/shard_map/merge/pallas_call | solution.py:282
  193.8 3.9 %merge.6.refs_9_ = bf16[896,2048]{1,0:T(8,128)(2,1)} custom-call(s32[1]{0:T(128)} %bitcast.refs_0_, bf16[896,4096]{1,0:T(8,128)(2,1)} %bitcast.24, bf16[256,2048]{1,0:T(8,128)(2,1)S(1)} %collective-permute-done.17.refs_2_, bf16[256,896]{1,0:T(8,128)(2,1)S(1)} %get-tuple-element.18.refs_3_, ...), custom_call_target="tpu_custom_call", output_to_operand_aliasing={{}: (9, {})} | custom-call | flops 268435456 | bytes 3145728 | tf_op jit(solution)/shard_map/merge/pallas_call | solution.py:282
  197.7 2.9 %merge.7 = bf16[896,2048]{1,0:T(8,128)(2,1)} custom-call(s32[1]{0:T(128)} %bitcast.refs_0_, bf16[896,4096]{1,0:T(8,128)(2,1)} %bitcast.25, bf16[128,2048]{1,0:T(8,128)(2,1)S(1)} %collective-permute-done.16.refs_2_, bf16[256,896]{1,0:T(8,128)(2,1)S(1)} %get-tuple-element.18.refs_3_, ...), custom_call_target="tpu_custom_call", output_to_operand_aliasing={{}: (9, {})} | custom-call | flops 134217728 | bytes 1572864 | tf_op jit(solution)/shard_map/merge/pallas_call | solution.py:282
  (53 shorter events, 3.3 us)
Async XLA Ops:
  0.6 6.6 %collective-permute-start.1 = (bf16[8,4096]{1,0:T(8,128)(2,1)}, bf16[8,4096]{1,0:T(8,128)(2,1)S(1)}, u32[]{:S(2)}, u32[]{:S(2)}) collective-permute-start(bf16[8,4096]{1,0:T(8,128)(2,1)} %bitcast.30), channel_id=1, source_target_pairs={{0,8},{1,3},{2,10},{3,1},{4,12},{5,7},{6,14},{7,5},{8,0},{9,11},{1... | collective-permute-start | bytes 196616 | tf_op jit(solution)/shard_map/ppermute | solution.py:42
  8.1 5.3 %collective-permute-start.2 = (bf16[16,4096]{1,0:T(8,128)(2,1)S(1)}, bf16[16,4096]{1,0:T(8,128)(2,1)S(1)}, u32[]{:S(2)}, u32[]{:S(2)}) collective-permute-start(bf16[16,4096]{1,0:T(8,128)(2,1)S(1)} %maximum_select_fusion.6), channel_id=1, source_target_pairs={{0,4},{1,9},{2,6},{3,11},{4,0},{5,13},{6,2},{7,15},{8,12},{9,1},{1... | collective-permute-start | bytes 393224 | tf_op jit(solution)/shard_map/ppermute | solution.py:42
  10.9 35.8 %collective-permute-start.15 = (bf16[8,2048]{1,0:T(8,128)(2,1)S(1)}, bf16[8,2048]{1,0:T(8,128)(2,1)S(1)}, u32[]{:S(2)}, u32[]{:S(2)}) collective-permute-start(bf16[8,2048]{1,0:T(8,128)(2,1)S(1)} %dynamic-slice_bitcast_fusion.4), channel_id=1, source_target_pairs={{0,16},{16,0},{1,17},{17,1},{2,18},{18,2},{3,19},{19,3},{4,20},{20... | collective-permute-start | bytes 98312 | tf_op jit(solution)/shard_map/ppermute | solution.py:327
  13.5 6.6 %collective-permute-start.3 = (bf16[32,4096]{1,0:T(8,128)(2,1)S(1)}, bf16[32,4096]{1,0:T(8,128)(2,1)S(1)}, u32[]{:S(2)}, u32[]{:S(2)}) collective-permute-start(bf16[32,4096]{1,0:T(8,128)(2,1)S(1)} %maximum_select_fusion.4), channel_id=1, source_target_pairs={{0,2},{1,5},{2,0},{3,7},{4,6},{5,1},{6,4},{7,3},{8,10},{9,13},{10,... | collective-permute-start | bytes 786440 | tf_op jit(solution)/shard_map/ppermute | solution.py:42
  18.6 122.6 %collective-permute-start.18 = (bf16[512,2048]{1,0:T(8,128)(2,1)}, bf16[512,2048]{1,0:T(8,128)(2,1)S(1)}, u32[]{:S(2)}, u32[]{:S(2)}) collective-permute-start(bf16[512,2048]{1,0:T(8,128)(2,1)} %dynamic-slice_bitcast_fusion.1), channel_id=1, source_target_pairs={{0,16},{16,0},{1,17},{17,1},{2,18},{18,2},{3,19},{19,3},{4,20},{20... | collective-permute-start | bytes 6291464 | tf_op jit(solution)/shard_map/ppermute | solution.py:327
  20.2 6.2 %copy-start.1 = (s32[1,2,896]{2,1,0:T(2,128)S(1)}, s32[1,2,896]{2,1,0:T(2,128)}, u32[]{:S(2)}) copy-start(s32[1,2,896]{2,1,0:T(2,128)} %param.11) | copy-start | bytes 21508
  20.2 8.8 %collective-permute-start.4 = (bf16[64,4096]{1,0:T(8,128)(2,1)S(1)}, bf16[64,4096]{1,0:T(8,128)(2,1)}, u32[]{:S(2)}, u32[]{:S(2)}) collective-permute-start(bf16[64,4096]{1,0:T(8,128)(2,1)S(1)} %maximum_select_fusion.2), channel_id=1, source_target_pairs={{0,1},{1,0},{2,3},{3,2},{4,5},{5,4},{6,7},{7,6},{8,9},{9,8},{10,11... | collective-permute-start | bytes 1572872 | tf_op jit(solution)/shard_map/ppermute | solution.py:342
  24.6 158.7 %collective-permute-start = (bf16[896,2048]{1,0:T(8,128)(2,1)}, bf16[896,2048]{1,0:T(8,128)(2,1)}, u32[]{:S(2)}, u32[]{:S(2)}) collective-permute-start(bf16[896,2048]{1,0:T(8,128)(2,1)} %dynamic-slice_bitcast_fusion), channel_id=1, source_target_pairs={{0,16},{16,0},{1,17},{17,1},{2,18},{18,2},{3,19},{19,3},{4,20},{20... | collective-permute-start | bytes 11010056 | tf_op jit(solution)/shard_map/ppermute | solution.py:327
  27.6 2.8 %copy-start = (s32[1,2,4096]{2,1,0:T(2,128)S(1)}, s32[1,2,4096]{2,1,0:T(2,128)}, u32[]{:S(2)}) copy-start(s32[1,2,4096]{2,1,0:T(2,128)} %param.10) | copy-start | bytes 98308
  46.4 23.9 %collective-permute-start.5 = (bf16[128,4096]{1,0:T(8,128)(2,1)S(1)}, bf16[128,4096]{1,0:T(8,128)(2,1)S(1)}, u32[]{:S(2)}, u32[]{:S(2)}) collective-permute-start(bf16[128,4096]{1,0:T(8,128)(2,1)S(1)} %get-tuple-element.13), channel_id=1, source_target_pairs={{0,1},{1,0},{2,3},{3,2},{4,5},{5,4},{6,7},{7,6},{8,9},{9,8},{10,11... | collective-permute-start | bytes 3145736 | tf_op jit(solution)/shard_map/ppermute | solution.py:357
  70.6 9.2 %collective-permute-start.6 = (bf16[64,4096]{1,0:T(8,128)(2,1)S(1)}, bf16[64,4096]{1,0:T(8,128)(2,1)S(1)}, u32[]{:S(2)}, u32[]{:S(2)}) collective-permute-start(bf16[64,4096]{1,0:T(8,128)(2,1)S(1)} %constant_dynamic-slice_fusion.2), channel_id=1, source_target_pairs={{0,2},{1,5},{2,0},{3,7},{4,6},{5,1},{6,4},{7,3},{8,10},{9,13},{10,... | collective-permute-start | bytes 1572872 | tf_op jit(solution)/shard_map/ppermute | solution.py:42
  80.0 9.1 %collective-permute-start.7 = (bf16[32,4096]{1,0:T(8,128)(2,1)S(1)}, bf16[32,4096]{1,0:T(8,128)(2,1)S(1)}, u32[]{:S(2)}, u32[]{:S(2)}) collective-permute-start(bf16[32,4096]{1,0:T(8,128)(2,1)S(1)} %constant_dynamic-slice_fusion.1), channel_id=1, source_target_pairs={{0,4},{1,9},{2,6},{3,11},{4,0},{5,13},{6,2},{7,15},{8,12},{9,1},{1... | collective-permute-start | bytes 786440 | tf_op jit(solution)/shard_map/ppermute | solution.py:42
  89.2 6.3 %collective-permute-start.8 = (bf16[16,4096]{1,0:T(8,128)(2,1)S(1)}, bf16[16,4096]{1,0:T(8,128)(2,1)S(1)}, u32[]{:S(2)}, u32[]{:S(2)}) collective-permute-start(bf16[16,4096]{1,0:T(8,128)(2,1)S(1)} %constant_dynamic-slice_fusion), channel_id=1, source_target_pairs={{0,8},{1,3},{2,10},{3,1},{4,12},{5,7},{6,14},{7,5},{8,0},{9,11},{1... | collective-permute-start | bytes 393224 | tf_op jit(solution)/shard_map/ppermute | solution.py:42
  95.6 9.6 %collective-permute-start.9 = (bf16[16,4096]{1,0:T(8,128)(2,1)S(1)}, bf16[16,4096]{1,0:T(8,128)(2,1)S(1)}, u32[]{:S(2)}, u32[]{:S(2)}) collective-permute-start(bf16[16,4096]{1,0:T(8,128)(2,1)S(1)} %add_convert_fusion.3), channel_id=1, source_target_pairs={{0,8},{1,3},{2,10},{3,1},{4,12},{5,7},{6,14},{7,5},{8,0},{9,11},{1... | collective-permute-start | bytes 393224 | tf_op jit(solution)/shard_map/ppermute | solution.py:42
  105.2 8.9 %collective-permute-start.10 = (bf16[32,4096]{1,0:T(8,128)(2,1)S(1)}, bf16[32,4096]{1,0:T(8,128)(2,1)S(1)}, u32[]{:S(2)}, u32[]{:S(2)}) collective-permute-start(bf16[32,4096]{1,0:T(8,128)(2,1)S(1)} %maximum_select_fusion.5), channel_id=1, source_target_pairs={{0,4},{1,9},{2,6},{3,11},{4,0},{5,13},{6,2},{7,15},{8,12},{9,1},{1... | collective-permute-start | bytes 786440 | tf_op jit(solution)/shard_map/ppermute | solution.py:42
  114.3 9.2 %collective-permute-start.11 = (bf16[64,4096]{1,0:T(8,128)(2,1)S(1)}, bf16[64,4096]{1,0:T(8,128)(2,1)S(1)}, u32[]{:S(2)}, u32[]{:S(2)}) collective-permute-start(bf16[64,4096]{1,0:T(8,128)(2,1)S(1)} %maximum_select_fusion.3), channel_id=1, source_target_pairs={{0,2},{1,5},{2,0},{3,7},{4,6},{5,1},{6,4},{7,3},{8,10},{9,13},{10,... | collective-permute-start | bytes 1572872 | tf_op jit(solution)/shard_map/ppermute | solution.py:42
  123.7 2.7 %collective-permute-start.12 = (bf16[128,4096]{1,0:T(8,128)(2,1)S(1)}, bf16[128,4096]{1,0:T(8,128)(2,1)S(1)}, u32[]{:S(2)}, u32[]{:S(2)}) collective-permute-start(bf16[128,4096]{1,0:T(8,128)(2,1)S(1)} %maximum_select_fusion.1.mine), channel_id=1, source_target_pairs={{0,1},{1,0},{2,3},{3,2},{4,5},{5,4},{6,7},{7,6},{8,9},{9,8},{10,11... | collective-permute-start | bytes 3145736 | tf_op jit(solution)/shard_map/ppermute | solution.py:359
  138.5 55.3 %collective-permute-start.17 = (bf16[256,2048]{1,0:T(8,128)(2,1)S(1)}, bf16[256,2048]{1,0:T(8,128)(2,1)S(1)}, u32[]{:S(2)}, u32[]{:S(2)}) collective-permute-start(bf16[256,2048]{1,0:T(8,128)(2,1)S(1)} %dynamic-slice_bitcast_fusion.2), channel_id=1, source_target_pairs={{0,16},{16,0},{1,17},{17,1},{2,18},{18,2},{3,19},{19,3},{4,20},{20... | collective-permute-start | bytes 3145736 | tf_op jit(solution)/shard_map/ppermute | solution.py:327
  139.1 38.0 %collective-permute-start.13 = (bf16[256,896]{1,0:T(8,128)(2,1)S(1)}, bf16[256,896]{1,0:T(8,128)(2,1)S(1)}, u32[]{:S(2)}, u32[]{:S(2)}) collective-permute-start(bf16[256,896]{1,0:T(8,128)(2,1)S(1)} %get-tuple-element.18.refs_3_), channel_id=1, source_target_pairs={{0,16},{16,0},{1,17},{17,1},{2,18},{18,2},{3,19},{19,3},{4,20},{20... | collective-permute-start | bytes 1376264 | tf_op jit(solution)/shard_map/ppermute | solution.py:327
  140.6 36.5 %collective-permute-start.14 = (f32[8,896]{1,0:T(8,128)S(1)}, f32[8,896]{1,0:T(8,128)S(1)}, u32[]{:S(2)}, u32[]{:S(2)}) collective-permute-start(f32[8,896]{1,0:T(8,128)S(1)} %get-tuple-element.19.refs_5_), channel_id=1, source_target_pairs={{0,16},{16,0},{1,17},{17,1},{2,18},{18,2},{3,19},{19,3},{4,20},{20... | collective-permute-start | bytes 86024 | tf_op jit(solution)/shard_map/ppermute | solution.py:327
  141.1 56.6 %collective-permute-start.16 = (bf16[128,2048]{1,0:T(8,128)(2,1)S(1)}, bf16[128,2048]{1,0:T(8,128)(2,1)S(1)}, u32[]{:S(2)}, u32[]{:S(2)}) collective-permute-start(bf16[128,2048]{1,0:T(8,128)(2,1)S(1)} %dynamic-slice_bitcast_fusion.3), channel_id=1, source_target_pairs={{0,16},{16,0},{1,17},{17,1},{2,18},{18,2},{3,19},{19,3},{4,20},{20... | collective-permute-start | bytes 1572872 | tf_op jit(solution)/shard_map/ppermute | solution.py:327

commit v2 on v1

--- a/solution.py
+++ b/solution.py
@@ -1,4 +1,5 @@
 import functools
+import math
 
 import jax
 import jax.numpy as jnp
@@ -9,6 +10,7 @@
 
 F32 = jnp.float32
 BF16 = jnp.bfloat16
+LANES = 128
 NT = (((1,), (1,)), ((), ()))
 NN = (((1,), (0,)), ((), ()))
 TN = (((0,), (0,)), ((), ()))
@@ -61,20 +63,21 @@
     return value
 
 
-def gather(value, axis, n):
-    for even, odd in reversed(hops(n)):
+def gather(value, axis, n, plan, after=lambda step, value: value):
+    for step, (even, odd) in enumerate(reversed(plan)):
         other = swap(value, axis, n, even, odd)
         first = side(axis, even, odd) == 0
         value = jnp.where(
             first, jnp.concatenate([value, other]), jnp.concatenate([other, value])
         )
+        value = after(step, value)
     return value
 
 
-def gather_order(n):
+def gather_order(n, plan):
     order = []
     for core in (0, 1):
-        bits = [pair[core] for pair in reversed(hops(n))]
+        bits = [pair[core] for pair in reversed(plan)]
         for place in range(n // 2):
             order.append(core + sum(((place >> j) & 1) << b for j, b in enumerate(bits)))
     return order
@@ -175,45 +178,26 @@
     )(core, x, gate, upper, down, row, col)
 
 
-def backward_kernel(core, mine, other, down, x, p, q, act, sd, grads, scale):
-    tokens, width = x.shape
-    units = down.shape[0]
+def backward_kernel(core, mine, other, down, p, q, act, sd, grads):
+    tokens = mine.shape[0]
     g_mine = dot(mine[...], down[...], NT)
     g_other = dot(other[...], down[...], NT)
     even = core[0] == 0
     gh = jnp.where(even, g_mine, g_other)
     gdh = jnp.where(even, g_other, g_mine)
-    both = (
-        (gdh * p[...] + gh * q[...]).astype(BF16),
-        (gdh * act[...] + gh * sd[...]).astype(BF16),
-    )
-    tile = tile_of(width)
-    lanes = 128 if tile % 128 == 0 else tile
-    rows = []
-    for k, grad in enumerate(both):
-        grads[k * tokens:(k + 1) * tokens, :] = grad
-        total = jnp.zeros((units, lanes), F32)
-        for at in range(0, width, tile):
-            e = jnp.abs(dot(grad, x[:, at:at + tile], TN))
-            for low in range(0, tile, lanes):
-                total = total + e[:, low:low + lanes]
-        mean = jnp.sum(total.T, axis=0, keepdims=True) * (1.0 / width)
-        rows.append(1.0 / (mean + 1e-06))
-    scale[...] = jnp.concatenate(rows + [jnp.zeros((6, units), F32)], axis=0)
-
-
-def backward(core, mine, other, down, x, kept):
-    tokens, width = x.shape
+    grads[:, :tokens] = (gdh * p[...] + gh * q[...]).T.astype(BF16)
+    grads[:, tokens:] = (gdh * act[...] + gh * sd[...]).T.astype(BF16)
+
+
+def backward(core, mine, other, down, kept):
+    tokens, width = mine.shape
     units = down.shape[0]
     block = rows_of(units)
     by_lane = pl.BlockSpec((tokens, block), lambda i, c: (0, i))
     fixed = pl.BlockSpec((tokens, width), lambda i, c: (0, 0))
     return pl.pallas_call(
         backward_kernel,
-        out_shape=(
-            jax.ShapeDtypeStruct((2 * tokens, units), BF16),
-            jax.ShapeDtypeStruct((8, units), F32),
-        ),
+        out_shape=jax.ShapeDtypeStruct((units, 2 * tokens), BF16),
         grid_spec=pltpu.PrefetchScalarGridSpec(
             num_scalar_prefetch=1,
             grid=(units // block,),
@@ -221,24 +205,60 @@
                 fixed,
                 fixed,
                 pl.BlockSpec((block, width), lambda i, c: (i, 0)),
-                fixed,
             ] + [by_lane] * 4,
-            out_specs=[
-                pl.BlockSpec((2 * tokens, block), lambda i, c: (0, i)),
-                pl.BlockSpec((8, block), lambda i, c: (0, i)),
-            ],
+            out_specs=pl.BlockSpec((block, 2 * tokens), lambda i, c: (i, 0)),
         ),
         compiler_params=params(),
         cost_estimate=pl.CostEstimate(
-            flops=8 * tokens * width * units,
+            flops=4 * tokens * width * units,
             bytes_accessed=2 * units * width,
             transcendentals=0,
         ),
         name="backward",
-    )(core, mine, other, down, x, *kept)
-
-
-def merge_kernel(which, members, *refs):
+    )(core, mine, other, down, *kept)
+
+
+def means_kernel(grads, x, scale):
+    tokens, width = x.shape
+    units = grads.shape[0]
+    tile = tile_of(width)
+    for k in (0, 1):
+        grad = grads[:, k * tokens:(k + 1) * tokens]
+        total = jnp.zeros((units, LANES), F32)
+        for at in range(0, width, tile):
+            e = jnp.abs(dot(grad, x[:, at:at + tile], NN))
+            for low in range(0, tile, LANES):
+                total = total + e[:, low:low + LANES]
+        mean = jnp.sum(total, axis=1, keepdims=True) * (1.0 / width)
+        scale[:, k * LANES:(k + 1) * LANES] = jnp.broadcast_to(
+            1.0 / (mean + 1e-06), (units, LANES)
+        )
+
+
+def means(grads, x):
+    tokens, width = x.shape
+    units = grads.shape[0]
+    block = rows_of(units)
+    return pl.pallas_call(
+        means_kernel,
+        out_shape=jax.ShapeDtypeStruct((units, 2 * LANES), F32),
+        grid=(units // block,),
+        in_specs=[
+            pl.BlockSpec((block, 2 * tokens), lambda i: (i, 0)),
+            pl.BlockSpec((tokens, width), lambda i: (0, 0)),
+        ],
+        out_specs=pl.BlockSpec((block, 2 * LANES), lambda i: (i, 0)),
+        compiler_params=params(),
+        cost_estimate=pl.CostEstimate(
+            flops=4 * tokens * width * units,
+            bytes_accessed=2 * tokens * width,
+            transcendentals=0,
+        ),
+        name="means",
+    )(grads, x)
+
+
+def merge_kernel(members, *refs):
     refs = refs[1:]
     weights, refs = refs[:members], refs[members:]
     grads, refs = refs[:members], refs[members:]
@@ -247,11 +267,11 @@
     out = refs[-1]
     width = out.shape[1]
     tile = tile_of(width)
-    columns = [scale[...].T[:, which:which + 1] for scale in scales]
+    columns = [scale[:, :1] for scale in scales]
     for at in range(0, width, tile):
         numer = denom = None
         for j in range(members):
-            hz = dot(grads[j][...], tokens[j][:, at:at + tile], TN)
+            hz = dot(grads[j][...], tokens[j][:, at:at + tile], NN)
             w = jnp.abs(hz) * columns[j]
             term = (w * weights[j][:, at:at + tile].astype(F32)).astype(BF16).astype(F32)
             w = w.astype(BF16).astype(F32)
@@ -260,27 +280,27 @@
         out[:, at:at + tile] = (numer / jnp.maximum(denom, 1.0)).astype(BF16)
 
 
-def merge(spot, which, start, weight, received, grads, scales, x, others, so_far):
-    members = 1 + len(received)
+def merge(spot, piece, weight, received, grads, scales, xs, so_far):
+    which, start, rows = piece
+    members = len(xs)
     units = weight.shape[0]
-    tokens, width = others[0].shape
-    block = rows_of(units)
-    rows = received[0].shape[0]
+    tokens = xs[0].shape[0]
+    width = received[0].shape[1]
+    block = math.gcd(rows, start, 128 if rows > 256 else 32)
     first = start // block
     in_specs = [pl.BlockSpec((block, width), lambda i, c: (first + i, c[0]))]
     in_specs += [pl.BlockSpec((block, width), lambda i, c: (i, 0))] * (members - 1)
-    in_specs += [pl.BlockSpec((tokens, block), lambda i, c: (which, first + i))] * members
-    in_specs += [pl.BlockSpec((8, block), lambda i, c: (0, first + i))] * members
-    in_specs += [pl.BlockSpec((tokens, width), lambda i, c: (0, c[0]))]
-    in_specs += [pl.BlockSpec((tokens, width), lambda i, c: (0, 0))] * (members - 1)
-    args = [spot, weight, *received, *grads, *scales, x, *others]
+    in_specs += [pl.BlockSpec((block, tokens), lambda i, c: (first + i, which))] * members
+    in_specs += [pl.BlockSpec((block, LANES), lambda i, c: (first + i, which))] * members
+    in_specs += [pl.BlockSpec((tokens, width), lambda i, c: (0, c[0]))] * members
+    args = [spot, weight, *received, *grads, *scales, *xs]
     aliases = {}
     if so_far is not None:
         aliases = {len(args): 0}
         in_specs.append(pl.BlockSpec(memory_space=pl.ANY))
         args.append(so_far)
     return pl.pallas_call(
-        functools.partial(merge_kernel, which, members),
+        functools.partial(merge_kernel, members),
         out_shape=jax.ShapeDtypeStruct((units, width), BF16),
         grid_spec=pltpu.PrefetchScalarGridSpec(
             num_scalar_prefetch=1,
@@ -299,17 +319,106 @@
     )(*args)
 
 
+def prepare_kernel(members, *refs):
+    refs = refs[1:]
+    weight, refs = refs[0], refs[1:]
+    grads, refs = refs[:members], refs[members:]
+    scales, refs = refs[:members], refs[members:]
+    tokens, outs = refs[:members], refs[members:]
+    numer, factor, others = outs[0], outs[1], outs[2:]
+    width = numer.shape[1]
+    tile = tile_of(width)
+    columns = [scale[:, :1] for scale in scales]
+    for at in range(0, width, tile):
+        denom = None
+        for j in range(members):
+            w = jnp.abs(dot(grads[j][...], tokens[j][:, at:at + tile], NN)) * columns[j]
+            if j == 0:
+                term = w * weight[:, at:at + tile].astype(F32)
+                numer[:, at:at + tile] = term.astype(BF16)
+            else:
+                others[j - 1][:, at:at + tile] = w
+            w = w.astype(BF16).astype(F32)
+            denom = w if denom is None else denom + w
+        factor[:, at:at + tile] = 1.0 / jnp.maximum(denom, 1.0)
+
+
+def prepare(spot, piece, weight, grads, scales, xs):
+    which, start, rows = piece
+    members = len(xs)
+    tokens = xs[0].shape[0]
+    width = weight.shape[1] // members
+    block = math.gcd(rows, start, 32)
+    first = start // block
+    own = pl.BlockSpec((block, width), lambda i, c: (first + i, c[0]))
+    in_specs = [own]
+    in_specs += [pl.BlockSpec((block, tokens), lambda i, c: (first + i, which))] * members
+    in_specs += [pl.BlockSpec((block, LANES), lambda i, c: (first + i, which))] * members
+    in_specs += [pl.BlockSpec((tokens, width), lambda i, c: (0, c[0]))] * members
+    return pl.pallas_call(
+        functools.partial(prepare_kernel, members),
+        out_shape=[jax.ShapeDtypeStruct((rows, width), BF16)]
+        + [jax.ShapeDtypeStruct((rows, width), F32)] * members,
+        grid_spec=pltpu.PrefetchScalarGridSpec(
+            num_scalar_prefetch=1,
+            grid=(rows // block,),
+            in_specs=in_specs,
+            out_specs=[pl.BlockSpec((block, width), lambda i, c: (i, 0))] * (members + 1),
+        ),
+        compiler_params=params(),
+        cost_estimate=pl.CostEstimate(
+            flops=2 * members * tokens * width * rows,
+            bytes_accessed=8 * (members + 1) * rows * width,
+            transcendentals=0,
+        ),
+        name="prepare",
+    )(spot, weight, *grads, *scales, *xs)
+
+
+def finish_kernel(members, numer, factor, *refs):
+    others, refs = refs[:members - 1], refs[members - 1:]
+    weights, out = refs[:members - 1], refs[-1]
+    total = numer[...].astype(F32)
+    for w, weight in zip(others, weights):
+        total = total + (w[...] * weight[...].astype(F32)).astype(BF16).astype(F32)
+    out[...] = (total * factor[...]).astype(BF16)
+
+
+def finish(piece, ready, received, so_far):
+    _, start, rows = piece
+    width = so_far.shape[1]
+    block = math.gcd(rows, start, 32)
+    first = start // block
+    args = [*ready, *received]
+    return pl.pallas_call(
+        functools.partial(finish_kernel, len(ready) - 1),
+        out_shape=jax.ShapeDtypeStruct(so_far.shape, BF16),
+        grid=(rows // block,),
+        in_specs=[pl.BlockSpec((block, width), lambda i: (i, 0))] * len(args)
+        + [pl.BlockSpec(memory_space=pl.ANY)],
+        out_specs=pl.BlockSpec((block, width), lambda i: (first + i, 0)),
+        input_output_aliases={len(args): 0},
+        compiler_params=params(),
+        cost_estimate=pl.CostEstimate(
+            flops=4 * rows * width, bytes_accessed=14 * rows * width, transcendentals=0
+        ),
+        name="finish",
+    )(*args, so_far)
+
+
 def pieces(units):
     block = rows_of(units)
     count = units // block
     if count < 4:
-        return [(0, 0, units), (1, 0, units)], []
-    last = block
-    third = block * max(1, count // 3)
-    head = units - last - third
+        return [], [(0, 0, units)], [(1, 0, units)], [], None
+    head = block * (count // 2)
+    tail = units - block
     return (
-        [(0, 0, units), (1, 0, head)],
-        [(1, head, third), (1, head + third, last)],
+        [(0, 0, block)],
+        [(0, block, units - block)],
+        [(1, 0, head)],
+        [(1, head, tail - head)],
+        (1, tail, block),
     )
 
 
@@ -322,55 +431,90 @@
     spot = lax.axis_index("ckpt")
     core = (lax.axis_index("fsdp") & 1).astype(jnp.int32).reshape(1)
     at = spot.astype(jnp.int32).reshape(1)
+    siblings = [(i, i ^ 1) for i in range(n_fsdp)]
+    shifts = range(1, n_ckpt)
 
     def across(value, shift):
         return lax.ppermute(
             value, "ckpt", [(i, (i + shift) % n_ckpt) for i in range(n_ckpt)]
         )
 
-    def cut(which, start, rows, shift):
-        left = lax.rem(spot + shift, n_ckpt) * part
-        return lax.dynamic_slice(weights[which], (start, left), (rows, part))
-
-    shifts = range(1, n_ckpt)
-    early, late = pieces(units)
-    arrived = {}
-    for piece in early:
-        arrived[piece] = [across(cut(*piece, s), s) for s in shifts]
-
-    x = gather(own, "fsdp", n_fsdp)
-    other = lax.ppermute(x, "fsdp", [(i, i ^ 1) for i in range(n_fsdp)])
-    even = core[0] == 0
-    x = jnp.where(even, jnp.concatenate([x, other]), jnp.concatenate([other, x]))
-
-    others = []
-    order = gather_order(n_fsdp)
+    def cut(which, start, rows):
+        lefts = [lax.rem(spot + s, n_ckpt) * part for s in shifts]
+        return [lax.dynamic_slice(weights[which], (start, left), (rows, part)) for left in lefts]
+
+    def cut_late(which, start, rows, spot):
+        step = math.gcd(rows, 32)
+        lefts = [lax.rem(spot + s, n_ckpt) * part for s in shifts]
+        return [
+            jnp.concatenate([
+                lax.dynamic_slice(weights[which], (low, left), (step, part))
+                for low in range(start, start + rows, step)
+            ]) for left in lefts
+        ]
+
+    def send_all(blocks):
+        return [across(block, s) for block, s in zip(blocks, shifts)]
+
+    def both(value):
+        other = lax.ppermute(value, "fsdp", siblings)
+        return jnp.where(
+            core[0] == 0, jnp.concatenate([value, other]), jnp.concatenate([other, value])
+        )
+
+    first, second, third, late, last = pieces(units)
+    arrived = {piece: send_all(cut(*piece)) for piece in first + second + third}
+
+    def have(some, value):
+        value, blocks = lax.optimization_barrier((value, [arrived[p] for p in some]))
+        arrived.update(zip(some, blocks))
+        return value
+
+    plan = hops(n_fsdp)
+    plain = [(even, even) for even, _ in plan]
+    x = both(gather(
+        own, "fsdp", n_fsdp, plan, lambda step, value: have(first, value) if step == 1 else value
+    ))
+    xs = [x]
+    places = gather_order(n_fsdp, plain)
     for s in shifts:
-        left = lax.rem(spot + s, n_ckpt) * part
-        mine = lax.dynamic_slice(own, (0, left), (own.shape[0], part))
-        natural = lax.all_gather(across(mine, s), "fsdp", axis=0, tiled=False)
-        others.append(jnp.concatenate([natural[i] for i in order]))
+        value = both(gather(across(own, s), "fsdp", n_fsdp, plain))
+        value = value.reshape(n_fsdp, *own.shape)
+        xs.append(jnp.concatenate(
+            [value[places.index(device)] for device in gather_order(n_fsdp, plan)]
+        ))
 
     *kept, send, keep = forward(
         core, x, weights[0], weights[1], down, row_code[0], col_code[0].T
     )
-    got = lax.ppermute(send, "fsdp", [(i, i ^ 1) for i in range(n_fsdp)])
-    total = gather(scatter_sum(add(keep, got), "fsdp", n_fsdp), "fsdp", n_fsdp)
-    other = lax.ppermute(total, "fsdp", [(i, i ^ 1) for i in range(n_fsdp)])
-    grads, scale = backward(core, total, other, down, x, kept)
-
+    send, later = lax.optimization_barrier((send, spot))
+    got = lax.ppermute(send, "fsdp", siblings)
+    total = scatter_sum(add(keep, got), "fsdp", n_fsdp)
+    total = gather(total, "fsdp", n_fsdp, plan)
+    other = lax.ppermute(total, "fsdp", siblings)
+    grads = backward(core, total, other, down, kept)
     all_grads = [grads] + [across(grads, s) for s in shifts]
-    all_scales = [scale] + [across(scale, s) for s in shifts]
-    for piece in late:
-        blocks, _ = lax.optimization_barrier(([cut(*piece, s) for s in shifts], grads))
-        arrived[piece] = [across(block, s) for block, s in zip(blocks, shifts)]
+    blocks, all_grads[1:] = lax.optimization_barrier(
+        ([cut_late(*p, later) for p in late], all_grads[1:])
+    )
+    arrived.update({p: send_all(b) for p, b in zip(late, blocks)})
+    scales = [means(grads, x)]
+    if last is not None:
+        blocks, scales = lax.optimization_barrier((cut_late(*last, later), scales))
+        arrived[last] = send_all(blocks)
+    scales += [means(g, v) for g, v in zip(all_grads[1:], xs[1:])]
 
     out = [None, None]
-    for which, start, rows in early + late:
+    for piece in first + second + third + late:
+        which = piece[0]
         out[which] = merge(
-            at, which, start, weights[which], arrived[which, start, rows], all_grads,
-            all_scales, x, others, out[which],
+            at, piece, weights[which], arrived[piece], all_grads, scales, xs, out[which]
         )
+    if last is not None:
+        which = last[0]
+        ready = prepare(at, last, weights[which], all_grads, scales, xs)
+        ready, out[which] = lax.optimization_barrier((ready, out[which]))
+        out[which] = finish(last, ready, arrived[last], out[which])
     return tuple(out)
 
 

time: 202 us -> 183 us (0.906)
  waiting for transfers between devices: 92.5 us -> 68.3 us
  blocking collectives: 23.6 us -> 0 us
  Pallas kernels: 51.4 us -> 63.2 us
  local copies, waits for them, and re-layouts: 11.1 us -> 22.4 us
  starting transfers between devices: 17.7 us -> 25.7 us
    all_gather x1 -> x0, blocking collectives: 23.6 us -> none  [on_device(): natural = lax.all_gather(across(mine, s), 'fsdp', axis=0, tiled=False)]
    ppermute x7, waiting for transfers between devices: 34.5 us -> 15.5 us  [across(): lax.ppermute(value, 'ckpt', [(i, (i + shift) % n_ckpt) for i in range(n_c...]
    pallas_call x5 -> x9, Pallas kernels: 35.5 us -> 46.9 us  [the longest x4 22.9 us: merge(): pl.pallas_call(functools.partial(merge_kernel, members), out_shape=jax.Sh...]
    unnamed x20 -> x49, local copies, waits for them, and re-layouts: 0.28 us -> 11.6 us
    ppermute x9 -> x12, starting transfers between devices: 8.46 us -> 15.1 us  [swap(): return lax.ppermute(value, axis, pairs)]
    ppermute x9 -> x12, waiting for transfers between devices: 55.4 us -> 48.9 us  [swap(): return lax.ppermute(value, axis, pairs)]
    dynamic_slice x5 -> x4, local copies, waits for them, and re-layouts: 10.7 us -> 8.92 us  [the longest x3 7.78 us: cut(): lax.dynamic_slice(weights[which], (start, left), (rows, part))]
  transfers between devices with their start and end apart: 19 -> 23, of which waited for: 10 -> 14; matrix products, arithmetic and copies ran while one was open for 7% -> 12% of each run, Pallas kernels for 24% -> 34%
where the time goes in v2:
time: 183 us; the launch traced here: 182 us
  waiting for transfers between devices  68.3 us (37%)
  Pallas kernels  63.2 us (35%)
  starting transfers between devices  25.7 us (14%)
  local copies, waits for them, and re-layouts  22.4 us (12%)
    ppermute x12, waiting for transfers between devices, swap(): return lax.ppermute(value, axis, pairs)  48.9 us
    pallas_call x4, Pallas kernels, merge(): pl.pallas_call(functools.partial(merge_kernel, members), out_shape=jax.Sh...  22.9 us
    pallas_call x1, Pallas kernels, forward(): pl.pallas_call(functools.partial(forward_kernel, width ** (-0.5), steps),...  16.2 us
    ppermute x7, waiting for transfers between devices, across(): lax.ppermute(value, 'ckpt', [(i, (i + shift) % n_ckpt) for i in range(n_c...  15.5 us
    ppermute x12, starting transfers between devices, swap(): return lax.ppermute(value, axis, pairs)  15.1 us
    unnamed x49, local copies, waits for them, and re-layouts  11.6 us
    pallas_call x2, Pallas kernels, means(): pl.pallas_call(means_kernel, out_shape=jax.ShapeDtypeStruct((units, 2 * L...  11 us
    ppermute x7, starting transfers between devices, across(): lax.ppermute(value, 'ckpt', [(i, (i + shift) % n_ckpt) for i in range(n_c...  9.99 us
  transfers between devices with their start and end apart: 23, of which 14 were waited for; matrix products, arithmetic and copies ran while one was open for 12% of the time, Pallas kernels for 34%

profile of v2, /device:TPU:0, one launch (start us, length us, event | category | flops | bytes accessed | tf_op | source)
XLA Modules:
  0.0 182.3 jit_solution(8742461926647565440)
XLA Ops:
  0.6 3.0 %collective-permute-start.15 = (bf16[8,4096]{1,0:T(8,128)(2,1)}, bf16[8,4096]{1,0:T(8,128)(2,1)S(1)}, u32[]{:S(2)}, u32[]{:S(2)}) collective-permute-start(bf16[8,4096]{1,0:T(8,128)(2,1)} %bitcast.59), channel_id=1, source_target_pairs={{0,16},{16,0},{1,17},{17,1},{2,18},{18,2},{3,19},{19,3},{4,20},{20... | collective-permute-start | bytes 196616 | tf_op jit(solution)/shard_map/ppermute | solution.py:438
  3.6 2.6 %collective-permute-start.1 = (bf16[8,4096]{1,0:T(8,128)(2,1)}, bf16[8,4096]{1,0:T(8,128)(2,1)S(1)}, u32[]{:S(2)}, u32[]{:S(2)}) collective-permute-start(bf16[8,4096]{1,0:T(8,128)(2,1)} %bitcast.60), channel_id=1, source_target_pairs={{0,8},{1,3},{2,10},{3,1},{4,12},{5,7},{6,14},{7,5},{8,0},{9,11},{1... | collective-permute-start | bytes 196616 | tf_op jit(solution)/shard_map/ppermute | solution.py:44
  9.2 2.7 %dynamic-slice_bitcast_fusion.1 = bf16[384,2048]{1,0:T(8,128)(2,1)} fusion(bf16[1,896,4096]{2,1,0:T(8,128)(2,1)} %param.8, s32[]{:T(128)S(6)} %select_n.132), kind=kLoop, calls=%fused_computation.2 | loop fusion | bytes 3145732 | tf_op jit(solution)/shard_map/dynamic_slice | solution.py:444
  13.5 1.6 collective-permute-start.17
  15.6 3.0 %collective-permute-done.17 = bf16[16,4096]{1,0:T(8,128)(2,1)S(1)} collective-permute-done((bf16[16,4096]{1,0:T(8,128)(2,1)S(1)}, bf16[16,4096]{1,0:T(8,128)(2,1)S(1)}, u32[]{:S(2)}, u32[]{:S(2)}) %collective-permute-start.17) | collective-permute-done | bytes 131104 | tf_op jit(solution)/shard_map/ppermute | solution.py:44
  18.7 2.6 %collective-permute-start.18 = (bf16[32,4096]{1,0:T(8,128)(2,1)S(1)}, bf16[32,4096]{1,0:T(8,128)(2,1)S(1)}, u32[]{:S(2)}, u32[]{:S(2)}) collective-permute-start(bf16[32,4096]{1,0:T(8,128)(2,1)S(1)} %maximum_select_fusion.8), channel_id=1, source_target_pairs={{0,2},{1,3},{2,0},{3,1},{4,6},{5,7},{6,4},{7,5},{8,10},{9,11},{10,... | collective-permute-start | bytes 786440 | tf_op jit(solution)/shard_map/ppermute | solution.py:44
  22.3 1.5 collective-permute-start.4
  23.8 1.9 %collective-permute-done.18 = bf16[32,4096]{1,0:T(8,128)(2,1)S(1)} collective-permute-done((bf16[32,4096]{1,0:T(8,128)(2,1)S(1)}, bf16[32,4096]{1,0:T(8,128)(2,1)S(1)}, u32[]{:S(2)}, u32[]{:S(2)}) %collective-permute-start.18) | collective-permute-done | bytes 262176 | tf_op jit(solution)/shard_map/ppermute | solution.py:44
  25.9 3.9 %dynamic-slice_bitcast_fusion = bf16[768,2048]{1,0:T(8,128)(2,1)} fusion(bf16[1,896,4096]{2,1,0:T(8,128)(2,1)} %param.7, s32[]{:T(128)S(6)} %select_n.132), kind=kLoop, calls=%fused_computation | loop fusion | bytes 6291460 | tf_op jit(solution)/shard_map/dynamic_slice | solution.py:444
  29.8 1.5 collective-permute-start
  33.8 16.2 %forward.1 = (f32[128,896]{1,0:T(8,128)S(1)}, f32[128,896]{1,0:T(8,128)S(1)}, f32[128,896]{1,0:T(8,128)S(1)}, f32[128,896]{1,0:T(8,128)S(1)}, bf16[128,4096]{1,0...) custom-call(s32[1]{0:T(128)} %bitcast.3.core, bf16[128,4096]{1,0:T(8,128)(2,1)S(1)} %maximum_select_fusion.x.refs_7_.refs_6_, ...), custom_call_target="tpu_custom_call" | custom-call | flops 5637144576 | bytes 22020096 | tf_op jit(solution)/shard_map/forward/pallas_call | solution.py:150
  50.4 2.4 %collective-permute-done.6 = bf16[128,4096]{1,0:T(8,128)(2,1)S(1)} collective-permute-done((bf16[128,4096]{1,0:T(8,128)(2,1)S(1)}, bf16[128,4096]{1,0:T(8,128)(2,1)S(1)}, u32[]{:S(2)}, u32[]{:S(2)}) %collective-permute-start.6) | collective-permute-done | bytes 1048608 | tf_op jit(solution)/shard_map/ppermute | solution.py:491
  53.2 1.6 collective-permute-start.7
  54.8 7.7 %collective-permute-done.7 = bf16[64,4096]{1,0:T(8,128)(2,1)S(1)} collective-permute-done((bf16[64,4096]{1,0:T(8,128)(2,1)S(1)}, bf16[64,4096]{1,0:T(8,128)(2,1)S(1)}, u32[]{:S(2)}, u32[]{:S(2)}) %collective-permute-start.7) | collective-permute-done | bytes 524320 | tf_op jit(solution)/shard_map/ppermute | solution.py:44
  63.5 8.0 %collective-permute-done.8 = bf16[32,4096]{1,0:T(8,128)(2,1)S(1)} collective-permute-done((bf16[32,4096]{1,0:T(8,128)(2,1)S(1)}, bf16[32,4096]{1,0:T(8,128)(2,1)S(1)}, u32[]{:S(2)}, u32[]{:S(2)}) %collective-permute-start.8) | collective-permute-done | bytes 262176 | tf_op jit(solution)/shard_map/ppermute | solution.py:44
  72.2 6.2 %collective-permute-done.9 = bf16[16,4096]{1,0:T(8,128)(2,1)S(1)} collective-permute-done((bf16[16,4096]{1,0:T(8,128)(2,1)S(1)}, bf16[16,4096]{1,0:T(8,128)(2,1)S(1)}, u32[]{:S(2)}, u32[]{:S(2)}) %collective-permute-start.9) | collective-permute-done | bytes 131104 | tf_op jit(solution)/shard_map/ppermute | solution.py:44
  78.6 10.4 %collective-permute-done.10 = bf16[16,4096]{1,0:T(8,128)(2,1)S(1)} collective-permute-done((bf16[16,4096]{1,0:T(8,128)(2,1)S(1)}, bf16[16,4096]{1,0:T(8,128)(2,1)S(1)}, u32[]{:S(2)}, u32[]{:S(2)}) %collective-permute-start.10) | collective-permute-done | bytes 131104 | tf_op jit(solution)/shard_map/ppermute | solution.py:44
  91.0 7.0 %collective-permute-done.11 = bf16[32,4096]{1,0:T(8,128)(2,1)S(1)} collective-permute-done((bf16[32,4096]{1,0:T(8,128)(2,1)S(1)}, bf16[32,4096]{1,0:T(8,128)(2,1)S(1)}, u32[]{:S(2)}, u32[]{:S(2)}) %collective-permute-start.11) | collective-permute-done | bytes 262176 | tf_op jit(solution)/shard_map/ppermute | solution.py:44
  98.0 1.7 collective-permute-start.12
  102.6 4.7 %collective-permute-done.12 = bf16[64,4096]{1,0:T(8,128)(2,1)S(1)} collective-permute-done((bf16[64,4096]{1,0:T(8,128)(2,1)S(1)}, bf16[64,4096]{1,0:T(8,128)(2,1)S(1)}, u32[]{:S(2)}, u32[]{:S(2)}) %collective-permute-start.12) | collective-permute-done | bytes 524320 | tf_op jit(solution)/shard_map/ppermute | solution.py:44
  112.4 8.2 %backward.1.grads.refs_3_.refs_2_ = bf16[896,256]{1,0:T(8,128)(2,1)S(1)} custom-call(s32[1]{0:T(128)} %bitcast.3.core, bf16[128,4096]{1,0:T(8,128)(2,1)S(1)} %maximum_select_fusion.1.mine, bf16[128,4096]{1,0:T(8,128)(2,1)S(1)} %collective-permute-done.13.other, bf16[896,4096]{1,0:T(8,128)(2,1)} %bitcast.58, f32[128,896]{1,0:T(8,128)S(1)} %get-tuple-element.27.p, ...), custom_call_target="tpu_custom_call" | custom-call | flops 1879048192 | bytes 7340032 | tf_op jit(solution)/shard_map/backward/pallas_call | solution.py:198
  124.7 8.9 %collective-permute-done.14.grads.refs_4_.refs_3_ = bf16[896,256]{1,0:T(8,128)(2,1)S(1)} collective-permute-done((bf16[896,256]{1,0:T(8,128)(2,1)S(1)}, bf16[896,256]{1,0:T(8,128)(2,1)S(1)}, u32[]{:S(2)}, u32[]{:S(2)}) %collective-permute-start.14) | collective-permute-done | bytes 458784 | tf_op jit(solution)/shard_map/ppermute | solution.py:438
  134.9 5.5 %means.2.refs_5_.refs_4_ = f32[896,256]{1,0:T(8,128)S(1)} custom-call(bf16[896,256]{1,0:T(8,128)(2,1)S(1)} %backward.1.grads.refs_3_.refs_2_, bf16[128,4096]{1,0:T(8,128)(2,1)S(1)} %maximum_select_fusion.x.refs_7_.refs_6_), custom_call_target="tpu_custom_call" | custom-call | flops 1879048192 | bytes 1048576 | tf_op jit(solution)/shard_map/means/pallas_call | solution.py:242
  142.1 5.5 %means.3.refs_6_.refs_5_ = f32[896,256]{1,0:T(8,128)S(1)} custom-call(bf16[896,256]{1,0:T(8,128)(2,1)S(1)} %collective-permute-done.14.grads.refs_4_.refs_3_, bf16[128,4096]{1,0:T(8,128)(2,1)S(1)} %slice_dynamic-update-slice_fusion.1.x.refs_8_.refs_7_), custom_call_target="tpu_custom_call" | custom-call | flops 1879048192 | bytes 1048576 | tf_op jit(solution)/shard_map/means/pallas_call | solution.py:242
  147.6 3.3 %prepare.1 = (bf16[128,2048]{1,0:T(8,128)(2,1)S(1)}, f32[128,2048]{1,0:T(8,128)S(1)}, f32[128,2048]{1,0:T(8,128)S(1)}) custom-call(s32[1]{0:T(128)} %bitcast.refs_0_, bf16[896,4096]{1,0:T(8,128)(2,1)} %bitcast.51, bf16[896,256]{1,0:T(8,128)(2,1)S(1)} %backward.1.grads.refs_3_.refs_2_, bf16[896,256]{1,0:T(8,128)(2,1)S(1)} %collective-permute-done.14.grads.refs_4_.refs_3_, ...), custom_call_target="tpu_custom_call" | custom-call | flops 134217728 | bytes 6291456 | tf_op jit(solution)/shard_map/prepare/pallas_call | solution.py:358
  151.0 3.8 %merge.4.refs_9_ = bf16[896,2048]{1,0:T(8,128)(2,1)} custom-call(s32[1]{0:T(128)} %bitcast.refs_0_, bf16[896,4096]{1,0:T(8,128)(2,1)} %bitcast.55, bf16[128,2048]{1,0:T(8,128)(2,1)S(1)} %collective-permute-done.3.refs_2_, bf16[896,256]{1,0:T(8,128)(2,1)S(1)} %backward.1.grads.refs_3_.refs_2_, ...), custom_call_target="tpu_custom_call" | custom-call | flops 134217728 | bytes 1572864 | tf_op jit(solution)/shard_map/merge/pallas_call | solution.py:302
  154.8 5.2 %merge.6.refs_9_ = bf16[896,2048]{1,0:T(8,128)(2,1)} custom-call(s32[1]{0:T(128)} %bitcast.refs_0_, bf16[896,4096]{1,0:T(8,128)(2,1)} %bitcast.52, bf16[384,2048]{1,0:T(8,128)(2,1)} %collective-permute-done.21.refs_2_, bf16[896,256]{1,0:T(8,128)(2,1)S(1)} %backward.1.grads.refs_3_.refs_2_, ...), custom_call_target="tpu_custom_call" | custom-call | flops 402653184 | bytes 4718592 | tf_op jit(solution)/shard_map/merge/pallas_call | solution.py:302
  160.1 8.7 %merge.5 = bf16[896,2048]{1,0:T(8,128)(2,1)} custom-call(s32[1]{0:T(128)} %bitcast.refs_0_, bf16[896,4096]{1,0:T(8,128)(2,1)} %bitcast.56, bf16[768,2048]{1,0:T(8,128)(2,1)} %collective-permute-done.refs_2_, bf16[896,256]{1,0:T(8,128)(2,1)S(1)} %backward.1.grads.refs_3_.refs_2_, ...), custom_call_target="tpu_custom_call", output_to_operand_aliasing={{}: (9, {})} | custom-call | flops 805306368 | bytes 9437184 | tf_op jit(solution)/shard_map/merge/pallas_call | solution.py:302
  168.7 2.2 %collective-permute-done.20.refs_2_ = bf16[384,2048]{1,0:T(8,128)(2,1)S(1)} collective-permute-done((bf16[384,2048]{1,0:T(8,128)(2,1)S(1)}, bf16[384,2048]{1,0:T(8,128)(2,1)S(1)}, u32[]{:S(2)}, u32[]{:S(2)}) %collective-permute-start.20) | collective-permute-done | bytes 1572896 | tf_op jit(solution)/shard_map/ppermute | solution.py:438
  172.1 5.2 %merge.7.refs_2_ = bf16[896,2048]{1,0:T(8,128)(2,1)} custom-call(s32[1]{0:T(128)} %bitcast.refs_0_, bf16[896,4096]{1,0:T(8,128)(2,1)} %bitcast.53, bf16[384,2048]{1,0:T(8,128)(2,1)} %copy-done.12, bf16[896,256]{1,0:T(8,128)(2,1)S(1)} %backward.1.grads.refs_3_.refs_2_, ...), custom_call_target="tpu_custom_call", output_to_operand_aliasing={{}: (9, {})} | custom-call | flops 402653184 | bytes 4718592 | tf_op jit(solution)/shard_map/merge/pallas_call | solution.py:302
  177.3 3.5 %collective-permute-done.22.refs_1_ = bf16[128,2048]{1,0:T(8,128)(2,1)S(1)} collective-permute-done((bf16[128,2048]{1,0:T(8,128)(2,1)S(1)}, bf16[128,2048]{1,0:T(8,128)(2,1)S(1)}, u32[]{:S(2)}, u32[]{:S(2)}) %collective-permute-start.22) | collective-permute-done | bytes 524320 | tf_op jit(solution)/shard_map/ppermute | solution.py:438
  180.8 1.5 finish.1
  (98 shorter events, 29.2 us)
Async XLA Ops:
  0.6 7.3 %collective-permute-start.15 = (bf16[8,4096]{1,0:T(8,128)(2,1)}, bf16[8,4096]{1,0:T(8,128)(2,1)S(1)}, u32[]{:S(2)}, u32[]{:S(2)}) collective-permute-start(bf16[8,4096]{1,0:T(8,128)(2,1)} %bitcast.59), channel_id=1, source_target_pairs={{0,16},{16,0},{1,17},{17,1},{2,18},{18,2},{3,19},{19,3},{4,20},{20... | collective-permute-start | bytes 196616 | tf_op jit(solution)/shard_map/ppermute | solution.py:438
  3.6 11.5 %collective-permute-start.1 = (bf16[8,4096]{1,0:T(8,128)(2,1)}, bf16[8,4096]{1,0:T(8,128)(2,1)S(1)}, u32[]{:S(2)}, u32[]{:S(2)}) collective-permute-start(bf16[8,4096]{1,0:T(8,128)(2,1)} %bitcast.60), channel_id=1, source_target_pairs={{0,8},{1,3},{2,10},{3,1},{4,12},{5,7},{6,14},{7,5},{8,0},{9,11},{1... | collective-permute-start | bytes 196616 | tf_op jit(solution)/shard_map/ppermute | solution.py:44
  6.2 8.9 %copy-start.13 = (bf16[1,8,4096]{2,1,0:T(8,128)(2,1)S(1)}, bf16[1,8,4096]{2,1,0:T(8,128)(2,1)}, u32[]{:S(2)}) copy-start(bf16[1,8,4096]{2,1,0:T(8,128)(2,1)} %param.6) | copy-start | bytes 196612
  7.3 14.9 %collective-permute-start.3 = (bf16[128,2048]{1,0:T(8,128)(2,1)S(1)}, bf16[128,2048]{1,0:T(8,128)(2,1)S(1)}, u32[]{:S(2)}, u32[]{:S(2)}) collective-permute-start(bf16[128,2048]{1,0:T(8,128)(2,1)S(1)} %dynamic-slice_bitcast_fusion.2), channel_id=1, source_target_pairs={{0,16},{16,0},{1,17},{17,1},{2,18},{18,2},{3,19},{19,3},{4,20},{20... | collective-permute-start | bytes 1572872 | tf_op jit(solution)/shard_map/ppermute | solution.py:438
  7.9 5.5 %collective-permute-start.16 = (bf16[8,4096]{1,0:T(8,128)(2,1)S(1)}, bf16[8,4096]{1,0:T(8,128)(2,1)S(1)}, u32[]{:S(2)}, u32[]{:S(2)}) collective-permute-start(bf16[8,4096]{1,0:T(8,128)(2,1)S(1)} %collective-permute-done.15), channel_id=1, source_target_pairs={{0,8},{1,9},{2,10},{3,11},{4,12},{5,13},{6,14},{7,15},{8,0},{9,1},... | collective-permute-start | bytes 196616 | tf_op jit(solution)/shard_map/ppermute | solution.py:44
  11.9 142.9 %collective-permute-start.21 = (bf16[384,2048]{1,0:T(8,128)(2,1)}, bf16[384,2048]{1,0:T(8,128)(2,1)}, u32[]{:S(2)}, u32[]{:S(2)}) collective-permute-start(bf16[384,2048]{1,0:T(8,128)(2,1)} %dynamic-slice_bitcast_fusion.1), channel_id=1, source_target_pairs={{0,16},{16,0},{1,17},{17,1},{2,18},{18,2},{3,19},{19,3},{4,20},{20... | collective-permute-start | bytes 4718600 | tf_op jit(solution)/shard_map/ppermute | solution.py:438
  13.5 5.2 %collective-permute-start.17 = (bf16[16,4096]{1,0:T(8,128)(2,1)S(1)}, bf16[16,4096]{1,0:T(8,128)(2,1)S(1)}, u32[]{:S(2)}, u32[]{:S(2)}) collective-permute-start(bf16[16,4096]{1,0:T(8,128)(2,1)S(1)} %maximum_select_fusion.10), channel_id=1, source_target_pairs={{0,4},{1,5},{2,6},{3,7},{4,0},{5,1},{6,2},{7,3},{8,12},{9,13},{10,... | collective-permute-start | bytes 393224 | tf_op jit(solution)/shard_map/ppermute | solution.py:44
  15.1 6.2 %collective-permute-start.2 = (bf16[16,4096]{1,0:T(8,128)(2,1)S(1)}, bf16[16,4096]{1,0:T(8,128)(2,1)S(1)}, u32[]{:S(2)}, u32[]{:S(2)}) collective-permute-start(bf16[16,4096]{1,0:T(8,128)(2,1)S(1)} %maximum_select_fusion.9), channel_id=1, source_target_pairs={{0,4},{1,9},{2,6},{3,11},{4,0},{5,13},{6,2},{7,15},{8,12},{9,1},{1... | collective-permute-start | bytes 393224 | tf_op jit(solution)/shard_map/ppermute | solution.py:44
  18.7 6.9 %collective-permute-start.18 = (bf16[32,4096]{1,0:T(8,128)(2,1)S(1)}, bf16[32,4096]{1,0:T(8,128)(2,1)S(1)}, u32[]{:S(2)}, u32[]{:S(2)}) collective-permute-start(bf16[32,4096]{1,0:T(8,128)(2,1)S(1)} %maximum_select_fusion.8), channel_id=1, source_target_pairs={{0,2},{1,3},{2,0},{3,1},{4,6},{5,7},{6,4},{7,5},{8,10},{9,11},{10,... | collective-permute-start | bytes 786440 | tf_op jit(solution)/shard_map/ppermute | solution.py:44
  22.3 9.3 %collective-permute-start.4 = (bf16[32,4096]{1,0:T(8,128)(2,1)S(1)}, bf16[32,4096]{1,0:T(8,128)(2,1)S(1)}, u32[]{:S(2)}, u32[]{:S(2)}) collective-permute-start(bf16[32,4096]{1,0:T(8,128)(2,1)S(1)} %maximum_select_fusion.6), channel_id=1, source_target_pairs={{0,2},{1,5},{2,0},{3,7},{4,6},{5,1},{6,4},{7,3},{8,10},{9,13},{10,... | collective-permute-start | bytes 786440 | tf_op jit(solution)/shard_map/ppermute | solution.py:44
  25.8 5.5 %copy-start.14 = (s32[1,2,896]{2,1,0:T(2,128)S(1)}, s32[1,2,896]{2,1,0:T(2,128)}, u32[]{:S(2)}) copy-start(s32[1,2,896]{2,1,0:T(2,128)} %param.11) | copy-start | bytes 21508
  25.8 6.1 %collective-permute-start.19 = (bf16[64,4096]{1,0:T(8,128)(2,1)S(1)}, bf16[64,4096]{1,0:T(8,128)(2,1)S(1)}, u32[]{:S(2)}, u32[]{:S(2)}) collective-permute-start(bf16[64,4096]{1,0:T(8,128)(2,1)S(1)} %maximum_select_fusion.5), channel_id=1, source_target_pairs={{0,1},{1,0},{2,3},{3,2},{4,5},{5,4},{6,7},{7,6},{8,9},{9,8},{10,11... | collective-permute-start | bytes 1572872 | tf_op jit(solution)/shard_map/ppermute | solution.py:460
  29.8 130.3 %collective-permute-start = (bf16[768,2048]{1,0:T(8,128)(2,1)}, bf16[768,2048]{1,0:T(8,128)(2,1)}, u32[]{:S(2)}, u32[]{:S(2)}) collective-permute-start(bf16[768,2048]{1,0:T(8,128)(2,1)} %dynamic-slice_bitcast_fusion), channel_id=1, source_target_pairs={{0,16},{16,0},{1,17},{17,1},{2,18},{18,2},{3,19},{19,3},{4,20},{20... | collective-permute-start | bytes 9437192 | tf_op jit(solution)/shard_map/ppermute | solution.py:438
  31.6 2.0 %collective-permute-start.5 = (bf16[64,4096]{1,0:T(8,128)(2,1)S(1)}, bf16[64,4096]{1,0:T(8,128)(2,1)S(1)}, u32[]{:S(2)}, u32[]{:S(2)}) collective-permute-start(bf16[64,4096]{1,0:T(8,128)(2,1)S(1)} %maximum_select_fusion.3), channel_id=1, source_target_pairs={{0,1},{1,0},{2,3},{3,2},{4,5},{5,4},{6,7},{7,6},{8,9},{9,8},{10,11... | collective-permute-start | bytes 1572872 | tf_op jit(solution)/shard_map/ppermute | solution.py:460
  32.1 46.4 %copy-start.11 = (bf16[128,4096]{1,0:T(8,128)(2,1)}, bf16[128,4096]{1,0:T(8,128)(2,1)S(1)}, u32[]{:S(2)}) copy-start(bf16[128,4096]{1,0:T(8,128)(2,1)S(1)} %maximum_select_fusion.2) | copy-start | bytes 3145732
  33.8 101.1 %copy-start = (bf16[128,4096]{1,0:T(8,128)(2,1)}, bf16[128,4096]{1,0:T(8,128)(2,1)S(1)}, u32[]{:S(2)}) copy-start(bf16[128,4096]{1,0:T(8,128)(2,1)S(1)} %maximum_select_fusion.x.refs_7_.refs_6_) | copy-start | bytes 3145732
  50.1 2.7 %collective-permute-start.6 = (bf16[128,4096]{1,0:T(8,128)(2,1)S(1)}, bf16[128,4096]{1,0:T(8,128)(2,1)S(1)}, u32[]{:S(2)}, u32[]{:S(2)}) collective-permute-start(bf16[128,4096]{1,0:T(8,128)(2,1)S(1)} %get-tuple-element.26), channel_id=1, source_target_pairs={{0,1},{1,0},{2,3},{3,2},{4,5},{5,4},{6,7},{7,6},{8,9},{9,8},{10,11... | collective-permute-start | bytes 3145736 | tf_op jit(solution)/shard_map/ppermute | solution.py:491
  53.2 9.2 %collective-permute-start.7 = (bf16[64,4096]{1,0:T(8,128)(2,1)S(1)}, bf16[64,4096]{1,0:T(8,128)(2,1)S(1)}, u32[]{:S(2)}, u32[]{:S(2)}) collective-permute-start(bf16[64,4096]{1,0:T(8,128)(2,1)S(1)} %constant_dynamic-slice_fusion.2), channel_id=1, source_target_pairs={{0,2},{1,5},{2,0},{3,7},{4,6},{5,1},{6,4},{7,3},{8,10},{9,13},{10,... | collective-permute-start | bytes 1572872 | tf_op jit(solution)/shard_map/ppermute | solution.py:44
  62.6 8.9 %collective-permute-start.8 = (bf16[32,4096]{1,0:T(8,128)(2,1)S(1)}, bf16[32,4096]{1,0:T(8,128)(2,1)S(1)}, u32[]{:S(2)}, u32[]{:S(2)}) collective-permute-start(bf16[32,4096]{1,0:T(8,128)(2,1)S(1)} %constant_dynamic-slice_fusion.1), channel_id=1, source_target_pairs={{0,4},{1,9},{2,6},{3,11},{4,0},{5,13},{6,2},{7,15},{8,12},{9,1},{1... | collective-permute-start | bytes 786440 | tf_op jit(solution)/shard_map/ppermute | solution.py:44
  71.6 6.8 %collective-permute-start.9 = (bf16[16,4096]{1,0:T(8,128)(2,1)S(1)}, bf16[16,4096]{1,0:T(8,128)(2,1)S(1)}, u32[]{:S(2)}, u32[]{:S(2)}) collective-permute-start(bf16[16,4096]{1,0:T(8,128)(2,1)S(1)} %constant_dynamic-slice_fusion), channel_id=1, source_target_pairs={{0,8},{1,3},{2,10},{3,1},{4,12},{5,7},{6,14},{7,5},{8,0},{9,11},{1... | collective-permute-start | bytes 393224 | tf_op jit(solution)/shard_map/ppermute | solution.py:44
  78.4 10.5 %collective-permute-start.10 = (bf16[16,4096]{1,0:T(8,128)(2,1)S(1)}, bf16[16,4096]{1,0:T(8,128)(2,1)S(1)}, u32[]{:S(2)}, u32[]{:S(2)}) collective-permute-start(bf16[16,4096]{1,0:T(8,128)(2,1)S(1)} %add_convert_fusion.3), channel_id=1, source_target_pairs={{0,8},{1,3},{2,10},{3,1},{4,12},{5,7},{6,14},{7,5},{8,0},{9,11},{1... | collective-permute-start | bytes 393224 | tf_op jit(solution)/shard_map/ppermute | solution.py:44
  89.0 8.9 %collective-permute-start.11 = (bf16[32,4096]{1,0:T(8,128)(2,1)S(1)}, bf16[32,4096]{1,0:T(8,128)(2,1)S(1)}, u32[]{:S(2)}, u32[]{:S(2)}) collective-permute-start(bf16[32,4096]{1,0:T(8,128)(2,1)S(1)} %maximum_select_fusion.7), channel_id=1, source_target_pairs={{0,4},{1,9},{2,6},{3,11},{4,0},{5,13},{6,2},{7,15},{8,12},{9,1},{1... | collective-permute-start | bytes 786440 | tf_op jit(solution)/shard_map/ppermute | solution.py:44
  98.0 9.2 %collective-permute-start.12 = (bf16[64,4096]{1,0:T(8,128)(2,1)S(1)}, bf16[64,4096]{1,0:T(8,128)(2,1)S(1)}, u32[]{:S(2)}, u32[]{:S(2)}) collective-permute-start(bf16[64,4096]{1,0:T(8,128)(2,1)S(1)} %maximum_select_fusion.4), channel_id=1, source_target_pairs={{0,2},{1,5},{2,0},{3,7},{4,6},{5,1},{6,4},{7,3},{8,10},{9,13},{10,... | collective-permute-start | bytes 1572872 | tf_op jit(solution)/shard_map/ppermute | solution.py:44
  102.5 9.9 %copy-start.5 = (f32[128,896]{1,0:T(8,128)S(1)}, f32[128,896]{1,0:T(8,128)}, u32[]{:S(2)}) copy-start(f32[128,896]{1,0:T(8,128)} %copy-done.4) | copy-start | bytes 1376260
  102.5 9.9 %copy-start.7 = (f32[128,896]{1,0:T(8,128)S(1)}, f32[128,896]{1,0:T(8,128)}, u32[]{:S(2)}) copy-start(f32[128,896]{1,0:T(8,128)} %copy-done.6) | copy-start | bytes 1376260
  102.5 9.9 %copy-start.9 = (f32[128,896]{1,0:T(8,128)S(1)}, f32[128,896]{1,0:T(8,128)}, u32[]{:S(2)}) copy-start(f32[128,896]{1,0:T(8,128)} %copy-done.8) | copy-start | bytes 1376260
  107.5 4.9 %collective-permute-start.13 = (bf16[128,4096]{1,0:T(8,128)(2,1)S(1)}, bf16[128,4096]{1,0:T(8,128)(2,1)S(1)}, u32[]{:S(2)}, u32[]{:S(2)}) collective-permute-start(bf16[128,4096]{1,0:T(8,128)(2,1)S(1)} %maximum_select_fusion.1.mine), channel_id=1, source_target_pairs={{0,1},{1,0},{2,3},{3,2},{4,5},{5,4},{6,7},{7,6},{8,9},{9,8},{10,11... | collective-permute-start | bytes 3145736 | tf_op jit(solution)/shard_map/ppermute | solution.py:494
  120.6 13.0 %collective-permute-start.14 = (bf16[896,256]{1,0:T(8,128)(2,1)S(1)}, bf16[896,256]{1,0:T(8,128)(2,1)S(1)}, u32[]{:S(2)}, u32[]{:S(2)}) collective-permute-start(bf16[896,256]{1,0:T(8,128)(2,1)S(1)} %backward.1.grads.refs_3_.refs_2_), channel_id=1, source_target_pairs={{0,16},{16,0},{1,17},{17,1},{2,18},{18,2},{3,19},{19,3},{4,20},{20... | collective-permute-start | bytes 1376264 | tf_op jit(solution)/shard_map/ppermute | solution.py:438
  133.6 37.3 %collective-permute-start.20 = (bf16[384,2048]{1,0:T(8,128)(2,1)S(1)}, bf16[384,2048]{1,0:T(8,128)(2,1)S(1)}, u32[]{:S(2)}, u32[]{:S(2)}) collective-permute-start(bf16[384,2048]{1,0:T(8,128)(2,1)S(1)} %bitcast_dynamic-update-slice_fusion), channel_id=1, source_target_pairs={{0,16},{16,0},{1,17},{17,1},{2,18},{18,2},{3,19},{19,3},{4,20},{20... | collective-permute-start | bytes 4718600 | tf_op jit(solution)/shard_map/ppermute | solution.py:438
  140.4 40.4 %collective-permute-start.22 = (bf16[128,2048]{1,0:T(8,128)(2,1)S(1)}, bf16[128,2048]{1,0:T(8,128)(2,1)S(1)}, u32[]{:S(2)}, u32[]{:S(2)}) collective-permute-start(bf16[128,2048]{1,0:T(8,128)(2,1)S(1)} %pad_maximum_fusion), channel_id=1, source_target_pairs={{0,16},{16,0},{1,17},{17,1},{2,18},{18,2},{3,19},{19,3},{4,20},{20... | collective-permute-start | bytes 1572872 | tf_op jit(solution)/shard_map/ppermute | solution.py:438
  142.1 5.5 %copy-start.2 = (bf16[128,4096]{1,0:T(8,128)(2,1)}, bf16[128,4096]{1,0:T(8,128)(2,1)S(1)}, u32[]{:S(2)}) copy-start(bf16[128,4096]{1,0:T(8,128)(2,1)S(1)} %slice_dynamic-update-slice_fusion.1.x.refs_8_.refs_7_) | copy-start | bytes 3145732
  147.6 3.4 %copy-start.1 = (bf16[128,4096]{1,0:T(8,128)(2,1)S(1)}, bf16[128,4096]{1,0:T(8,128)(2,1)}, u32[]{:S(2)}) copy-start(bf16[128,4096]{1,0:T(8,128)(2,1)} %copy-done) | copy-start | bytes 3145732
  (6 other events, 15.5 us)

commit v3 on v2

--- a/solution.py
+++ b/solution.py
@@ -28,6 +28,10 @@
 
 def rows_of(units):
     return 128 if units % 128 == 0 else units
+
+
+def step_of(rows):
+    return max((b for b in range(16, 129, 16) if rows % b == 0), default=rows)
 
 
 def tile_of(width):
@@ -273,8 +277,7 @@
         for j in range(members):
             hz = dot(grads[j][...], tokens[j][:, at:at + tile], NN)
             w = jnp.abs(hz) * columns[j]
-            term = (w * weights[j][:, at:at + tile].astype(F32)).astype(BF16).astype(F32)
-            w = w.astype(BF16).astype(F32)
+            term = w * weights[j][:, at:at + tile].astype(F32)
             numer = term if numer is None else numer + term
             denom = w if denom is None else denom + w
         out[:, at:at + tile] = (numer / jnp.maximum(denom, 1.0)).astype(BF16)
@@ -286,7 +289,7 @@
     units = weight.shape[0]
     tokens = xs[0].shape[0]
     width = received[0].shape[1]
-    block = math.gcd(rows, start, 128 if rows > 256 else 32)
+    block = step_of(math.gcd(rows, start))
     first = start // block
     in_specs = [pl.BlockSpec((block, width), lambda i, c: (first + i, c[0]))]
     in_specs += [pl.BlockSpec((block, width), lambda i, c: (i, 0))] * (members - 1)
@@ -325,22 +328,20 @@
     grads, refs = refs[:members], refs[members:]
     scales, refs = refs[:members], refs[members:]
     tokens, outs = refs[:members], refs[members:]
-    numer, factor, others = outs[0], outs[1], outs[2:]
-    width = numer.shape[1]
+    share, others = outs[0], outs[1:]
+    width = share.shape[1]
     tile = tile_of(width)
     columns = [scale[:, :1] for scale in scales]
     for at in range(0, width, tile):
-        denom = None
-        for j in range(members):
-            w = jnp.abs(dot(grads[j][...], tokens[j][:, at:at + tile], NN)) * columns[j]
-            if j == 0:
-                term = w * weight[:, at:at + tile].astype(F32)
-                numer[:, at:at + tile] = term.astype(BF16)
-            else:
-                others[j - 1][:, at:at + tile] = w
-            w = w.astype(BF16).astype(F32)
-            denom = w if denom is None else denom + w
-        factor[:, at:at + tile] = 1.0 / jnp.maximum(denom, 1.0)
+        ws = [
+            jnp.abs(dot(grads[j][...], tokens[j][:, at:at + tile], NN)) * columns[j]
+            for j in range(members)
+        ]
+        factor = 1.0 / jnp.maximum(sum(ws[1:], ws[0]), 1.0)
+        own = ws[0] * weight[:, at:at + tile].astype(F32)
+        share[:, at:at + tile] = (own * factor).astype(BF16)
+        for other, w in zip(others, ws[1:]):
+            other[:, at:at + tile] = (w * factor).astype(BF16)
 
 
 def prepare(spot, piece, weight, grads, scales, xs):
@@ -357,31 +358,30 @@
     in_specs += [pl.BlockSpec((tokens, width), lambda i, c: (0, c[0]))] * members
     return pl.pallas_call(
         functools.partial(prepare_kernel, members),
-        out_shape=[jax.ShapeDtypeStruct((rows, width), BF16)]
-        + [jax.ShapeDtypeStruct((rows, width), F32)] * members,
+        out_shape=[jax.ShapeDtypeStruct((rows, width), BF16)] * members,
         grid_spec=pltpu.PrefetchScalarGridSpec(
             num_scalar_prefetch=1,
             grid=(rows // block,),
             in_specs=in_specs,
-            out_specs=[pl.BlockSpec((block, width), lambda i, c: (i, 0))] * (members + 1),
+            out_specs=[pl.BlockSpec((block, width), lambda i, c: (i, 0))] * members,
         ),
         compiler_params=params(),
         cost_estimate=pl.CostEstimate(
             flops=2 * members * tokens * width * rows,
-            bytes_accessed=8 * (members + 1) * rows * width,
+            bytes_accessed=2 * (members + 1) * rows * width,
             transcendentals=0,
         ),
         name="prepare",
     )(spot, weight, *grads, *scales, *xs)
 
 
-def finish_kernel(members, numer, factor, *refs):
+def finish_kernel(members, share, *refs):
     others, refs = refs[:members - 1], refs[members - 1:]
     weights, out = refs[:members - 1], refs[-1]
-    total = numer[...].astype(F32)
+    total = share[...].astype(F32)
     for w, weight in zip(others, weights):
-        total = total + (w[...] * weight[...].astype(F32)).astype(BF16).astype(F32)
-    out[...] = (total * factor[...]).astype(BF16)
+        total = total + w[...].astype(F32) * weight[...].astype(F32)
+    out[...] = total.astype(BF16)
 
 
 def finish(piece, ready, received, so_far):
@@ -391,7 +391,7 @@
     first = start // block
     args = [*ready, *received]
     return pl.pallas_call(
-        functools.partial(finish_kernel, len(ready) - 1),
+        functools.partial(finish_kernel, len(ready)),
         out_shape=jax.ShapeDtypeStruct(so_far.shape, BF16),
         grid=(rows // block,),
         in_specs=[pl.BlockSpec((block, width), lambda i: (i, 0))] * len(args)
@@ -400,7 +400,7 @@
         input_output_aliases={len(args): 0},
         compiler_params=params(),
         cost_estimate=pl.CostEstimate(
-            flops=4 * rows * width, bytes_accessed=14 * rows * width, transcendentals=0
+            flops=2 * rows * width, bytes_accessed=8 * rows * width, transcendentals=0
         ),
         name="finish",
     )(*args, so_far)
@@ -411,14 +411,16 @@
     count = units // block
     if count < 4:
         return [], [(0, 0, units)], [(1, 0, units)], [], None
-    head = block * (count // 2)
-    tail = units - block
+    head = block * (count // 2 + 1)
+    tail = units - block // 2
+    count = -(-(tail - head) // block)
+    marks = [head + (tail - head) // 32 * i // count * 32 for i in range(count)] + [tail]
     return (
         [(0, 0, block)],
         [(0, block, units - block)],
         [(1, 0, head)],
-        [(1, head, tail - head)],
-        (1, tail, block),
+        [(1, low, high - low) for low, high in zip(marks, marks[1:])],
+        (1, tail, units - tail),
     )
 
 
@@ -444,7 +446,7 @@
         return [lax.dynamic_slice(weights[which], (start, left), (rows, part)) for left in lefts]
 
     def cut_late(which, start, rows, spot):
-        step = math.gcd(rows, 32)
+        step = math.gcd(rows, 16)
         lefts = [lax.rem(spot + s, n_ckpt) * part for s in shifts]
         return [
             jnp.concatenate([
@@ -472,13 +474,15 @@
 
     plan = hops(n_fsdp)
     plain = [(even, even) for even, _ in plan]
+    moved = [across(own, s) for s in shifts]
+    start, moved = lax.optimization_barrier((own, moved))
     x = both(gather(
-        own, "fsdp", n_fsdp, plan, lambda step, value: have(first, value) if step == 1 else value
+        start, "fsdp", n_fsdp, plan, lambda step, value: have(first, value) if step == 1 else value
     ))
     xs = [x]
     places = gather_order(n_fsdp, plain)
-    for s in shifts:
-        value = both(gather(across(own, s), "fsdp", n_fsdp, plain))
+    for value in moved:
+        value = both(gather(value, "fsdp", n_fsdp, plain))
         value = value.reshape(n_fsdp, *own.shape)
         xs.append(jnp.concatenate(
             [value[places.index(device)] for device in gather_order(n_fsdp, plan)]
@@ -494,26 +498,30 @@
     other = lax.ppermute(total, "fsdp", siblings)
     grads = backward(core, total, other, down, kept)
     all_grads = [grads] + [across(grads, s) for s in shifts]
-    blocks, all_grads[1:] = lax.optimization_barrier(
-        ([cut_late(*p, later) for p in late], all_grads[1:])
-    )
+    scales = [means(grads, x)]
+    blocks, scales = lax.optimization_barrier(([cut_late(*p, later) for p in late], scales))
     arrived.update({p: send_all(b) for p, b in zip(late, blocks)})
-    scales = [means(grads, x)]
     if last is not None:
-        blocks, scales = lax.optimization_barrier((cut_late(*last, later), scales))
+        blocks, all_grads[1:] = lax.optimization_barrier((cut_late(*last, later), all_grads[1:]))
         arrived[last] = send_all(blocks)
     scales += [means(g, v) for g, v in zip(all_grads[1:], xs[1:])]
 
     out = [None, None]
-    for piece in first + second + third + late:
+
+    def place(piece):
         which = piece[0]
         out[which] = merge(
             at, piece, weights[which], arrived[piece], all_grads, scales, xs, out[which]
         )
+
+    for piece in first + second + third:
+        place(piece)
     if last is not None:
         which = last[0]
         ready = prepare(at, last, weights[which], all_grads, scales, xs)
-        ready, out[which] = lax.optimization_barrier((ready, out[which]))
+        for piece in late:
+            ready, out, arrived[piece] = lax.optimization_barrier((ready, out, arrived[piece]))
+            place(piece)
         out[which] = finish(last, ready, arrived[last], out[which])
     return tuple(out)
 

time: 183 us -> 179 us (0.978)
  local copies, waits for them, and re-layouts: 22.4 us -> 17.6 us
  other arithmetic: 1.58 us -> 5.25 us
  starting transfers between devices: 25.7 us -> 23.5 us
    ppermute x12, waiting for transfers between devices: 48.9 us -> 62.3 us  [swap(): return lax.ppermute(value, axis, pairs)]
    ppermute x7 -> x9, waiting for transfers between devices: 15.5 us -> 3.59 us  [across(): lax.ppermute(value, 'ckpt', [(i, (i + shift) % n_ckpt) for i in range(n_c...]
    unnamed x49 -> x29, local copies, waits for them, and re-layouts: 11.6 us -> 7.47 us
    ppermute x12, starting transfers between devices: 15.1 us -> 11.4 us  [swap(): return lax.ppermute(value, axis, pairs)]
    select_n x9, other arithmetic: 0.65 us -> 3.05 us  [gather(): jnp.where(first, jnp.concatenate([value, other]), jnp.concatenate([other,...]
    pallas_call x4 -> x6, Pallas kernels: 22.9 us -> 24.9 us  [merge(): pl.pallas_call(functools.partial(merge_kernel, members), out_shape=jax.Sh...]
    ppermute x7 -> x9, starting transfers between devices: 9.99 us -> 11.4 us  [across(): lax.ppermute(value, 'ckpt', [(i, (i + shift) % n_ckpt) for i in range(n_c...]
  transfers between devices with their start and end apart: 23 -> 25, of which waited for: 14 -> 12; matrix products, arithmetic and copies ran while one was open for 12% -> 12% of each run, Pallas kernels for 34% -> 35%
where the time goes in v3:
time: 179 us; the launch traced here: 178 us
  waiting for transfers between devices  68.1 us (38%)
  Pallas kernels  62.5 us (35%)
  starting transfers between devices  23.5 us (13%)
  local copies, waits for them, and re-layouts  17.6 us (10%)
  other arithmetic  5.25 us (3%)
    ppermute x12, waiting for transfers between devices, swap(): return lax.ppermute(value, axis, pairs)  62.3 us
    pallas_call x6, Pallas kernels, merge(): pl.pallas_call(functools.partial(merge_kernel, members), out_shape=jax.Sh...  24.9 us
    pallas_call x1, Pallas kernels, forward(): pl.pallas_call(functools.partial(forward_kernel, width ** (-0.5), steps),...  16.1 us
    ppermute x9, starting transfers between devices, across(): lax.ppermute(value, 'ckpt', [(i, (i + shift) % n_ckpt) for i in range(n_c...  11.4 us
    ppermute x12, starting transfers between devices, swap(): return lax.ppermute(value, axis, pairs)  11.4 us
    pallas_call x2, Pallas kernels, means(): pl.pallas_call(means_kernel, out_shape=jax.ShapeDtypeStruct((units, 2 * L...  11 us
    dynamic_slice x3, local copies, waits for them, and re-layouts, cut(): lax.dynamic_slice(weights[which], (start, left), (rows, part))  8.17 us
    pallas_call x1, Pallas kernels, backward(): pl.pallas_call(backward_kernel, out_shape=jax.ShapeDtypeStruct((units, 2...  8.17 us
  transfers between devices with their start and end apart: 25, of which 12 were waited for; matrix products, arithmetic and copies ran while one was open for 12% of the time, Pallas kernels for 35%

profile of v3, /device:TPU:0, one launch (start us, length us, event | category | flops | bytes accessed | tf_op | source)
XLA Modules:
  0.0 178.0 jit_solution(10565015559571033367)
XLA Ops:
  0.6 3.0 %collective-permute-start = (bf16[8,4096]{1,0:T(8,128)(2,1)}, bf16[8,4096]{1,0:T(8,128)(2,1)S(1)}, u32[]{:S(2)}, u32[]{:S(2)}) collective-permute-start(bf16[8,4096]{1,0:T(8,128)(2,1)} %bitcast.77), channel_id=1, source_target_pairs={{0,16},{16,0},{1,17},{17,1},{2,18},{18,2},{3,19},{19,3},{4,20},{20... | collective-permute-start | bytes 196616 | tf_op jit(solution)/shard_map/ppermute | solution.py:440
  4.8 1.6 collective-permute-done
  6.4 2.8 %collective-permute-start.15 = (bf16[8,4096]{1,0:T(8,128)(2,1)S(1)}, bf16[8,4096]{1,0:T(8,128)(2,1)S(1)}, u32[]{:S(2)}, u32[]{:S(2)}) collective-permute-start(bf16[8,4096]{1,0:T(8,128)(2,1)S(1)} %collective-permute-done), channel_id=1, source_target_pairs={{0,8},{1,9},{2,10},{3,11},{4,12},{5,13},{6,14},{7,15},{8,0},{9,1},... | collective-permute-start | bytes 196616 | tf_op jit(solution)/shard_map/ppermute | solution.py:48
  9.2 3.9 %dynamic-slice_bitcast_fusion = bf16[768,2048]{1,0:T(8,128)(2,1)} fusion(bf16[1,896,4096]{2,1,0:T(8,128)(2,1)} %param.7, s32[]{:T(128)S(6)} %select_n.152), kind=kLoop, calls=%fused_computation | loop fusion | bytes 6291460 | tf_op jit(solution)/shard_map/dynamic_slice | solution.py:446
  13.1 2.1 %collective-permute-start.19 = (bf16[768,2048]{1,0:T(8,128)(2,1)}, bf16[768,2048]{1,0:T(8,128)(2,1)}, u32[]{:S(2)}, u32[]{:S(2)}) collective-permute-start(bf16[768,2048]{1,0:T(8,128)(2,1)} %dynamic-slice_bitcast_fusion), channel_id=1, source_target_pairs={{0,16},{16,0},{1,17},{17,1},{2,18},{18,2},{3,19},{19,3},{4,20},{20... | collective-permute-start | bytes 9437192 | tf_op jit(solution)/shard_map/ppermute | solution.py:440
  17.3 5.6 %collective-permute-done.1 = bf16[8,4096]{1,0:T(8,128)(2,1)S(1)} collective-permute-done((bf16[8,4096]{1,0:T(8,128)(2,1)S(1)}, bf16[8,4096]{1,0:T(8,128)(2,1)S(1)}, u32[]{:S(2)}, u32[]{:S(2)}) %collective-permute-start.1) | collective-permute-done | bytes 65568 | tf_op jit(solution)/shard_map/ppermute | solution.py:48
  23.1 1.6 collective-permute-start.17
  24.7 4.7 %collective-permute-done.2 = bf16[16,4096]{1,0:T(8,128)(2,1)S(1)} collective-permute-done((bf16[16,4096]{1,0:T(8,128)(2,1)S(1)}, bf16[16,4096]{1,0:T(8,128)(2,1)S(1)}, u32[]{:S(2)}, u32[]{:S(2)}) %collective-permute-start.2) | collective-permute-done | bytes 131104 | tf_op jit(solution)/shard_map/ppermute | solution.py:48
  31.2 4.7 %collective-permute-done.4 = bf16[32,4096]{1,0:T(8,128)(2,1)S(1)} collective-permute-done((bf16[32,4096]{1,0:T(8,128)(2,1)S(1)}, bf16[32,4096]{1,0:T(8,128)(2,1)S(1)}, u32[]{:S(2)}, u32[]{:S(2)}) %collective-permute-start.4) | collective-permute-done | bytes 262176 | tf_op jit(solution)/shard_map/ppermute | solution.py:48
  36.0 3.2 %dynamic-slice_bitcast_fusion.1 = bf16[512,2048]{1,0:T(8,128)(2,1)} fusion(bf16[1,896,4096]{2,1,0:T(8,128)(2,1)} %param.8, s32[]{:T(128)S(6)} %select_n.152), kind=kLoop, calls=%fused_computation.1 | loop fusion | bytes 4194308 | tf_op jit(solution)/shard_map/dynamic_slice | solution.py:446
  41.2 16.1 %forward.1 = (f32[128,896]{1,0:T(8,128)S(1)}, f32[128,896]{1,0:T(8,128)S(1)}, f32[128,896]{1,0:T(8,128)S(1)}, f32[128,896]{1,0:T(8,128)S(1)}, bf16[128,4096]{1,0...) custom-call(s32[1]{0:T(128)} %bitcast.2.core, bf16[128,4096]{1,0:T(8,128)(2,1)S(1)} %maximum_select_fusion.x.refs_6_.refs_7_, ...), custom_call_target="tpu_custom_call" | custom-call | flops 5637144576 | bytes 22020096 | tf_op jit(solution)/shard_map/forward/pallas_call | solution.py:154
  58.6 2.2 %collective-permute-done.6 = bf16[128,4096]{1,0:T(8,128)(2,1)S(1)} collective-permute-done((bf16[128,4096]{1,0:T(8,128)(2,1)S(1)}, bf16[128,4096]{1,0:T(8,128)(2,1)S(1)}, u32[]{:S(2)}, u32[]{:S(2)}) %collective-permute-start.6) | collective-permute-done | bytes 1048608 | tf_op jit(solution)/shard_map/ppermute | solution.py:495
  62.7 7.7 %collective-permute-done.7 = bf16[64,4096]{1,0:T(8,128)(2,1)S(1)} collective-permute-done((bf16[64,4096]{1,0:T(8,128)(2,1)S(1)}, bf16[64,4096]{1,0:T(8,128)(2,1)S(1)}, u32[]{:S(2)}, u32[]{:S(2)}) %collective-permute-start.7) | collective-permute-done | bytes 524320 | tf_op jit(solution)/shard_map/ppermute | solution.py:48
  70.7 9.0 %collective-permute-done.8 = bf16[32,4096]{1,0:T(8,128)(2,1)S(1)} collective-permute-done((bf16[32,4096]{1,0:T(8,128)(2,1)S(1)}, bf16[32,4096]{1,0:T(8,128)(2,1)S(1)}, u32[]{:S(2)}, u32[]{:S(2)}) %collective-permute-start.8) | collective-permute-done | bytes 262176 | tf_op jit(solution)/shard_map/ppermute | solution.py:48
  79.8 6.3 %collective-permute-done.9 = bf16[16,4096]{1,0:T(8,128)(2,1)S(1)} collective-permute-done((bf16[16,4096]{1,0:T(8,128)(2,1)S(1)}, bf16[16,4096]{1,0:T(8,128)(2,1)S(1)}, u32[]{:S(2)}, u32[]{:S(2)}) %collective-permute-start.9) | collective-permute-done | bytes 131104 | tf_op jit(solution)/shard_map/ppermute | solution.py:48
  86.2 10.4 %collective-permute-done.10 = bf16[16,4096]{1,0:T(8,128)(2,1)S(1)} collective-permute-done((bf16[16,4096]{1,0:T(8,128)(2,1)S(1)}, bf16[16,4096]{1,0:T(8,128)(2,1)S(1)}, u32[]{:S(2)}, u32[]{:S(2)}) %collective-permute-start.10) | collective-permute-done | bytes 131104 | tf_op jit(solution)/shard_map/ppermute | solution.py:48
  96.7 7.8 %collective-permute-done.11 = bf16[32,4096]{1,0:T(8,128)(2,1)S(1)} collective-permute-done((bf16[32,4096]{1,0:T(8,128)(2,1)S(1)}, bf16[32,4096]{1,0:T(8,128)(2,1)S(1)}, u32[]{:S(2)}, u32[]{:S(2)}) %collective-permute-start.11) | collective-permute-done | bytes 262176 | tf_op jit(solution)/shard_map/ppermute | solution.py:48
  108.7 6.2 %collective-permute-done.12 = bf16[64,4096]{1,0:T(8,128)(2,1)} collective-permute-done((bf16[64,4096]{1,0:T(8,128)(2,1)}, bf16[64,4096]{1,0:T(8,128)(2,1)}, u32[]{:S(2)}, u32[]{:S(2)}) %collective-permute-start.12) | collective-permute-done | bytes 524320 | tf_op jit(solution)/shard_map/ppermute | solution.py:48
  114.9 1.8 %maximum_select_fusion.1.mine = bf16[128,4096]{1,0:T(8,128)(2,1)S(1)} fusion(bf16[64,4096]{1,0:T(8,128)(2,1)} %collective-permute-done.12, bf16[64,4096]{1,0:T(8,128)(2,1)} %maximum_select_fusion.4, pred[]{:T(512)S(6)} %eq.17), kind=kLoop, calls=%fused_computation.4 | loop fusion | flops 4718592 | bytes 2097153 | tf_op jit(solution)/shard_map/jit(_where)/select_n | solution.py:74
  121.5 8.2 %backward.1.grads.refs_2_.refs_3_ = bf16[896,256]{1,0:T(8,128)(2,1)S(1)} custom-call(s32[1]{0:T(128)} %bitcast.2.core, bf16[128,4096]{1,0:T(8,128)(2,1)S(1)} %maximum_select_fusion.1.mine, bf16[128,4096]{1,0:T(8,128)(2,1)S(1)} %collective-permute-done.13.other, bf16[896,4096]{1,0:T(8,128)(2,1)} %bitcast.76, f32[128,896]{1,0:T(8,128)S(1)} %get-tuple-element.42.p, ...), custom_call_target="tpu_custom_call" | custom-call | flops 1879048192 | bytes 7340032 | tf_op jit(solution)/shard_map/backward/pallas_call | solution.py:202
  129.7 2.0 %collective-permute-start.14 = (bf16[896,256]{1,0:T(8,128)(2,1)S(1)}, bf16[896,256]{1,0:T(8,128)(2,1)S(1)}, u32[]{:S(2)}, u32[]{:S(2)}) collective-permute-start(bf16[896,256]{1,0:T(8,128)(2,1)S(1)} %backward.1.grads.refs_2_.refs_3_), channel_id=1, source_target_pairs={{0,16},{16,0},{1,17},{17,1},{2,18},{18,2},{3,19},{19,3},{4,20},{20... | collective-permute-start | bytes 1376264 | tf_op jit(solution)/shard_map/ppermute | solution.py:440
  133.5 5.5 %means.2.refs_4_.refs_5_ = f32[896,256]{1,0:T(8,128)S(1)} custom-call(bf16[896,256]{1,0:T(8,128)(2,1)S(1)} %backward.1.grads.refs_2_.refs_3_, bf16[128,4096]{1,0:T(8,128)(2,1)S(1)} %maximum_select_fusion.x.refs_6_.refs_7_), custom_call_target="tpu_custom_call" | custom-call | flops 1879048192 | bytes 1048576 | tf_op jit(solution)/shard_map/means/pallas_call | solution.py:246
  139.2 1.9 %collective-permute-start.22 = (bf16[96,2048]{1,0:T(8,128)(2,1)S(1)}, bf16[96,2048]{1,0:T(8,128)(2,1)S(1)}, u32[]{:S(2)}, u32[]{:S(2)}) collective-permute-start(bf16[96,2048]{1,0:T(8,128)(2,1)S(1)} %get-tuple-element.59), channel_id=1, source_target_pairs={{0,16},{16,0},{1,17},{17,1},{2,18},{18,2},{3,19},{19,3},{4,20},{20... | collective-permute-start | bytes 1179656 | tf_op jit(solution)/shard_map/ppermute | solution.py:440
  141.2 2.0 %collective-permute-done.14.grads.refs_3_.refs_4_ = bf16[896,256]{1,0:T(8,128)(2,1)S(1)} collective-permute-done((bf16[896,256]{1,0:T(8,128)(2,1)S(1)}, bf16[896,256]{1,0:T(8,128)(2,1)S(1)}, u32[]{:S(2)}, u32[]{:S(2)}) %collective-permute-start.14) | collective-permute-done | bytes 458784 | tf_op jit(solution)/shard_map/ppermute | solution.py:440
  143.1 1.9 %collective-permute-start.23 = (bf16[128,2048]{1,0:T(8,128)(2,1)S(1)}, bf16[128,2048]{1,0:T(8,128)(2,1)S(1)}, u32[]{:S(2)}, u32[]{:S(2)}) collective-permute-start(bf16[128,2048]{1,0:T(8,128)(2,1)S(1)} %get-tuple-element.65), channel_id=1, source_target_pairs={{0,16},{16,0},{1,17},{17,1},{2,18},{18,2},{3,19},{19,3},{4,20},{20... | collective-permute-start | bytes 1572872 | tf_op jit(solution)/shard_map/ppermute | solution.py:440
  145.2 5.5 %means.3.refs_5_.refs_6_ = f32[896,256]{1,0:T(8,128)S(1)} custom-call(bf16[896,256]{1,0:T(8,128)(2,1)S(1)} %collective-permute-done.14.grads.refs_3_.refs_4_, bf16[128,4096]{1,0:T(8,128)(2,1)S(1)} %slice_dynamic-update-slice_fusion.1.x.refs_7_.refs_8_), custom_call_target="tpu_custom_call" | custom-call | flops 1879048192 | bytes 1048576 | tf_op jit(solution)/shard_map/means/pallas_call | solution.py:246
  152.3 2.5 %merge.6.refs_9_ = bf16[896,2048]{1,0:T(8,128)(2,1)} custom-call(s32[1]{0:T(128)} %bitcast.refs_0_, bf16[896,4096]{1,0:T(8,128)(2,1)} %bitcast.73, bf16[128,2048]{1,0:T(8,128)(2,1)S(1)} %collective-permute-done.3.refs_2_, bf16[896,256]{1,0:T(8,128)(2,1)S(1)} %backward.1.grads.refs_2_.refs_3_, ...), custom_call_target="tpu_custom_call" | custom-call | flops 134217728 | bytes 1572864 | tf_op jit(solution)/shard_map/merge/pallas_call | solution.py:305
  154.9 5.7 %merge.8.refs_9_ = bf16[896,2048]{1,0:T(8,128)(2,1)} custom-call(s32[1]{0:T(128)} %bitcast.refs_0_, bf16[896,4096]{1,0:T(8,128)(2,1)} %bitcast.68, bf16[512,2048]{1,0:T(8,128)(2,1)} %collective-permute-done.20.refs_2_, bf16[896,256]{1,0:T(8,128)(2,1)S(1)} %backward.1.grads.refs_2_.refs_3_, ...), custom_call_target="tpu_custom_call" | custom-call | flops 536870912 | bytes 6291456 | tf_op jit(solution)/shard_map/merge/pallas_call | solution.py:305
  160.5 7.9 %merge.7 = bf16[896,2048]{1,0:T(8,128)(2,1)} custom-call(s32[1]{0:T(128)} %bitcast.refs_0_, bf16[896,4096]{1,0:T(8,128)(2,1)} %bitcast.74, bf16[768,2048]{1,0:T(8,128)(2,1)} %collective-permute-done.19.refs_2_, bf16[896,256]{1,0:T(8,128)(2,1)S(1)} %backward.1.grads.refs_2_.refs_3_, ...), custom_call_target="tpu_custom_call", output_to_operand_aliasing={{}: (9, {})} | custom-call | flops 805306368 | bytes 9437184 | tf_op jit(solution)/shard_map/merge/pallas_call | solution.py:305
  168.4 3.2 %merge.9.refs_9_ = bf16[896,2048]{1,0:T(8,128)(2,1)} custom-call(s32[1]{0:T(128)} %bitcast.refs_0_, bf16[896,4096]{1,0:T(8,128)(2,1)} %bitcast.69, bf16[96,2048]{1,0:T(8,128)(2,1)S(1)} %collective-permute-done.21.refs_2_, bf16[896,256]{1,0:T(8,128)(2,1)S(1)} %backward.1.grads.refs_2_.refs_3_, ...), custom_call_target="tpu_custom_call", output_to_operand_aliasing={{}: (9, {})} | custom-call | flops 100663296 | bytes 1179648 | tf_op jit(solution)/shard_map/merge/pallas_call | solution.py:305
  171.6 3.1 %merge.10.refs_9_ = bf16[896,2048]{1,0:T(8,128)(2,1)} custom-call(s32[1]{0:T(128)} %bitcast.refs_0_, bf16[896,4096]{1,0:T(8,128)(2,1)} %bitcast.70, bf16[96,2048]{1,0:T(8,128)(2,1)S(1)} %collective-permute-done.22.refs_2_, bf16[896,256]{1,0:T(8,128)(2,1)S(1)} %backward.1.grads.refs_2_.refs_3_, ...), custom_call_target="tpu_custom_call", output_to_operand_aliasing={{}: (9, {})} | custom-call | flops 100663296 | bytes 1179648 | tf_op jit(solution)/shard_map/merge/pallas_call | solution.py:305
  174.7 2.5 %merge.11.refs_2_ = bf16[896,2048]{1,0:T(8,128)(2,1)} custom-call(s32[1]{0:T(128)} %bitcast.refs_0_, bf16[896,4096]{1,0:T(8,128)(2,1)} %bitcast.71, bf16[128,2048]{1,0:T(8,128)(2,1)S(1)} %collective-permute-done.23.refs_2_, bf16[896,256]{1,0:T(8,128)(2,1)S(1)} %backward.1.grads.refs_2_.refs_3_, ...), custom_call_target="tpu_custom_call", output_to_operand_aliasing={{}: (9, {})} | custom-call | flops 134217728 | bytes 1572864 | tf_op jit(solution)/shard_map/merge/pallas_call | solution.py:305
  (84 shorter events, 24.6 us)
Async XLA Ops:
  0.6 5.8 %collective-permute-start = (bf16[8,4096]{1,0:T(8,128)(2,1)}, bf16[8,4096]{1,0:T(8,128)(2,1)S(1)}, u32[]{:S(2)}, u32[]{:S(2)}) collective-permute-start(bf16[8,4096]{1,0:T(8,128)(2,1)} %bitcast.77), channel_id=1, source_target_pairs={{0,16},{16,0},{1,17},{17,1},{2,18},{18,2},{3,19},{19,3},{4,20},{20... | collective-permute-start | bytes 196616 | tf_op jit(solution)/shard_map/ppermute | solution.py:440
  4.7 10.6 %copy-start.5 = (bf16[1,8,4096]{2,1,0:T(8,128)(2,1)S(1)}, bf16[1,8,4096]{2,1,0:T(8,128)(2,1)}, u32[]{:S(2)}) copy-start(bf16[1,8,4096]{2,1,0:T(8,128)(2,1)} %param.6) | copy-start | bytes 196612
  4.7 24.7 %collective-permute-start.3 = (bf16[128,2048]{1,0:T(8,128)(2,1)S(1)}, bf16[128,2048]{1,0:T(8,128)(2,1)S(1)}, u32[]{:S(2)}, u32[]{:S(2)}) collective-permute-start(bf16[128,2048]{1,0:T(8,128)(2,1)S(1)} %dynamic-slice_bitcast_fusion.2), channel_id=1, source_target_pairs={{0,16},{16,0},{1,17},{17,1},{2,18},{18,2},{3,19},{19,3},{4,20},{20... | collective-permute-start | bytes 1572872 | tf_op jit(solution)/shard_map/ppermute | solution.py:440
  6.4 9.2 %collective-permute-start.15 = (bf16[8,4096]{1,0:T(8,128)(2,1)S(1)}, bf16[8,4096]{1,0:T(8,128)(2,1)S(1)}, u32[]{:S(2)}, u32[]{:S(2)}) collective-permute-start(bf16[8,4096]{1,0:T(8,128)(2,1)S(1)} %collective-permute-done), channel_id=1, source_target_pairs={{0,8},{1,9},{2,10},{3,11},{4,12},{5,13},{6,14},{7,15},{8,0},{9,1},... | collective-permute-start | bytes 196616 | tf_op jit(solution)/shard_map/ppermute | solution.py:48
  13.1 147.4 %collective-permute-start.19 = (bf16[768,2048]{1,0:T(8,128)(2,1)}, bf16[768,2048]{1,0:T(8,128)(2,1)}, u32[]{:S(2)}, u32[]{:S(2)}) collective-permute-start(bf16[768,2048]{1,0:T(8,128)(2,1)} %dynamic-slice_bitcast_fusion), channel_id=1, source_target_pairs={{0,16},{16,0},{1,17},{17,1},{2,18},{18,2},{3,19},{19,3},{4,20},{20... | collective-permute-start | bytes 9437192 | tf_op jit(solution)/shard_map/ppermute | solution.py:440
  15.3 7.6 %collective-permute-start.1 = (bf16[8,4096]{1,0:T(8,128)(2,1)S(1)}, bf16[8,4096]{1,0:T(8,128)(2,1)S(1)}, u32[]{:S(2)}, u32[]{:S(2)}) collective-permute-start(bf16[8,4096]{1,0:T(8,128)(2,1)S(1)} %bitcast.78), channel_id=1, source_target_pairs={{0,8},{1,3},{2,10},{3,1},{4,12},{5,7},{6,14},{7,5},{8,0},{9,11},{1... | collective-permute-start | bytes 196616 | tf_op jit(solution)/shard_map/ppermute | solution.py:48
  15.7 7.3 %collective-permute-start.16 = (bf16[16,4096]{1,0:T(8,128)(2,1)S(1)}, bf16[16,4096]{1,0:T(8,128)(2,1)S(1)}, u32[]{:S(2)}, u32[]{:S(2)}) collective-permute-start(bf16[16,4096]{1,0:T(8,128)(2,1)S(1)} %maximum_select_fusion.10), channel_id=1, source_target_pairs={{0,4},{1,5},{2,6},{3,7},{4,0},{5,1},{6,2},{7,3},{8,12},{9,13},{10,... | collective-permute-start | bytes 393224 | tf_op jit(solution)/shard_map/ppermute | solution.py:48
  22.9 6.4 %collective-permute-start.2 = (bf16[16,4096]{1,0:T(8,128)(2,1)S(1)}, bf16[16,4096]{1,0:T(8,128)(2,1)S(1)}, u32[]{:S(2)}, u32[]{:S(2)}) collective-permute-start(bf16[16,4096]{1,0:T(8,128)(2,1)S(1)} %maximum_select_fusion.9), channel_id=1, source_target_pairs={{0,4},{1,9},{2,6},{3,11},{4,0},{5,13},{6,2},{7,15},{8,12},{9,1},{1... | collective-permute-start | bytes 393224 | tf_op jit(solution)/shard_map/ppermute | solution.py:48
  23.1 8.0 %collective-permute-start.17 = (bf16[32,4096]{1,0:T(8,128)(2,1)S(1)}, bf16[32,4096]{1,0:T(8,128)(2,1)S(1)}, u32[]{:S(2)}, u32[]{:S(2)}) collective-permute-start(bf16[32,4096]{1,0:T(8,128)(2,1)S(1)} %maximum_select_fusion.8), channel_id=1, source_target_pairs={{0,2},{1,3},{2,0},{3,1},{4,6},{5,7},{6,4},{7,5},{8,10},{9,11},{10,... | collective-permute-start | bytes 786440 | tf_op jit(solution)/shard_map/ppermute | solution.py:48
  29.4 9.8 %copy-start.6 = (s32[1,2,896]{2,1,0:T(2,128)S(1)}, s32[1,2,896]{2,1,0:T(2,128)}, u32[]{:S(2)}) copy-start(s32[1,2,896]{2,1,0:T(2,128)} %param.11) | copy-start | bytes 21508
  29.4 6.4 %collective-permute-start.4 = (bf16[32,4096]{1,0:T(8,128)(2,1)S(1)}, bf16[32,4096]{1,0:T(8,128)(2,1)S(1)}, u32[]{:S(2)}, u32[]{:S(2)}) collective-permute-start(bf16[32,4096]{1,0:T(8,128)(2,1)S(1)} %maximum_select_fusion.6), channel_id=1, source_target_pairs={{0,2},{1,5},{2,0},{3,7},{4,6},{5,1},{6,4},{7,3},{8,10},{9,13},{10,... | collective-permute-start | bytes 786440 | tf_op jit(solution)/shard_map/ppermute | solution.py:48
  31.1 8.3 %collective-permute-start.18 = (bf16[64,4096]{1,0:T(8,128)(2,1)S(1)}, bf16[64,4096]{1,0:T(8,128)(2,1)S(1)}, u32[]{:S(2)}, u32[]{:S(2)}) collective-permute-start(bf16[64,4096]{1,0:T(8,128)(2,1)S(1)} %maximum_select_fusion.5), channel_id=1, source_target_pairs={{0,1},{1,0},{2,3},{3,2},{4,5},{5,4},{6,7},{7,6},{8,9},{9,8},{10,11... | collective-permute-start | bytes 1572872 | tf_op jit(solution)/shard_map/ppermute | solution.py:462
  36.0 3.7 %collective-permute-start.5 = (bf16[64,4096]{1,0:T(8,128)(2,1)S(1)}, bf16[64,4096]{1,0:T(8,128)(2,1)}, u32[]{:S(2)}, u32[]{:S(2)}) collective-permute-start(bf16[64,4096]{1,0:T(8,128)(2,1)S(1)} %maximum_select_fusion.3), channel_id=1, source_target_pairs={{0,1},{1,0},{2,3},{3,2},{4,5},{5,4},{6,7},{7,6},{8,9},{9,8},{10,11... | collective-permute-start | bytes 1572872 | tf_op jit(solution)/shard_map/ppermute | solution.py:462
  39.2 2.0 %copy-start.4 = (s32[1,2,4096]{2,1,0:T(2,128)S(1)}, s32[1,2,4096]{2,1,0:T(2,128)}, u32[]{:S(2)}) copy-start(s32[1,2,4096]{2,1,0:T(2,128)} %param.10) | copy-start | bytes 98308
  39.2 105.8 %collective-permute-start.20 = (bf16[512,2048]{1,0:T(8,128)(2,1)}, bf16[512,2048]{1,0:T(8,128)(2,1)}, u32[]{:S(2)}, u32[]{:S(2)}) collective-permute-start(bf16[512,2048]{1,0:T(8,128)(2,1)} %dynamic-slice_bitcast_fusion.1), channel_id=1, source_target_pairs={{0,16},{16,0},{1,17},{17,1},{2,18},{18,2},{3,19},{19,3},{4,20},{20... | collective-permute-start | bytes 6291464 | tf_op jit(solution)/shard_map/ppermute | solution.py:440
  57.3 0.8 copy-start
  58.1 12.5 %copy-start.2 = (f32[128,896]{1,0:T(8,128)}, f32[128,896]{1,0:T(8,128)S(1)}, u32[]{:S(2)}) copy-start(f32[128,896]{1,0:T(8,128)S(1)} %get-tuple-element.45.sd) | copy-start | bytes 1376260
  58.1 2.8 %collective-permute-start.6 = (bf16[128,4096]{1,0:T(8,128)(2,1)S(1)}, bf16[128,4096]{1,0:T(8,128)(2,1)S(1)}, u32[]{:S(2)}, u32[]{:S(2)}) collective-permute-start(bf16[128,4096]{1,0:T(8,128)(2,1)S(1)} %get-tuple-element.41), channel_id=1, source_target_pairs={{0,1},{1,0},{2,3},{3,2},{4,5},{5,4},{6,7},{7,6},{8,9},{9,8},{10,11... | collective-permute-start | bytes 3145736 | tf_op jit(solution)/shard_map/ppermute | solution.py:495
  61.1 9.2 %collective-permute-start.7 = (bf16[64,4096]{1,0:T(8,128)(2,1)S(1)}, bf16[64,4096]{1,0:T(8,128)(2,1)S(1)}, u32[]{:S(2)}, u32[]{:S(2)}) collective-permute-start(bf16[64,4096]{1,0:T(8,128)(2,1)S(1)} %constant_dynamic-slice_fusion.2), channel_id=1, source_target_pairs={{0,2},{1,5},{2,0},{3,7},{4,6},{5,1},{6,4},{7,3},{8,10},{9,13},{10,... | collective-permute-start | bytes 1572872 | tf_op jit(solution)/shard_map/ppermute | solution.py:48
  70.6 9.1 %collective-permute-start.8 = (bf16[32,4096]{1,0:T(8,128)(2,1)S(1)}, bf16[32,4096]{1,0:T(8,128)(2,1)S(1)}, u32[]{:S(2)}, u32[]{:S(2)}) collective-permute-start(bf16[32,4096]{1,0:T(8,128)(2,1)S(1)} %constant_dynamic-slice_fusion.1), channel_id=1, source_target_pairs={{0,4},{1,9},{2,6},{3,11},{4,0},{5,13},{6,2},{7,15},{8,12},{9,1},{1... | collective-permute-start | bytes 786440 | tf_op jit(solution)/shard_map/ppermute | solution.py:48
  79.7 6.3 %collective-permute-start.9 = (bf16[16,4096]{1,0:T(8,128)(2,1)S(1)}, bf16[16,4096]{1,0:T(8,128)(2,1)S(1)}, u32[]{:S(2)}, u32[]{:S(2)}) collective-permute-start(bf16[16,4096]{1,0:T(8,128)(2,1)S(1)} %constant_dynamic-slice_fusion), channel_id=1, source_target_pairs={{0,8},{1,3},{2,10},{3,1},{4,12},{5,7},{6,14},{7,5},{8,0},{9,11},{1... | collective-permute-start | bytes 393224 | tf_op jit(solution)/shard_map/ppermute | solution.py:48
  86.1 10.5 %collective-permute-start.10 = (bf16[16,4096]{1,0:T(8,128)(2,1)S(1)}, bf16[16,4096]{1,0:T(8,128)(2,1)S(1)}, u32[]{:S(2)}, u32[]{:S(2)}) collective-permute-start(bf16[16,4096]{1,0:T(8,128)(2,1)S(1)} %add_convert_fusion.3), channel_id=1, source_target_pairs={{0,8},{1,3},{2,10},{3,1},{4,12},{5,7},{6,14},{7,5},{8,0},{9,11},{1... | collective-permute-start | bytes 393224 | tf_op jit(solution)/shard_map/ppermute | solution.py:48
  96.6 7.9 %collective-permute-start.11 = (bf16[32,4096]{1,0:T(8,128)(2,1)S(1)}, bf16[32,4096]{1,0:T(8,128)(2,1)S(1)}, u32[]{:S(2)}, u32[]{:S(2)}) collective-permute-start(bf16[32,4096]{1,0:T(8,128)(2,1)S(1)} %maximum_select_fusion.7), channel_id=1, source_target_pairs={{0,4},{1,9},{2,6},{3,11},{4,0},{5,13},{6,2},{7,15},{8,12},{9,1},{1... | collective-permute-start | bytes 786440 | tf_op jit(solution)/shard_map/ppermute | solution.py:48
  105.4 9.5 %collective-permute-start.12 = (bf16[64,4096]{1,0:T(8,128)(2,1)}, bf16[64,4096]{1,0:T(8,128)(2,1)}, u32[]{:S(2)}, u32[]{:S(2)}) collective-permute-start(bf16[64,4096]{1,0:T(8,128)(2,1)} %maximum_select_fusion.4), channel_id=1, source_target_pairs={{0,2},{1,5},{2,0},{3,7},{4,6},{5,1},{6,4},{7,3},{8,10},{9,13},{10,... | collective-permute-start | bytes 1572872 | tf_op jit(solution)/shard_map/ppermute | solution.py:48
  106.9 14.5 %copy-start.1 = (f32[128,896]{1,0:T(8,128)S(1)}, f32[128,896]{1,0:T(8,128)}, u32[]{:S(2)}) copy-start(f32[128,896]{1,0:T(8,128)} %copy-done) | copy-start | bytes 1376260
  106.9 14.5 %copy-start.3 = (f32[128,896]{1,0:T(8,128)S(1)}, f32[128,896]{1,0:T(8,128)}, u32[]{:S(2)}) copy-start(f32[128,896]{1,0:T(8,128)} %copy-done.2) | copy-start | bytes 1376260
  116.7 4.7 %collective-permute-start.13 = (bf16[128,4096]{1,0:T(8,128)(2,1)S(1)}, bf16[128,4096]{1,0:T(8,128)(2,1)S(1)}, u32[]{:S(2)}, u32[]{:S(2)}) collective-permute-start(bf16[128,4096]{1,0:T(8,128)(2,1)S(1)} %maximum_select_fusion.1.mine), channel_id=1, source_target_pairs={{0,1},{1,0},{2,3},{3,2},{4,5},{5,4},{6,7},{7,6},{8,9},{9,8},{10,11... | collective-permute-start | bytes 3145736 | tf_op jit(solution)/shard_map/ppermute | solution.py:498
  129.7 13.5 %collective-permute-start.14 = (bf16[896,256]{1,0:T(8,128)(2,1)S(1)}, bf16[896,256]{1,0:T(8,128)(2,1)S(1)}, u32[]{:S(2)}, u32[]{:S(2)}) collective-permute-start(bf16[896,256]{1,0:T(8,128)(2,1)S(1)} %backward.1.grads.refs_2_.refs_3_), channel_id=1, source_target_pairs={{0,16},{16,0},{1,17},{17,1},{2,18},{18,2},{3,19},{19,3},{4,20},{20... | collective-permute-start | bytes 1376264 | tf_op jit(solution)/shard_map/ppermute | solution.py:440
  139.1 29.4 %collective-permute-start.21 = (bf16[96,2048]{1,0:T(8,128)(2,1)S(1)}, bf16[96,2048]{1,0:T(8,128)(2,1)S(1)}, u32[]{:S(2)}, u32[]{:S(2)}) collective-permute-start(bf16[96,2048]{1,0:T(8,128)(2,1)S(1)} %get-tuple-element.53), channel_id=1, source_target_pairs={{0,16},{16,0},{1,17},{17,1},{2,18},{18,2},{3,19},{19,3},{4,20},{20... | collective-permute-start | bytes 1179656 | tf_op jit(solution)/shard_map/ppermute | solution.py:440
  139.2 32.4 %collective-permute-start.22 = (bf16[96,2048]{1,0:T(8,128)(2,1)S(1)}, bf16[96,2048]{1,0:T(8,128)(2,1)S(1)}, u32[]{:S(2)}, u32[]{:S(2)}) collective-permute-start(bf16[96,2048]{1,0:T(8,128)(2,1)S(1)} %get-tuple-element.59), channel_id=1, source_target_pairs={{0,16},{16,0},{1,17},{17,1},{2,18},{18,2},{3,19},{19,3},{4,20},{20... | collective-permute-start | bytes 1179656 | tf_op jit(solution)/shard_map/ppermute | solution.py:440
  143.1 31.6 %collective-permute-start.23 = (bf16[128,2048]{1,0:T(8,128)(2,1)S(1)}, bf16[128,2048]{1,0:T(8,128)(2,1)S(1)}, u32[]{:S(2)}, u32[]{:S(2)}) collective-permute-start(bf16[128,2048]{1,0:T(8,128)(2,1)S(1)} %get-tuple-element.65), channel_id=1, source_target_pairs={{0,16},{16,0},{1,17},{17,1},{2,18},{18,2},{3,19},{19,3},{4,20},{20... | collective-permute-start | bytes 1572872 | tf_op jit(solution)/shard_map/ppermute | solution.py:440
  145.0 32.2 %collective-permute-start.24 = (bf16[64,2048]{1,0:T(8,128)(2,1)S(1)}, bf16[64,2048]{1,0:T(8,128)(2,1)S(1)}, u32[]{:S(2)}, u32[]{:S(2)}) collective-permute-start(bf16[64,2048]{1,0:T(8,128)(2,1)S(1)} %pad_maximum_fusion), channel_id=1, source_target_pairs={{0,16},{16,0},{1,17},{17,1},{2,18},{18,2},{3,19},{19,3},{4,20},{20... | collective-permute-start | bytes 786440 | tf_op jit(solution)/shard_map/ppermute | solution.py:440

commit v4 on v3

--- a/solution.py
+++ b/solution.py
@@ -30,8 +30,8 @@
     return 128 if units % 128 == 0 else units
 
 
-def step_of(rows):
-    return max((b for b in range(16, 129, 16) if rows % b == 0), default=rows)
+def step_of(rows, most=128):
+    return max((b for b in range(16, most + 1, 16) if rows % b == 0), default=rows)
 
 
 def tile_of(width):
@@ -98,22 +98,19 @@
     def _():
         copy.start()
 
-    a = dot(x[...], gate[...], NT) * factor
-    b = dot(x[...], upper[...], NT) * factor
+    ab = dot(jnp.concatenate([gate[...], upper[...]]), x[...], NT) * factor
     tile = tile_of(width)
-    da = jnp.zeros((tokens, units), F32)
-    db = jnp.zeros((tokens, units), F32)
+    dab = jnp.zeros((2 * units, tokens), F32)
     for at in range(0, width, tile):
-        part = x[:, at:at + tile]
         signs = []
         for k in (0, 1):
             code = jnp.bitwise_and(col[:, k:k + 1], row[k:k + 1, at:at + tile])
             odd = jnp.bitwise_and(lax.population_count(code), 1)
             signs.append((1 - 2 * odd).astype(F32).astype(BF16))
-        da = da + dot(part, signs[0], NT)
-        db = db + dot(part, signs[1], NT)
-    da = da * factor
-    db = db * factor
+        dab = dab + dot(jnp.concatenate(signs), x[:, at:at + tile], NT)
+    dab = dab * factor
+    a, b = ab[:units], ab[units:]
+    da, db = dab[:units], dab[units:]
     sigma = jax.nn.sigmoid(a)
     s = a * sigma
     slope = sigma * (1.0 + a * (1.0 - sigma))
@@ -125,18 +122,16 @@
     hidden = s * b
     d_hidden = slope * da * b + s * db
     even = core[0] == 0
-    if steps == 1:
-        place = slice(None)
-    else:
-        place = pl.ds(pl.multiple_of(step * units, units), units)
-    hid[:tokens, place] = jnp.where(even, d_hidden, hidden).astype(BF16)
-    hid[tokens:, place] = jnp.where(even, hidden, d_hidden).astype(BF16)
+    place = pl.ds(pl.multiple_of(step * units, 16), units)
+    hid[place, :tokens] = jnp.where(even, d_hidden, hidden)
+    hid[place, tokens:] = jnp.where(even, hidden, d_hidden)
 
     @pl.when(step == steps - 1)
     def _():
+        left = hid[...].T.astype(BF16)
         copy.wait()
         for at in range(0, width, tile):
-            both = dot(hid[...], whole[:, at:at + tile], NN)
+            both = dot(left, whole[:, at:at + tile], NN)
             send[:, at:at + tile] = both[:tokens].astype(BF16)
             keep[:, at:at + tile] = both[tokens:].astype(BF16)
 
@@ -144,12 +139,12 @@
 def forward(core, x, gate, upper, down, row, col):
     tokens, width = x.shape
     units = gate.shape[0]
-    block = rows_of(units)
+    block = step_of(units, 224)
     steps = units // block
     by_unit = pl.BlockSpec((block, width), lambda i, c: (i, 0))
-    by_lane = pl.BlockSpec((tokens, block), lambda i, c: (0, i))
+    by_lane = pl.BlockSpec((block, tokens), lambda i, c: (i, 0))
     fixed = pl.BlockSpec((tokens, width), lambda i, c: (0, 0))
-    wide = jax.ShapeDtypeStruct((tokens, units), F32)
+    wide = jax.ShapeDtypeStruct((units, tokens), F32)
     out = jax.ShapeDtypeStruct((tokens, width), BF16)
     return pl.pallas_call(
         functools.partial(forward_kernel, width ** (-0.5), steps),
@@ -167,7 +162,7 @@
             ],
             out_specs=[by_lane] * 4 + [fixed] * 2,
             scratch_shapes=[
-                pltpu.VMEM((2 * tokens, units), BF16),
+                pltpu.VMEM((units, 2 * tokens), F32),
                 pltpu.VMEM((units, width), BF16),
                 pltpu.SemaphoreType.DMA,
             ],
@@ -184,20 +179,20 @@
 
 def backward_kernel(core, mine, other, down, p, q, act, sd, grads):
     tokens = mine.shape[0]
-    g_mine = dot(mine[...], down[...], NT)
-    g_other = dot(other[...], down[...], NT)
+    g = dot(down[...], jnp.concatenate([mine[...], other[...]]), NT)
+    g_mine, g_other = g[:, :tokens], g[:, tokens:]
     even = core[0] == 0
     gh = jnp.where(even, g_mine, g_other)
     gdh = jnp.where(even, g_other, g_mine)
-    grads[:, :tokens] = (gdh * p[...] + gh * q[...]).T.astype(BF16)
-    grads[:, tokens:] = (gdh * act[...] + gh * sd[...]).T.astype(BF16)
+    grads[:, :tokens] = (gdh * p[...] + gh * q[...]).astype(BF16)
+    grads[:, tokens:] = (gdh * act[...] + gh * sd[...]).astype(BF16)
 
 
 def backward(core, mine, other, down, kept):
     tokens, width = mine.shape
     units = down.shape[0]
-    block = rows_of(units)
-    by_lane = pl.BlockSpec((tokens, block), lambda i, c: (0, i))
+    block = step_of(units, 448)
+    by_lane = pl.BlockSpec((block, tokens), lambda i, c: (i, 0))
     fixed = pl.BlockSpec((tokens, width), lambda i, c: (0, 0))
     return pl.pallas_call(
         backward_kernel,
@@ -242,7 +237,7 @@
 def means(grads, x):
     tokens, width = x.shape
     units = grads.shape[0]
-    block = rows_of(units)
+    block = step_of(units, 448)
     return pl.pallas_call(
         means_kernel,
         out_shape=jax.ShapeDtypeStruct((units, 2 * LANES), F32),
@@ -411,7 +406,7 @@
     count = units // block
     if count < 4:
         return [], [(0, 0, units)], [(1, 0, units)], [], None
-    head = block * (count // 2 + 1)
+    head = block * (count // 2 + 1) - block // 4
     tail = units - block // 2
     count = -(-(tail - head) // block)
     marks = [head + (tail - head) // 32 * i // count * 32 for i in range(count)] + [tail]

time: 179 us -> 176 us (0.983)
  Pallas kernels: 62.5 us -> 53 us
  waiting for transfers between devices: 68.1 us -> 74.5 us
    ppermute x9, waiting for transfers between devices: 3.59 us -> 10.1 us  [across(): lax.ppermute(value, 'ckpt', [(i, (i + shift) % n_ckpt) for i in range(n_c...]
    pallas_call x1, Pallas kernels: 8.17 us -> 4.38 us  [backward(): pl.pallas_call(backward_kernel, out_shape=jax.ShapeDtypeStruct((units, 2...]
    pallas_call x1, Pallas kernels: 16.1 us -> 13.5 us  [forward(): pl.pallas_call(functools.partial(forward_kernel, width ** (-0.5), steps),...]
    pallas_call x2, Pallas kernels: 11 us -> 8.62 us  [means(): pl.pallas_call(means_kernel, out_shape=jax.ShapeDtypeStruct((units, 2 * L...]
  transfers between devices with their start and end apart: 25 -> 25, of which waited for: 12 -> 14; matrix products, arithmetic and copies ran while one was open for 12% -> 13% of each run, Pallas kernels for 35% -> 30%
where the time goes in v4:
time: 176 us; the launch traced here: 175 us
  waiting for transfers between devices  74.5 us (42%)
  Pallas kernels  53 us (30%)
  starting transfers between devices  23.5 us (13%)
  local copies, waits for them, and re-layouts  17.6 us (10%)
  other arithmetic  5.19 us (3%)
    ppermute x12, waiting for transfers between devices, swap(): return lax.ppermute(value, axis, pairs)  62.2 us
    pallas_call x6, Pallas kernels, merge(): pl.pallas_call(functools.partial(merge_kernel, members), out_shape=jax.Sh...  23.9 us
    pallas_call x1, Pallas kernels, forward(): pl.pallas_call(functools.partial(forward_kernel, width ** (-0.5), steps),...  13.5 us
    ppermute x9, starting transfers between devices, across(): lax.ppermute(value, 'ckpt', [(i, (i + shift) % n_ckpt) for i in range(n_c...  11.4 us
    ppermute x12, starting transfers between devices, swap(): return lax.ppermute(value, axis, pairs)  11.4 us
    ppermute x9, waiting for transfers between devices, across(): lax.ppermute(value, 'ckpt', [(i, (i + shift) % n_ckpt) for i in range(n_c...  10.1 us
    pallas_call x2, Pallas kernels, means(): pl.pallas_call(means_kernel, out_shape=jax.ShapeDtypeStruct((units, 2 * L...  8.62 us
    dynamic_slice x3, local copies, waits for them, and re-layouts, cut(): lax.dynamic_slice(weights[which], (start, left), (rows, part))  8.08 us
  transfers between devices with their start and end apart: 25, of which 14 were waited for; matrix products, arithmetic and copies ran while one was open for 13% of the time, Pallas kernels for 30%

profile of v4, /device:TPU:0, one launch (start us, length us, event | category | flops | bytes accessed | tf_op | source)
XLA Modules:
  0.0 174.8 jit_solution(6608235205238229860)
XLA Ops:
  0.6 3.0 %collective-permute-start = (bf16[8,4096]{1,0:T(8,128)(2,1)}, bf16[8,4096]{1,0:T(8,128)(2,1)S(1)}, u32[]{:S(2)}, u32[]{:S(2)}) collective-permute-start(bf16[8,4096]{1,0:T(8,128)(2,1)} %bitcast.81), channel_id=1, source_target_pairs={{0,16},{16,0},{1,17},{17,1},{2,18},{18,2},{3,19},{19,3},{4,20},{20... | collective-permute-start | bytes 196616 | tf_op jit(solution)/shard_map/ppermute | solution.py:435
  6.4 2.8 %collective-permute-start.15 = (bf16[8,4096]{1,0:T(8,128)(2,1)S(1)}, bf16[8,4096]{1,0:T(8,128)(2,1)S(1)}, u32[]{:S(2)}, u32[]{:S(2)}) collective-permute-start(bf16[8,4096]{1,0:T(8,128)(2,1)S(1)} %collective-permute-done), channel_id=1, source_target_pairs={{0,8},{1,9},{2,10},{3,11},{4,12},{5,13},{6,14},{7,15},{8,0},{9,1},... | collective-permute-start | bytes 196616 | tf_op jit(solution)/shard_map/ppermute | solution.py:48
  9.2 4.0 %dynamic-slice_bitcast_fusion = bf16[768,2048]{1,0:T(8,128)(2,1)} fusion(bf16[1,896,4096]{2,1,0:T(8,128)(2,1)} %param.7, s32[]{:T(128)S(6)} %select_n.154), kind=kLoop, calls=%fused_computation | loop fusion | bytes 6291460 | tf_op jit(solution)/shard_map/dynamic_slice | solution.py:441
  13.2 2.1 %collective-permute-start.19 = (bf16[768,2048]{1,0:T(8,128)(2,1)}, bf16[768,2048]{1,0:T(8,128)(2,1)}, u32[]{:S(2)}, u32[]{:S(2)}) collective-permute-start(bf16[768,2048]{1,0:T(8,128)(2,1)} %dynamic-slice_bitcast_fusion), channel_id=1, source_target_pairs={{0,16},{16,0},{1,17},{17,1},{2,18},{18,2},{3,19},{19,3},{4,20},{20... | collective-permute-start | bytes 9437192 | tf_op jit(solution)/shard_map/ppermute | solution.py:435
  17.3 5.6 %collective-permute-done.1 = bf16[8,4096]{1,0:T(8,128)(2,1)S(1)} collective-permute-done((bf16[8,4096]{1,0:T(8,128)(2,1)S(1)}, bf16[8,4096]{1,0:T(8,128)(2,1)S(1)}, u32[]{:S(2)}, u32[]{:S(2)}) %collective-permute-start.1) | collective-permute-done | bytes 65568 | tf_op jit(solution)/shard_map/ppermute | solution.py:48
  24.7 4.7 %collective-permute-done.2 = bf16[16,4096]{1,0:T(8,128)(2,1)S(1)} collective-permute-done((bf16[16,4096]{1,0:T(8,128)(2,1)S(1)}, bf16[16,4096]{1,0:T(8,128)(2,1)S(1)}, u32[]{:S(2)}, u32[]{:S(2)}) %collective-permute-start.2) | collective-permute-done | bytes 131104 | tf_op jit(solution)/shard_map/ppermute | solution.py:48
  31.2 4.7 %collective-permute-done.4 = bf16[32,4096]{1,0:T(8,128)(2,1)S(1)} collective-permute-done((bf16[32,4096]{1,0:T(8,128)(2,1)S(1)}, bf16[32,4096]{1,0:T(8,128)(2,1)S(1)}, u32[]{:S(2)}, u32[]{:S(2)}) %collective-permute-start.4) | collective-permute-done | bytes 262176 | tf_op jit(solution)/shard_map/ppermute | solution.py:48
  36.1 3.1 %dynamic-slice_bitcast_fusion.1 = bf16[480,2048]{1,0:T(8,128)(2,1)} fusion(bf16[1,896,4096]{2,1,0:T(8,128)(2,1)} %param.8, s32[]{:T(128)S(6)} %select_n.154), kind=kLoop, calls=%fused_computation.2 | loop fusion | bytes 3932164 | tf_op jit(solution)/shard_map/dynamic_slice | solution.py:441
  41.1 13.5 %forward.1 = (f32[896,128]{1,0:T(8,128)S(1)}, f32[896,128]{1,0:T(8,128)S(1)}, f32[896,128]{1,0:T(8,128)S(1)}, f32[896,128]{1,0:T(8,128)S(1)}, bf16[128,4096]{1,0...) custom-call(s32[1]{0:T(128)} %bitcast.2.core, bf16[128,4096]{1,0:T(8,128)(2,1)S(1)} %maximum_select_fusion.x.refs_6_.refs_7_, ...), custom_call_target="tpu_custom_call" | custom-call | flops 5637144576 | bytes 22020096 | tf_op jit(solution)/shard_map/forward/pallas_call | solution.py:149
  55.9 2.2 %collective-permute-done.6 = bf16[128,4096]{1,0:T(8,128)(2,1)S(1)} collective-permute-done((bf16[128,4096]{1,0:T(8,128)(2,1)S(1)}, bf16[128,4096]{1,0:T(8,128)(2,1)S(1)}, u32[]{:S(2)}, u32[]{:S(2)}) %collective-permute-start.6) | collective-permute-done | bytes 1048608 | tf_op jit(solution)/shard_map/ppermute | solution.py:490
  60.0 7.7 %collective-permute-done.7 = bf16[64,4096]{1,0:T(8,128)(2,1)S(1)} collective-permute-done((bf16[64,4096]{1,0:T(8,128)(2,1)S(1)}, bf16[64,4096]{1,0:T(8,128)(2,1)S(1)}, u32[]{:S(2)}, u32[]{:S(2)}) %collective-permute-start.7) | collective-permute-done | bytes 524320 | tf_op jit(solution)/shard_map/ppermute | solution.py:48
  68.0 9.0 %collective-permute-done.8 = bf16[32,4096]{1,0:T(8,128)(2,1)S(1)} collective-permute-done((bf16[32,4096]{1,0:T(8,128)(2,1)S(1)}, bf16[32,4096]{1,0:T(8,128)(2,1)S(1)}, u32[]{:S(2)}, u32[]{:S(2)}) %collective-permute-start.8) | collective-permute-done | bytes 262176 | tf_op jit(solution)/shard_map/ppermute | solution.py:48
  77.1 6.3 %collective-permute-done.9 = bf16[16,4096]{1,0:T(8,128)(2,1)S(1)} collective-permute-done((bf16[16,4096]{1,0:T(8,128)(2,1)S(1)}, bf16[16,4096]{1,0:T(8,128)(2,1)S(1)}, u32[]{:S(2)}, u32[]{:S(2)}) %collective-permute-start.9) | collective-permute-done | bytes 131104 | tf_op jit(solution)/shard_map/ppermute | solution.py:48
  83.5 10.4 %collective-permute-done.10 = bf16[16,4096]{1,0:T(8,128)(2,1)S(1)} collective-permute-done((bf16[16,4096]{1,0:T(8,128)(2,1)S(1)}, bf16[16,4096]{1,0:T(8,128)(2,1)S(1)}, u32[]{:S(2)}, u32[]{:S(2)}) %collective-permute-start.10) | collective-permute-done | bytes 131104 | tf_op jit(solution)/shard_map/ppermute | solution.py:48
  94.0 7.8 %collective-permute-done.11 = bf16[32,4096]{1,0:T(8,128)(2,1)S(1)} collective-permute-done((bf16[32,4096]{1,0:T(8,128)(2,1)S(1)}, bf16[32,4096]{1,0:T(8,128)(2,1)S(1)}, u32[]{:S(2)}, u32[]{:S(2)}) %collective-permute-start.11) | collective-permute-done | bytes 262176 | tf_op jit(solution)/shard_map/ppermute | solution.py:48
  106.1 6.1 %collective-permute-done.12 = bf16[64,4096]{1,0:T(8,128)(2,1)} collective-permute-done((bf16[64,4096]{1,0:T(8,128)(2,1)}, bf16[64,4096]{1,0:T(8,128)(2,1)}, u32[]{:S(2)}, u32[]{:S(2)}) %collective-permute-start.12) | collective-permute-done | bytes 524320 | tf_op jit(solution)/shard_map/ppermute | solution.py:48
  112.2 1.8 %maximum_select_fusion.1.mine = bf16[128,4096]{1,0:T(8,128)(2,1)S(1)} fusion(bf16[64,4096]{1,0:T(8,128)(2,1)} %collective-permute-done.12, bf16[64,4096]{1,0:T(8,128)(2,1)} %maximum_select_fusion.4, pred[]{:T(512)S(6)} %eq.17), kind=kLoop, calls=%fused_computation.4 | loop fusion | flops 4718592 | bytes 2097153 | tf_op jit(solution)/shard_map/jit(_where)/select_n | solution.py:74
  118.8 4.4 %backward.1.grads.refs_2_.refs_3_ = bf16[896,256]{1,0:T(8,128)(2,1)S(1)} custom-call(s32[1]{0:T(128)} %bitcast.2.core, bf16[128,4096]{1,0:T(8,128)(2,1)S(1)} %maximum_select_fusion.1.mine, bf16[128,4096]{1,0:T(8,128)(2,1)S(1)} %collective-permute-done.13.other, bf16[896,4096]{1,0:T(8,128)(2,1)} %bitcast.80, f32[896,128]{1,0:T(8,128)S(1)} %get-tuple-element.42.p, ...), custom_call_target="tpu_custom_call" | custom-call | flops 1879048192 | bytes 7340032 | tf_op jit(solution)/shard_map/backward/pallas_call | solution.py:197
  123.2 2.0 %collective-permute-start.14 = (bf16[896,256]{1,0:T(8,128)(2,1)S(1)}, bf16[896,256]{1,0:T(8,128)(2,1)S(1)}, u32[]{:S(2)}, u32[]{:S(2)}) collective-permute-start(bf16[896,256]{1,0:T(8,128)(2,1)S(1)} %backward.1.grads.refs_2_.refs_3_), channel_id=1, source_target_pairs={{0,16},{16,0},{1,17},{17,1},{2,18},{18,2},{3,19},{19,3},{4,20},{20... | collective-permute-start | bytes 1376264 | tf_op jit(solution)/shard_map/ppermute | solution.py:435
  127.0 4.3 %means.2.refs_4_.refs_5_ = f32[896,256]{1,0:T(8,128)S(1)} custom-call(bf16[896,256]{1,0:T(8,128)(2,1)S(1)} %backward.1.grads.refs_2_.refs_3_, bf16[128,4096]{1,0:T(8,128)(2,1)S(1)} %maximum_select_fusion.x.refs_6_.refs_7_), custom_call_target="tpu_custom_call" | custom-call | flops 1879048192 | bytes 1048576 | tf_op jit(solution)/shard_map/means/pallas_call | solution.py:241
  131.5 1.9 %collective-permute-start.22 = (bf16[128,2048]{1,0:T(8,128)(2,1)S(1)}, bf16[128,2048]{1,0:T(8,128)(2,1)S(1)}, u32[]{:S(2)}, u32[]{:S(2)}) collective-permute-start(bf16[128,2048]{1,0:T(8,128)(2,1)S(1)} %get-tuple-element.59), channel_id=1, source_target_pairs={{0,16},{16,0},{1,17},{17,1},{2,18},{18,2},{3,19},{19,3},{4,20},{20... | collective-permute-start | bytes 1572872 | tf_op jit(solution)/shard_map/ppermute | solution.py:435
  133.5 5.2 %collective-permute-done.14.grads.refs_3_.refs_4_ = bf16[896,256]{1,0:T(8,128)(2,1)S(1)} collective-permute-done((bf16[896,256]{1,0:T(8,128)(2,1)S(1)}, bf16[896,256]{1,0:T(8,128)(2,1)S(1)}, u32[]{:S(2)}, u32[]{:S(2)}) %collective-permute-start.14) | collective-permute-done | bytes 458784 | tf_op jit(solution)/shard_map/ppermute | solution.py:435
  139.0 1.8 %collective-permute-start.24 = (bf16[64,2048]{1,0:T(8,128)(2,1)S(1)}, bf16[64,2048]{1,0:T(8,128)(2,1)S(1)}, u32[]{:S(2)}, u32[]{:S(2)}) collective-permute-start(bf16[64,2048]{1,0:T(8,128)(2,1)S(1)} %pad_maximum_fusion), channel_id=1, source_target_pairs={{0,16},{16,0},{1,17},{17,1},{2,18},{18,2},{3,19},{19,3},{4,20},{20... | collective-permute-start | bytes 786440 | tf_op jit(solution)/shard_map/ppermute | solution.py:435
  140.8 4.3 %means.3.refs_5_.refs_6_ = f32[896,256]{1,0:T(8,128)S(1)} custom-call(bf16[896,256]{1,0:T(8,128)(2,1)S(1)} %collective-permute-done.14.grads.refs_3_.refs_4_, bf16[128,4096]{1,0:T(8,128)(2,1)S(1)} %slice_dynamic-update-slice_fusion.1.x.refs_7_.refs_8_), custom_call_target="tpu_custom_call" | custom-call | flops 1879048192 | bytes 1048576 | tf_op jit(solution)/shard_map/means/pallas_call | solution.py:241
  145.1 1.8 %prepare.1 = (bf16[64,2048]{1,0:T(8,128)(2,1)S(1)}, bf16[64,2048]{1,0:T(8,128)(2,1)S(1)}) custom-call(s32[1]{0:T(128)} %bitcast.refs_0_, bf16[896,4096]{1,0:T(8,128)(2,1)} %bitcast.71, bf16[896,256]{1,0:T(8,128)(2,1)S(1)} %backward.1.grads.refs_2_.refs_3_, bf16[896,256]{1,0:T(8,128)(2,1)S(1)} %collective-permute-done.14.grads.refs_3_.refs_4_, ...), custom_call_target="tpu_custom_call" | custom-call | flops 67108864 | bytes 786432 | tf_op jit(solution)/shard_map/prepare/pallas_call | solution.py:354
  146.9 2.5 %merge.6.refs_9_ = bf16[896,2048]{1,0:T(8,128)(2,1)} custom-call(s32[1]{0:T(128)} %bitcast.refs_0_, bf16[896,4096]{1,0:T(8,128)(2,1)} %bitcast.77, bf16[128,2048]{1,0:T(8,128)(2,1)S(1)} %collective-permute-done.3.refs_2_, bf16[896,256]{1,0:T(8,128)(2,1)S(1)} %backward.1.grads.refs_2_.refs_3_, ...), custom_call_target="tpu_custom_call" | custom-call | flops 134217728 | bytes 1572864 | tf_op jit(solution)/shard_map/merge/pallas_call | solution.py:300
  149.5 6.2 %merge.8.refs_9_ = bf16[896,2048]{1,0:T(8,128)(2,1)} custom-call(s32[1]{0:T(128)} %bitcast.refs_0_, bf16[896,4096]{1,0:T(8,128)(2,1)} %bitcast.72, bf16[480,2048]{1,0:T(8,128)(2,1)} %collective-permute-done.20.refs_2_, bf16[896,256]{1,0:T(8,128)(2,1)S(1)} %backward.1.grads.refs_2_.refs_3_, ...), custom_call_target="tpu_custom_call" | custom-call | flops 503316480 | bytes 5898240 | tf_op jit(solution)/shard_map/merge/pallas_call | solution.py:300
  155.7 7.9 %merge.7 = bf16[896,2048]{1,0:T(8,128)(2,1)} custom-call(s32[1]{0:T(128)} %bitcast.refs_0_, bf16[896,4096]{1,0:T(8,128)(2,1)} %bitcast.78, bf16[768,2048]{1,0:T(8,128)(2,1)} %collective-permute-done.19.refs_2_, bf16[896,256]{1,0:T(8,128)(2,1)S(1)} %backward.1.grads.refs_2_.refs_3_, ...), custom_call_target="tpu_custom_call", output_to_operand_aliasing={{}: (9, {})} | custom-call | flops 805306368 | bytes 9437184 | tf_op jit(solution)/shard_map/merge/pallas_call | solution.py:300
  163.5 2.3 %merge.9.refs_9_ = bf16[896,2048]{1,0:T(8,128)(2,1)} custom-call(s32[1]{0:T(128)} %bitcast.refs_0_, bf16[896,4096]{1,0:T(8,128)(2,1)} %bitcast.73, bf16[96,2048]{1,0:T(8,128)(2,1)S(1)} %collective-permute-done.21.refs_2_, bf16[896,256]{1,0:T(8,128)(2,1)S(1)} %backward.1.grads.refs_2_.refs_3_, ...), custom_call_target="tpu_custom_call", output_to_operand_aliasing={{}: (9, {})} | custom-call | flops 100663296 | bytes 1179648 | tf_op jit(solution)/shard_map/merge/pallas_call | solution.py:300
  165.8 2.5 %merge.10.refs_9_ = bf16[896,2048]{1,0:T(8,128)(2,1)} custom-call(s32[1]{0:T(128)} %bitcast.refs_0_, bf16[896,4096]{1,0:T(8,128)(2,1)} %bitcast.74, bf16[128,2048]{1,0:T(8,128)(2,1)S(1)} %collective-permute-done.22.refs_2_, bf16[896,256]{1,0:T(8,128)(2,1)S(1)} %backward.1.grads.refs_2_.refs_3_, ...), custom_call_target="tpu_custom_call", output_to_operand_aliasing={{}: (9, {})} | custom-call | flops 134217728 | bytes 1572864 | tf_op jit(solution)/shard_map/merge/pallas_call | solution.py:300
  169.6 2.5 %merge.11.refs_2_ = bf16[896,2048]{1,0:T(8,128)(2,1)} custom-call(s32[1]{0:T(128)} %bitcast.refs_0_, bf16[896,4096]{1,0:T(8,128)(2,1)} %bitcast.75, bf16[128,2048]{1,0:T(8,128)(2,1)S(1)} %collective-permute-done.23.refs_2_, bf16[896,256]{1,0:T(8,128)(2,1)S(1)} %backward.1.grads.refs_2_.refs_3_, ...), custom_call_target="tpu_custom_call", output_to_operand_aliasing={{}: (9, {})} | custom-call | flops 134217728 | bytes 1572864 | tf_op jit(solution)/shard_map/merge/pallas_call | solution.py:300
  172.1 2.0 %collective-permute-done.24.refs_1_ = bf16[64,2048]{1,0:T(8,128)(2,1)S(1)} collective-permute-done((bf16[64,2048]{1,0:T(8,128)(2,1)S(1)}, bf16[64,2048]{1,0:T(8,128)(2,1)S(1)}, u32[]{:S(2)}, u32[]{:S(2)}) %collective-permute-start.24) | collective-permute-done | bytes 262176 | tf_op jit(solution)/shard_map/ppermute | solution.py:435
  (84 shorter events, 27.5 us)
Async XLA Ops:
  0.6 5.8 %collective-permute-start = (bf16[8,4096]{1,0:T(8,128)(2,1)}, bf16[8,4096]{1,0:T(8,128)(2,1)S(1)}, u32[]{:S(2)}, u32[]{:S(2)}) collective-permute-start(bf16[8,4096]{1,0:T(8,128)(2,1)} %bitcast.81), channel_id=1, source_target_pairs={{0,16},{16,0},{1,17},{17,1},{2,18},{18,2},{3,19},{19,3},{4,20},{20... | collective-permute-start | bytes 196616 | tf_op jit(solution)/shard_map/ppermute | solution.py:435
  4.7 10.6 %copy-start.5 = (bf16[1,8,4096]{2,1,0:T(8,128)(2,1)S(1)}, bf16[1,8,4096]{2,1,0:T(8,128)(2,1)}, u32[]{:S(2)}) copy-start(bf16[1,8,4096]{2,1,0:T(8,128)(2,1)} %param.6) | copy-start | bytes 196612
  4.7 24.7 %collective-permute-start.3 = (bf16[128,2048]{1,0:T(8,128)(2,1)S(1)}, bf16[128,2048]{1,0:T(8,128)(2,1)S(1)}, u32[]{:S(2)}, u32[]{:S(2)}) collective-permute-start(bf16[128,2048]{1,0:T(8,128)(2,1)S(1)} %dynamic-slice_bitcast_fusion.2), channel_id=1, source_target_pairs={{0,16},{16,0},{1,17},{17,1},{2,18},{18,2},{3,19},{19,3},{4,20},{20... | collective-permute-start | bytes 1572872 | tf_op jit(solution)/shard_map/ppermute | solution.py:435
  6.4 9.3 %collective-permute-start.15 = (bf16[8,4096]{1,0:T(8,128)(2,1)S(1)}, bf16[8,4096]{1,0:T(8,128)(2,1)S(1)}, u32[]{:S(2)}, u32[]{:S(2)}) collective-permute-start(bf16[8,4096]{1,0:T(8,128)(2,1)S(1)} %collective-permute-done), channel_id=1, source_target_pairs={{0,8},{1,9},{2,10},{3,11},{4,12},{5,13},{6,14},{7,15},{8,0},{9,1},... | collective-permute-start | bytes 196616 | tf_op jit(solution)/shard_map/ppermute | solution.py:48
  13.2 142.5 %collective-permute-start.19 = (bf16[768,2048]{1,0:T(8,128)(2,1)}, bf16[768,2048]{1,0:T(8,128)(2,1)}, u32[]{:S(2)}, u32[]{:S(2)}) collective-permute-start(bf16[768,2048]{1,0:T(8,128)(2,1)} %dynamic-slice_bitcast_fusion), channel_id=1, source_target_pairs={{0,16},{16,0},{1,17},{17,1},{2,18},{18,2},{3,19},{19,3},{4,20},{20... | collective-permute-start | bytes 9437192 | tf_op jit(solution)/shard_map/ppermute | solution.py:435
  15.3 7.6 %collective-permute-start.1 = (bf16[8,4096]{1,0:T(8,128)(2,1)S(1)}, bf16[8,4096]{1,0:T(8,128)(2,1)S(1)}, u32[]{:S(2)}, u32[]{:S(2)}) collective-permute-start(bf16[8,4096]{1,0:T(8,128)(2,1)S(1)} %bitcast.82), channel_id=1, source_target_pairs={{0,8},{1,3},{2,10},{3,1},{4,12},{5,7},{6,14},{7,5},{8,0},{9,11},{1... | collective-permute-start | bytes 196616 | tf_op jit(solution)/shard_map/ppermute | solution.py:48
  15.7 7.3 %collective-permute-start.16 = (bf16[16,4096]{1,0:T(8,128)(2,1)S(1)}, bf16[16,4096]{1,0:T(8,128)(2,1)S(1)}, u32[]{:S(2)}, u32[]{:S(2)}) collective-permute-start(bf16[16,4096]{1,0:T(8,128)(2,1)S(1)} %maximum_select_fusion.10), channel_id=1, source_target_pairs={{0,4},{1,5},{2,6},{3,7},{4,0},{5,1},{6,2},{7,3},{8,12},{9,13},{10,... | collective-permute-start | bytes 393224 | tf_op jit(solution)/shard_map/ppermute | solution.py:48
  22.9 6.4 %collective-permute-start.2 = (bf16[16,4096]{1,0:T(8,128)(2,1)S(1)}, bf16[16,4096]{1,0:T(8,128)(2,1)S(1)}, u32[]{:S(2)}, u32[]{:S(2)}) collective-permute-start(bf16[16,4096]{1,0:T(8,128)(2,1)S(1)} %maximum_select_fusion.9), channel_id=1, source_target_pairs={{0,4},{1,9},{2,6},{3,11},{4,0},{5,13},{6,2},{7,15},{8,12},{9,1},{1... | collective-permute-start | bytes 393224 | tf_op jit(solution)/shard_map/ppermute | solution.py:48
  23.1 8.0 %collective-permute-start.17 = (bf16[32,4096]{1,0:T(8,128)(2,1)S(1)}, bf16[32,4096]{1,0:T(8,128)(2,1)S(1)}, u32[]{:S(2)}, u32[]{:S(2)}) collective-permute-start(bf16[32,4096]{1,0:T(8,128)(2,1)S(1)} %maximum_select_fusion.8), channel_id=1, source_target_pairs={{0,2},{1,3},{2,0},{3,1},{4,6},{5,7},{6,4},{7,5},{8,10},{9,11},{10,... | collective-permute-start | bytes 786440 | tf_op jit(solution)/shard_map/ppermute | solution.py:48
  29.4 9.7 %copy-start.6 = (s32[1,2,896]{2,1,0:T(2,128)S(1)}, s32[1,2,896]{2,1,0:T(2,128)}, u32[]{:S(2)}) copy-start(s32[1,2,896]{2,1,0:T(2,128)} %param.11) | copy-start | bytes 21508
  29.4 6.4 %collective-permute-start.4 = (bf16[32,4096]{1,0:T(8,128)(2,1)S(1)}, bf16[32,4096]{1,0:T(8,128)(2,1)S(1)}, u32[]{:S(2)}, u32[]{:S(2)}) collective-permute-start(bf16[32,4096]{1,0:T(8,128)(2,1)S(1)} %maximum_select_fusion.6), channel_id=1, source_target_pairs={{0,2},{1,5},{2,0},{3,7},{4,6},{5,1},{6,4},{7,3},{8,10},{9,13},{10,... | collective-permute-start | bytes 786440 | tf_op jit(solution)/shard_map/ppermute | solution.py:48
  31.1 8.2 %collective-permute-start.18 = (bf16[64,4096]{1,0:T(8,128)(2,1)S(1)}, bf16[64,4096]{1,0:T(8,128)(2,1)S(1)}, u32[]{:S(2)}, u32[]{:S(2)}) collective-permute-start(bf16[64,4096]{1,0:T(8,128)(2,1)S(1)} %maximum_select_fusion.5), channel_id=1, source_target_pairs={{0,1},{1,0},{2,3},{3,2},{4,5},{5,4},{6,7},{7,6},{8,9},{9,8},{10,11... | collective-permute-start | bytes 1572872 | tf_op jit(solution)/shard_map/ppermute | solution.py:457
  36.0 3.6 %collective-permute-start.5 = (bf16[64,4096]{1,0:T(8,128)(2,1)S(1)}, bf16[64,4096]{1,0:T(8,128)(2,1)}, u32[]{:S(2)}, u32[]{:S(2)}) collective-permute-start(bf16[64,4096]{1,0:T(8,128)(2,1)S(1)} %maximum_select_fusion.3), channel_id=1, source_target_pairs={{0,1},{1,0},{2,3},{3,2},{4,5},{5,4},{6,7},{7,6},{8,9},{9,8},{10,11... | collective-permute-start | bytes 1572872 | tf_op jit(solution)/shard_map/ppermute | solution.py:457
  39.1 1.9 %copy-start.4 = (s32[1,2,4096]{2,1,0:T(2,128)S(1)}, s32[1,2,4096]{2,1,0:T(2,128)}, u32[]{:S(2)}) copy-start(s32[1,2,4096]{2,1,0:T(2,128)} %param.10) | copy-start | bytes 98308
  39.1 99.9 %collective-permute-start.20 = (bf16[480,2048]{1,0:T(8,128)(2,1)}, bf16[480,2048]{1,0:T(8,128)(2,1)}, u32[]{:S(2)}, u32[]{:S(2)}) collective-permute-start(bf16[480,2048]{1,0:T(8,128)(2,1)} %dynamic-slice_bitcast_fusion.1), channel_id=1, source_target_pairs={{0,16},{16,0},{1,17},{17,1},{2,18},{18,2},{3,19},{19,3},{4,20},{20... | collective-permute-start | bytes 5898248 | tf_op jit(solution)/shard_map/ppermute | solution.py:435
  54.6 0.8 copy-start
  55.4 12.5 %copy-start.2 = (f32[896,128]{1,0:T(8,128)}, f32[896,128]{1,0:T(8,128)S(1)}, u32[]{:S(2)}) copy-start(f32[896,128]{1,0:T(8,128)S(1)} %get-tuple-element.45.sd) | copy-start | bytes 1376260
  55.4 2.8 %collective-permute-start.6 = (bf16[128,4096]{1,0:T(8,128)(2,1)S(1)}, bf16[128,4096]{1,0:T(8,128)(2,1)S(1)}, u32[]{:S(2)}, u32[]{:S(2)}) collective-permute-start(bf16[128,4096]{1,0:T(8,128)(2,1)S(1)} %get-tuple-element.41), channel_id=1, source_target_pairs={{0,1},{1,0},{2,3},{3,2},{4,5},{5,4},{6,7},{7,6},{8,9},{9,8},{10,11... | collective-permute-start | bytes 3145736 | tf_op jit(solution)/shard_map/ppermute | solution.py:490
  58.4 9.2 %collective-permute-start.7 = (bf16[64,4096]{1,0:T(8,128)(2,1)S(1)}, bf16[64,4096]{1,0:T(8,128)(2,1)S(1)}, u32[]{:S(2)}, u32[]{:S(2)}) collective-permute-start(bf16[64,4096]{1,0:T(8,128)(2,1)S(1)} %constant_dynamic-slice_fusion.2), channel_id=1, source_target_pairs={{0,2},{1,5},{2,0},{3,7},{4,6},{5,1},{6,4},{7,3},{8,10},{9,13},{10,... | collective-permute-start | bytes 1572872 | tf_op jit(solution)/shard_map/ppermute | solution.py:48
  67.9 9.1 %collective-permute-start.8 = (bf16[32,4096]{1,0:T(8,128)(2,1)S(1)}, bf16[32,4096]{1,0:T(8,128)(2,1)S(1)}, u32[]{:S(2)}, u32[]{:S(2)}) collective-permute-start(bf16[32,4096]{1,0:T(8,128)(2,1)S(1)} %constant_dynamic-slice_fusion.1), channel_id=1, source_target_pairs={{0,4},{1,9},{2,6},{3,11},{4,0},{5,13},{6,2},{7,15},{8,12},{9,1},{1... | collective-permute-start | bytes 786440 | tf_op jit(solution)/shard_map/ppermute | solution.py:48
  77.0 6.3 %collective-permute-start.9 = (bf16[16,4096]{1,0:T(8,128)(2,1)S(1)}, bf16[16,4096]{1,0:T(8,128)(2,1)S(1)}, u32[]{:S(2)}, u32[]{:S(2)}) collective-permute-start(bf16[16,4096]{1,0:T(8,128)(2,1)S(1)} %constant_dynamic-slice_fusion), channel_id=1, source_target_pairs={{0,8},{1,3},{2,10},{3,1},{4,12},{5,7},{6,14},{7,5},{8,0},{9,11},{1... | collective-permute-start | bytes 393224 | tf_op jit(solution)/shard_map/ppermute | solution.py:48
  83.4 10.5 %collective-permute-start.10 = (bf16[16,4096]{1,0:T(8,128)(2,1)S(1)}, bf16[16,4096]{1,0:T(8,128)(2,1)S(1)}, u32[]{:S(2)}, u32[]{:S(2)}) collective-permute-start(bf16[16,4096]{1,0:T(8,128)(2,1)S(1)} %add_convert_fusion.3), channel_id=1, source_target_pairs={{0,8},{1,3},{2,10},{3,1},{4,12},{5,7},{6,14},{7,5},{8,0},{9,11},{1... | collective-permute-start | bytes 393224 | tf_op jit(solution)/shard_map/ppermute | solution.py:48
  93.9 7.9 %collective-permute-start.11 = (bf16[32,4096]{1,0:T(8,128)(2,1)S(1)}, bf16[32,4096]{1,0:T(8,128)(2,1)S(1)}, u32[]{:S(2)}, u32[]{:S(2)}) collective-permute-start(bf16[32,4096]{1,0:T(8,128)(2,1)S(1)} %maximum_select_fusion.7), channel_id=1, source_target_pairs={{0,4},{1,9},{2,6},{3,11},{4,0},{5,13},{6,2},{7,15},{8,12},{9,1},{1... | collective-permute-start | bytes 786440 | tf_op jit(solution)/shard_map/ppermute | solution.py:48
  102.7 9.5 %collective-permute-start.12 = (bf16[64,4096]{1,0:T(8,128)(2,1)}, bf16[64,4096]{1,0:T(8,128)(2,1)}, u32[]{:S(2)}, u32[]{:S(2)}) collective-permute-start(bf16[64,4096]{1,0:T(8,128)(2,1)} %maximum_select_fusion.4), channel_id=1, source_target_pairs={{0,2},{1,5},{2,0},{3,7},{4,6},{5,1},{6,4},{7,3},{8,10},{9,13},{10,... | collective-permute-start | bytes 1572872 | tf_op jit(solution)/shard_map/ppermute | solution.py:48
  104.2 14.5 %copy-start.1 = (f32[896,128]{1,0:T(8,128)S(1)}, f32[896,128]{1,0:T(8,128)}, u32[]{:S(2)}) copy-start(f32[896,128]{1,0:T(8,128)} %copy-done) | copy-start | bytes 1376260
  104.2 14.5 %copy-start.3 = (f32[896,128]{1,0:T(8,128)S(1)}, f32[896,128]{1,0:T(8,128)}, u32[]{:S(2)}) copy-start(f32[896,128]{1,0:T(8,128)} %copy-done.2) | copy-start | bytes 1376260
  114.0 4.7 %collective-permute-start.13 = (bf16[128,4096]{1,0:T(8,128)(2,1)S(1)}, bf16[128,4096]{1,0:T(8,128)(2,1)S(1)}, u32[]{:S(2)}, u32[]{:S(2)}) collective-permute-start(bf16[128,4096]{1,0:T(8,128)(2,1)S(1)} %maximum_select_fusion.1.mine), channel_id=1, source_target_pairs={{0,1},{1,0},{2,3},{3,2},{4,5},{5,4},{6,7},{7,6},{8,9},{9,8},{10,11... | collective-permute-start | bytes 3145736 | tf_op jit(solution)/shard_map/ppermute | solution.py:493
  123.2 15.5 %collective-permute-start.14 = (bf16[896,256]{1,0:T(8,128)(2,1)S(1)}, bf16[896,256]{1,0:T(8,128)(2,1)S(1)}, u32[]{:S(2)}, u32[]{:S(2)}) collective-permute-start(bf16[896,256]{1,0:T(8,128)(2,1)S(1)} %backward.1.grads.refs_2_.refs_3_), channel_id=1, source_target_pairs={{0,16},{16,0},{1,17},{17,1},{2,18},{18,2},{3,19},{19,3},{4,20},{20... | collective-permute-start | bytes 1376264 | tf_op jit(solution)/shard_map/ppermute | solution.py:435
  131.4 32.2 %collective-permute-start.21 = (bf16[96,2048]{1,0:T(8,128)(2,1)S(1)}, bf16[96,2048]{1,0:T(8,128)(2,1)S(1)}, u32[]{:S(2)}, u32[]{:S(2)}) collective-permute-start(bf16[96,2048]{1,0:T(8,128)(2,1)S(1)} %get-tuple-element.53), channel_id=1, source_target_pairs={{0,16},{16,0},{1,17},{17,1},{2,18},{18,2},{3,19},{19,3},{4,20},{20... | collective-permute-start | bytes 1179656 | tf_op jit(solution)/shard_map/ppermute | solution.py:435
  131.5 34.3 %collective-permute-start.22 = (bf16[128,2048]{1,0:T(8,128)(2,1)S(1)}, bf16[128,2048]{1,0:T(8,128)(2,1)S(1)}, u32[]{:S(2)}, u32[]{:S(2)}) collective-permute-start(bf16[128,2048]{1,0:T(8,128)(2,1)S(1)} %get-tuple-element.59), channel_id=1, source_target_pairs={{0,16},{16,0},{1,17},{17,1},{2,18},{18,2},{3,19},{19,3},{4,20},{20... | collective-permute-start | bytes 1572872 | tf_op jit(solution)/shard_map/ppermute | solution.py:435
  138.7 30.9 %collective-permute-start.23 = (bf16[128,2048]{1,0:T(8,128)(2,1)S(1)}, bf16[128,2048]{1,0:T(8,128)(2,1)S(1)}, u32[]{:S(2)}, u32[]{:S(2)}) collective-permute-start(bf16[128,2048]{1,0:T(8,128)(2,1)S(1)} %get-tuple-element.65), channel_id=1, source_target_pairs={{0,16},{16,0},{1,17},{17,1},{2,18},{18,2},{3,19},{19,3},{4,20},{20... | collective-permute-start | bytes 1572872 | tf_op jit(solution)/shard_map/ppermute | solution.py:435
  139.0 35.0 %collective-permute-start.24 = (bf16[64,2048]{1,0:T(8,128)(2,1)S(1)}, bf16[64,2048]{1,0:T(8,128)(2,1)S(1)}, u32[]{:S(2)}, u32[]{:S(2)}) collective-permute-start(bf16[64,2048]{1,0:T(8,128)(2,1)S(1)} %pad_maximum_fusion), channel_id=1, source_target_pairs={{0,16},{16,0},{1,17},{17,1},{2,18},{18,2},{3,19},{19,3},{4,20},{20... | collective-permute-start | bytes 786440 | tf_op jit(solution)/shard_map/ppermute | solution.py:435

commit v5 on v4

--- a/solution.py
+++ b/solution.py
@@ -370,30 +370,40 @@
     )(spot, weight, *grads, *scales, *xs)
 
 
-def finish_kernel(members, share, *refs):
+def finish_kernel(members, start, parts, share, *refs):
     others, refs = refs[:members - 1], refs[members - 1:]
-    weights, out = refs[:members - 1], refs[-1]
-    total = share[...].astype(F32)
-    for w, weight in zip(others, weights):
-        total = total + w[...].astype(F32) * weight[...].astype(F32)
-    out[...] = total.astype(BF16)
+    weights, refs = refs[:members - 1], refs[members - 1:]
+    _, out, made, sems = refs
+    rows = share.shape[0] // parts
+    copies = []
+    for part in range(parts):
+        here = pl.ds(part * rows, rows)
+        total = share[here, :].astype(F32)
+        for w, weight in zip(others, weights):
+            total = total + w[here, :].astype(F32) * weight[here, :].astype(F32)
+        made[here, :] = total.astype(BF16)
+        copies.append(pltpu.make_async_copy(
+            made.at[here, :], out.at[pl.ds(start + part * rows, rows), :], sems.at[part]
+        ))
+        copies[-1].start()
+    for copy in copies:
+        copy.wait()
 
 
 def finish(piece, ready, received, so_far):
     _, start, rows = piece
     width = so_far.shape[1]
-    block = math.gcd(rows, start, 32)
-    first = start // block
+    parts = 2 if rows % 32 == 0 else 1
     args = [*ready, *received]
     return pl.pallas_call(
-        functools.partial(finish_kernel, len(ready)),
+        functools.partial(finish_kernel, len(ready), start, parts),
         out_shape=jax.ShapeDtypeStruct(so_far.shape, BF16),
-        grid=(rows // block,),
-        in_specs=[pl.BlockSpec((block, width), lambda i: (i, 0))] * len(args)
+        in_specs=[pl.BlockSpec(memory_space=pltpu.VMEM)] * len(args)
         + [pl.BlockSpec(memory_space=pl.ANY)],
-        out_specs=pl.BlockSpec((block, width), lambda i: (first + i, 0)),
+        out_specs=pl.BlockSpec(memory_space=pl.ANY),
+        scratch_shapes=[pltpu.VMEM((rows, width), BF16), pltpu.SemaphoreType.DMA((parts,))],
         input_output_aliases={len(args): 0},
-        compiler_params=params(),
+        compiler_params=pltpu.CompilerParams(vmem_limit_bytes=16 * 1024 * 1024),
         cost_estimate=pl.CostEstimate(
             flops=2 * rows * width, bytes_accessed=8 * rows * width, transcendentals=0
         ),

time: 176 us -> 176 us (level)
  no operation moved by 1% of the time
where the time goes in v5:
time: 176 us; the launch traced here: 175 us
  waiting for transfers between devices  74.5 us (42%)
  Pallas kernels  53 us (30%)
  starting transfers between devices  23.5 us (13%)
  local copies, waits for them, and re-layouts  17.6 us (10%)
  other arithmetic  5.19 us (3%)
    ppermute x12, waiting for transfers between devices, swap(): return lax.ppermute(value, axis, pairs)  62.2 us
    pallas_call x6, Pallas kernels, merge(): pl.pallas_call(functools.partial(merge_kernel, members), out_shape=jax.Sh...  23.9 us
    pallas_call x1, Pallas kernels, forward(): pl.pallas_call(functools.partial(forward_kernel, width ** (-0.5), steps),...  13.5 us
    ppermute x9, starting transfers between devices, across(): lax.ppermute(value, 'ckpt', [(i, (i + shift) % n_ckpt) for i in range(n_c...  11.4 us
    ppermute x12, starting transfers between devices, swap(): return lax.ppermute(value, axis, pairs)  11.4 us
    ppermute x9, waiting for transfers between devices, across(): lax.ppermute(value, 'ckpt', [(i, (i + shift) % n_ckpt) for i in range(n_c...  10.1 us
    pallas_call x2, Pallas kernels, means(): pl.pallas_call(means_kernel, out_shape=jax.ShapeDtypeStruct((units, 2 * L...  8.62 us
    dynamic_slice x3, local copies, waits for them, and re-layouts, cut(): lax.dynamic_slice(weights[which], (start, left), (rows, part))  8.08 us
  transfers between devices with their start and end apart: 25, of which 14 were waited for; matrix products, arithmetic and copies ran while one was open for 13% of the time, Pallas kernels for 30%

profile of v5, /device:TPU:0, one launch (start us, length us, event | category | flops | bytes accessed | tf_op | source)
XLA Modules:
  0.0 175.0 jit_solution(4052206420441958001)
XLA Ops:
  0.6 3.0 %collective-permute-start = (bf16[8,4096]{1,0:T(8,128)(2,1)}, bf16[8,4096]{1,0:T(8,128)(2,1)S(1)}, u32[]{:S(2)}, u32[]{:S(2)}) collective-permute-start(bf16[8,4096]{1,0:T(8,128)(2,1)} %bitcast.81), channel_id=1, source_target_pairs={{0,16},{16,0},{1,17},{17,1},{2,18},{18,2},{3,19},{19,3},{4,20},{20... | collective-permute-start | bytes 196616 | tf_op jit(solution)/shard_map/ppermute | solution.py:445
  6.4 2.8 %collective-permute-start.15 = (bf16[8,4096]{1,0:T(8,128)(2,1)S(1)}, bf16[8,4096]{1,0:T(8,128)(2,1)S(1)}, u32[]{:S(2)}, u32[]{:S(2)}) collective-permute-start(bf16[8,4096]{1,0:T(8,128)(2,1)S(1)} %collective-permute-done), channel_id=1, source_target_pairs={{0,8},{1,9},{2,10},{3,11},{4,12},{5,13},{6,14},{7,15},{8,0},{9,1},... | collective-permute-start | bytes 196616 | tf_op jit(solution)/shard_map/ppermute | solution.py:48
  9.2 4.0 %dynamic-slice_bitcast_fusion = bf16[768,2048]{1,0:T(8,128)(2,1)} fusion(bf16[1,896,4096]{2,1,0:T(8,128)(2,1)} %param.7, s32[]{:T(128)S(6)} %select_n.154), kind=kLoop, calls=%fused_computation | loop fusion | bytes 6291460 | tf_op jit(solution)/shard_map/dynamic_slice | solution.py:451
  13.2 2.1 %collective-permute-start.19 = (bf16[768,2048]{1,0:T(8,128)(2,1)}, bf16[768,2048]{1,0:T(8,128)(2,1)}, u32[]{:S(2)}, u32[]{:S(2)}) collective-permute-start(bf16[768,2048]{1,0:T(8,128)(2,1)} %dynamic-slice_bitcast_fusion), channel_id=1, source_target_pairs={{0,16},{16,0},{1,17},{17,1},{2,18},{18,2},{3,19},{19,3},{4,20},{20... | collective-permute-start | bytes 9437192 | tf_op jit(solution)/shard_map/ppermute | solution.py:445
  17.3 5.6 %collective-permute-done.1 = bf16[8,4096]{1,0:T(8,128)(2,1)S(1)} collective-permute-done((bf16[8,4096]{1,0:T(8,128)(2,1)S(1)}, bf16[8,4096]{1,0:T(8,128)(2,1)S(1)}, u32[]{:S(2)}, u32[]{:S(2)}) %collective-permute-start.1) | collective-permute-done | bytes 65568 | tf_op jit(solution)/shard_map/ppermute | solution.py:48
  24.7 4.7 %collective-permute-done.2 = bf16[16,4096]{1,0:T(8,128)(2,1)S(1)} collective-permute-done((bf16[16,4096]{1,0:T(8,128)(2,1)S(1)}, bf16[16,4096]{1,0:T(8,128)(2,1)S(1)}, u32[]{:S(2)}, u32[]{:S(2)}) %collective-permute-start.2) | collective-permute-done | bytes 131104 | tf_op jit(solution)/shard_map/ppermute | solution.py:48
  31.2 4.7 %collective-permute-done.4 = bf16[32,4096]{1,0:T(8,128)(2,1)S(1)} collective-permute-done((bf16[32,4096]{1,0:T(8,128)(2,1)S(1)}, bf16[32,4096]{1,0:T(8,128)(2,1)S(1)}, u32[]{:S(2)}, u32[]{:S(2)}) %collective-permute-start.4) | collective-permute-done | bytes 262176 | tf_op jit(solution)/shard_map/ppermute | solution.py:48
  36.1 3.1 %dynamic-slice_bitcast_fusion.1 = bf16[480,2048]{1,0:T(8,128)(2,1)} fusion(bf16[1,896,4096]{2,1,0:T(8,128)(2,1)} %param.8, s32[]{:T(128)S(6)} %select_n.154), kind=kLoop, calls=%fused_computation.2 | loop fusion | bytes 3932164 | tf_op jit(solution)/shard_map/dynamic_slice | solution.py:451
  41.1 13.5 %forward.1 = (f32[896,128]{1,0:T(8,128)S(1)}, f32[896,128]{1,0:T(8,128)S(1)}, f32[896,128]{1,0:T(8,128)S(1)}, f32[896,128]{1,0:T(8,128)S(1)}, bf16[128,4096]{1,0...) custom-call(s32[1]{0:T(128)} %bitcast.2.core, bf16[128,4096]{1,0:T(8,128)(2,1)S(1)} %maximum_select_fusion.x.refs_6_.refs_7_, ...), custom_call_target="tpu_custom_call" | custom-call | flops 5637144576 | bytes 22020096 | tf_op jit(solution)/shard_map/forward/pallas_call | solution.py:149
  55.9 2.2 %collective-permute-done.6 = bf16[128,4096]{1,0:T(8,128)(2,1)S(1)} collective-permute-done((bf16[128,4096]{1,0:T(8,128)(2,1)S(1)}, bf16[128,4096]{1,0:T(8,128)(2,1)S(1)}, u32[]{:S(2)}, u32[]{:S(2)}) %collective-permute-start.6) | collective-permute-done | bytes 1048608 | tf_op jit(solution)/shard_map/ppermute | solution.py:500
  60.0 7.7 %collective-permute-done.7 = bf16[64,4096]{1,0:T(8,128)(2,1)S(1)} collective-permute-done((bf16[64,4096]{1,0:T(8,128)(2,1)S(1)}, bf16[64,4096]{1,0:T(8,128)(2,1)S(1)}, u32[]{:S(2)}, u32[]{:S(2)}) %collective-permute-start.7) | collective-permute-done | bytes 524320 | tf_op jit(solution)/shard_map/ppermute | solution.py:48
  68.0 9.0 %collective-permute-done.8 = bf16[32,4096]{1,0:T(8,128)(2,1)S(1)} collective-permute-done((bf16[32,4096]{1,0:T(8,128)(2,1)S(1)}, bf16[32,4096]{1,0:T(8,128)(2,1)S(1)}, u32[]{:S(2)}, u32[]{:S(2)}) %collective-permute-start.8) | collective-permute-done | bytes 262176 | tf_op jit(solution)/shard_map/ppermute | solution.py:48
  77.1 6.3 %collective-permute-done.9 = bf16[16,4096]{1,0:T(8,128)(2,1)S(1)} collective-permute-done((bf16[16,4096]{1,0:T(8,128)(2,1)S(1)}, bf16[16,4096]{1,0:T(8,128)(2,1)S(1)}, u32[]{:S(2)}, u32[]{:S(2)}) %collective-permute-start.9) | collective-permute-done | bytes 131104 | tf_op jit(solution)/shard_map/ppermute | solution.py:48
  83.5 10.4 %collective-permute-done.10 = bf16[16,4096]{1,0:T(8,128)(2,1)S(1)} collective-permute-done((bf16[16,4096]{1,0:T(8,128)(2,1)S(1)}, bf16[16,4096]{1,0:T(8,128)(2,1)S(1)}, u32[]{:S(2)}, u32[]{:S(2)}) %collective-permute-start.10) | collective-permute-done | bytes 131104 | tf_op jit(solution)/shard_map/ppermute | solution.py:48
  94.0 7.8 %collective-permute-done.11 = bf16[32,4096]{1,0:T(8,128)(2,1)S(1)} collective-permute-done((bf16[32,4096]{1,0:T(8,128)(2,1)S(1)}, bf16[32,4096]{1,0:T(8,128)(2,1)S(1)}, u32[]{:S(2)}, u32[]{:S(2)}) %collective-permute-start.11) | collective-permute-done | bytes 262176 | tf_op jit(solution)/shard_map/ppermute | solution.py:48
  106.1 6.1 %collective-permute-done.12 = bf16[64,4096]{1,0:T(8,128)(2,1)} collective-permute-done((bf16[64,4096]{1,0:T(8,128)(2,1)}, bf16[64,4096]{1,0:T(8,128)(2,1)}, u32[]{:S(2)}, u32[]{:S(2)}) %collective-permute-start.12) | collective-permute-done | bytes 524320 | tf_op jit(solution)/shard_map/ppermute | solution.py:48
  112.2 1.8 %maximum_select_fusion.1.mine = bf16[128,4096]{1,0:T(8,128)(2,1)S(1)} fusion(bf16[64,4096]{1,0:T(8,128)(2,1)} %collective-permute-done.12, bf16[64,4096]{1,0:T(8,128)(2,1)} %maximum_select_fusion.4, pred[]{:T(512)S(6)} %eq.17), kind=kLoop, calls=%fused_computation.4 | loop fusion | flops 4718592 | bytes 2097153 | tf_op jit(solution)/shard_map/jit(_where)/select_n | solution.py:74
  118.8 4.4 %backward.1.grads.refs_2_.refs_3_ = bf16[896,256]{1,0:T(8,128)(2,1)S(1)} custom-call(s32[1]{0:T(128)} %bitcast.2.core, bf16[128,4096]{1,0:T(8,128)(2,1)S(1)} %maximum_select_fusion.1.mine, bf16[128,4096]{1,0:T(8,128)(2,1)S(1)} %collective-permute-done.13.other, bf16[896,4096]{1,0:T(8,128)(2,1)} %bitcast.80, f32[896,128]{1,0:T(8,128)S(1)} %get-tuple-element.42.p, ...), custom_call_target="tpu_custom_call" | custom-call | flops 1879048192 | bytes 7340032 | tf_op jit(solution)/shard_map/backward/pallas_call | solution.py:197
  123.2 2.0 %collective-permute-start.14 = (bf16[896,256]{1,0:T(8,128)(2,1)S(1)}, bf16[896,256]{1,0:T(8,128)(2,1)S(1)}, u32[]{:S(2)}, u32[]{:S(2)}) collective-permute-start(bf16[896,256]{1,0:T(8,128)(2,1)S(1)} %backward.1.grads.refs_2_.refs_3_), channel_id=1, source_target_pairs={{0,16},{16,0},{1,17},{17,1},{2,18},{18,2},{3,19},{19,3},{4,20},{20... | collective-permute-start | bytes 1376264 | tf_op jit(solution)/shard_map/ppermute | solution.py:445
  127.0 4.3 %means.2.refs_4_.refs_5_ = f32[896,256]{1,0:T(8,128)S(1)} custom-call(bf16[896,256]{1,0:T(8,128)(2,1)S(1)} %backward.1.grads.refs_2_.refs_3_, bf16[128,4096]{1,0:T(8,128)(2,1)S(1)} %maximum_select_fusion.x.refs_6_.refs_7_), custom_call_target="tpu_custom_call" | custom-call | flops 1879048192 | bytes 1048576 | tf_op jit(solution)/shard_map/means/pallas_call | solution.py:241
  131.5 1.9 %collective-permute-start.22 = (bf16[128,2048]{1,0:T(8,128)(2,1)S(1)}, bf16[128,2048]{1,0:T(8,128)(2,1)S(1)}, u32[]{:S(2)}, u32[]{:S(2)}) collective-permute-start(bf16[128,2048]{1,0:T(8,128)(2,1)S(1)} %get-tuple-element.59), channel_id=1, source_target_pairs={{0,16},{16,0},{1,17},{17,1},{2,18},{18,2},{3,19},{19,3},{4,20},{20... | collective-permute-start | bytes 1572872 | tf_op jit(solution)/shard_map/ppermute | solution.py:445
  133.5 5.2 %collective-permute-done.14.grads.refs_3_.refs_4_ = bf16[896,256]{1,0:T(8,128)(2,1)S(1)} collective-permute-done((bf16[896,256]{1,0:T(8,128)(2,1)S(1)}, bf16[896,256]{1,0:T(8,128)(2,1)S(1)}, u32[]{:S(2)}, u32[]{:S(2)}) %collective-permute-start.14) | collective-permute-done | bytes 458784 | tf_op jit(solution)/shard_map/ppermute | solution.py:445
  139.0 1.8 %collective-permute-start.24 = (bf16[64,2048]{1,0:T(8,128)(2,1)S(1)}, bf16[64,2048]{1,0:T(8,128)(2,1)S(1)}, u32[]{:S(2)}, u32[]{:S(2)}) collective-permute-start(bf16[64,2048]{1,0:T(8,128)(2,1)S(1)} %pad_maximum_fusion), channel_id=1, source_target_pairs={{0,16},{16,0},{1,17},{17,1},{2,18},{18,2},{3,19},{19,3},{4,20},{20... | collective-permute-start | bytes 786440 | tf_op jit(solution)/shard_map/ppermute | solution.py:445
  140.8 4.3 %means.3.refs_5_.refs_6_ = f32[896,256]{1,0:T(8,128)S(1)} custom-call(bf16[896,256]{1,0:T(8,128)(2,1)S(1)} %collective-permute-done.14.grads.refs_3_.refs_4_, bf16[128,4096]{1,0:T(8,128)(2,1)S(1)} %slice_dynamic-update-slice_fusion.1.x.refs_7_.refs_8_), custom_call_target="tpu_custom_call" | custom-call | flops 1879048192 | bytes 1048576 | tf_op jit(solution)/shard_map/means/pallas_call | solution.py:241
  145.1 1.8 %prepare.1 = (bf16[64,2048]{1,0:T(8,128)(2,1)S(1)}, bf16[64,2048]{1,0:T(8,128)(2,1)S(1)}) custom-call(s32[1]{0:T(128)} %bitcast.refs_0_, bf16[896,4096]{1,0:T(8,128)(2,1)} %bitcast.71, bf16[896,256]{1,0:T(8,128)(2,1)S(1)} %backward.1.grads.refs_2_.refs_3_, bf16[896,256]{1,0:T(8,128)(2,1)S(1)} %collective-permute-done.14.grads.refs_3_.refs_4_, ...), custom_call_target="tpu_custom_call" | custom-call | flops 67108864 | bytes 786432 | tf_op jit(solution)/shard_map/prepare/pallas_call | solution.py:354
  146.9 2.5 %merge.6.refs_9_ = bf16[896,2048]{1,0:T(8,128)(2,1)} custom-call(s32[1]{0:T(128)} %bitcast.refs_0_, bf16[896,4096]{1,0:T(8,128)(2,1)} %bitcast.77, bf16[128,2048]{1,0:T(8,128)(2,1)S(1)} %collective-permute-done.3.refs_2_, bf16[896,256]{1,0:T(8,128)(2,1)S(1)} %backward.1.grads.refs_2_.refs_3_, ...), custom_call_target="tpu_custom_call" | custom-call | flops 134217728 | bytes 1572864 | tf_op jit(solution)/shard_map/merge/pallas_call | solution.py:300
  149.5 6.2 %merge.8.refs_9_ = bf16[896,2048]{1,0:T(8,128)(2,1)} custom-call(s32[1]{0:T(128)} %bitcast.refs_0_, bf16[896,4096]{1,0:T(8,128)(2,1)} %bitcast.72, bf16[480,2048]{1,0:T(8,128)(2,1)} %collective-permute-done.20.refs_2_, bf16[896,256]{1,0:T(8,128)(2,1)S(1)} %backward.1.grads.refs_2_.refs_3_, ...), custom_call_target="tpu_custom_call" | custom-call | flops 503316480 | bytes 5898240 | tf_op jit(solution)/shard_map/merge/pallas_call | solution.py:300
  155.7 7.9 %merge.7 = bf16[896,2048]{1,0:T(8,128)(2,1)} custom-call(s32[1]{0:T(128)} %bitcast.refs_0_, bf16[896,4096]{1,0:T(8,128)(2,1)} %bitcast.78, bf16[768,2048]{1,0:T(8,128)(2,1)} %collective-permute-done.19.refs_2_, bf16[896,256]{1,0:T(8,128)(2,1)S(1)} %backward.1.grads.refs_2_.refs_3_, ...), custom_call_target="tpu_custom_call", output_to_operand_aliasing={{}: (9, {})} | custom-call | flops 805306368 | bytes 9437184 | tf_op jit(solution)/shard_map/merge/pallas_call | solution.py:300
  163.5 2.3 %merge.9.refs_9_ = bf16[896,2048]{1,0:T(8,128)(2,1)} custom-call(s32[1]{0:T(128)} %bitcast.refs_0_, bf16[896,4096]{1,0:T(8,128)(2,1)} %bitcast.73, bf16[96,2048]{1,0:T(8,128)(2,1)S(1)} %collective-permute-done.21.refs_2_, bf16[896,256]{1,0:T(8,128)(2,1)S(1)} %backward.1.grads.refs_2_.refs_3_, ...), custom_call_target="tpu_custom_call", output_to_operand_aliasing={{}: (9, {})} | custom-call | flops 100663296 | bytes 1179648 | tf_op jit(solution)/shard_map/merge/pallas_call | solution.py:300
  165.8 2.5 %merge.10.refs_9_ = bf16[896,2048]{1,0:T(8,128)(2,1)} custom-call(s32[1]{0:T(128)} %bitcast.refs_0_, bf16[896,4096]{1,0:T(8,128)(2,1)} %bitcast.74, bf16[128,2048]{1,0:T(8,128)(2,1)S(1)} %collective-permute-done.22.refs_2_, bf16[896,256]{1,0:T(8,128)(2,1)S(1)} %backward.1.grads.refs_2_.refs_3_, ...), custom_call_target="tpu_custom_call", output_to_operand_aliasing={{}: (9, {})} | custom-call | flops 134217728 | bytes 1572864 | tf_op jit(solution)/shard_map/merge/pallas_call | solution.py:300
  169.6 2.5 %merge.11.refs_2_ = bf16[896,2048]{1,0:T(8,128)(2,1)} custom-call(s32[1]{0:T(128)} %bitcast.refs_0_, bf16[896,4096]{1,0:T(8,128)(2,1)} %bitcast.75, bf16[128,2048]{1,0:T(8,128)(2,1)S(1)} %collective-permute-done.23.refs_2_, bf16[896,256]{1,0:T(8,128)(2,1)S(1)} %backward.1.grads.refs_2_.refs_3_, ...), custom_call_target="tpu_custom_call", output_to_operand_aliasing={{}: (9, {})} | custom-call | flops 134217728 | bytes 1572864 | tf_op jit(solution)/shard_map/merge/pallas_call | solution.py:300
  172.1 2.0 %collective-permute-done.24.refs_1_ = bf16[64,2048]{1,0:T(8,128)(2,1)S(1)} collective-permute-done((bf16[64,2048]{1,0:T(8,128)(2,1)S(1)}, bf16[64,2048]{1,0:T(8,128)(2,1)S(1)}, u32[]{:S(2)}, u32[]{:S(2)}) %collective-permute-start.24) | collective-permute-done | bytes 262176 | tf_op jit(solution)/shard_map/ppermute | solution.py:445
  (84 shorter events, 27.5 us)
Async XLA Ops:
  0.6 5.8 %collective-permute-start = (bf16[8,4096]{1,0:T(8,128)(2,1)}, bf16[8,4096]{1,0:T(8,128)(2,1)S(1)}, u32[]{:S(2)}, u32[]{:S(2)}) collective-permute-start(bf16[8,4096]{1,0:T(8,128)(2,1)} %bitcast.81), channel_id=1, source_target_pairs={{0,16},{16,0},{1,17},{17,1},{2,18},{18,2},{3,19},{19,3},{4,20},{20... | collective-permute-start | bytes 196616 | tf_op jit(solution)/shard_map/ppermute | solution.py:445
  4.7 10.6 %copy-start.5 = (bf16[1,8,4096]{2,1,0:T(8,128)(2,1)S(1)}, bf16[1,8,4096]{2,1,0:T(8,128)(2,1)}, u32[]{:S(2)}) copy-start(bf16[1,8,4096]{2,1,0:T(8,128)(2,1)} %param.6) | copy-start | bytes 196612
  4.7 24.7 %collective-permute-start.3 = (bf16[128,2048]{1,0:T(8,128)(2,1)S(1)}, bf16[128,2048]{1,0:T(8,128)(2,1)S(1)}, u32[]{:S(2)}, u32[]{:S(2)}) collective-permute-start(bf16[128,2048]{1,0:T(8,128)(2,1)S(1)} %dynamic-slice_bitcast_fusion.2), channel_id=1, source_target_pairs={{0,16},{16,0},{1,17},{17,1},{2,18},{18,2},{3,19},{19,3},{4,20},{20... | collective-permute-start | bytes 1572872 | tf_op jit(solution)/shard_map/ppermute | solution.py:445
  6.4 9.3 %collective-permute-start.15 = (bf16[8,4096]{1,0:T(8,128)(2,1)S(1)}, bf16[8,4096]{1,0:T(8,128)(2,1)S(1)}, u32[]{:S(2)}, u32[]{:S(2)}) collective-permute-start(bf16[8,4096]{1,0:T(8,128)(2,1)S(1)} %collective-permute-done), channel_id=1, source_target_pairs={{0,8},{1,9},{2,10},{3,11},{4,12},{5,13},{6,14},{7,15},{8,0},{9,1},... | collective-permute-start | bytes 196616 | tf_op jit(solution)/shard_map/ppermute | solution.py:48
  13.2 142.5 %collective-permute-start.19 = (bf16[768,2048]{1,0:T(8,128)(2,1)}, bf16[768,2048]{1,0:T(8,128)(2,1)}, u32[]{:S(2)}, u32[]{:S(2)}) collective-permute-start(bf16[768,2048]{1,0:T(8,128)(2,1)} %dynamic-slice_bitcast_fusion), channel_id=1, source_target_pairs={{0,16},{16,0},{1,17},{17,1},{2,18},{18,2},{3,19},{19,3},{4,20},{20... | collective-permute-start | bytes 9437192 | tf_op jit(solution)/shard_map/ppermute | solution.py:445
  15.3 7.6 %collective-permute-start.1 = (bf16[8,4096]{1,0:T(8,128)(2,1)S(1)}, bf16[8,4096]{1,0:T(8,128)(2,1)S(1)}, u32[]{:S(2)}, u32[]{:S(2)}) collective-permute-start(bf16[8,4096]{1,0:T(8,128)(2,1)S(1)} %bitcast.82), channel_id=1, source_target_pairs={{0,8},{1,3},{2,10},{3,1},{4,12},{5,7},{6,14},{7,5},{8,0},{9,11},{1... | collective-permute-start | bytes 196616 | tf_op jit(solution)/shard_map/ppermute | solution.py:48
  15.7 7.3 %collective-permute-start.16 = (bf16[16,4096]{1,0:T(8,128)(2,1)S(1)}, bf16[16,4096]{1,0:T(8,128)(2,1)S(1)}, u32[]{:S(2)}, u32[]{:S(2)}) collective-permute-start(bf16[16,4096]{1,0:T(8,128)(2,1)S(1)} %maximum_select_fusion.10), channel_id=1, source_target_pairs={{0,4},{1,5},{2,6},{3,7},{4,0},{5,1},{6,2},{7,3},{8,12},{9,13},{10,... | collective-permute-start | bytes 393224 | tf_op jit(solution)/shard_map/ppermute | solution.py:48
  22.9 6.4 %collective-permute-start.2 = (bf16[16,4096]{1,0:T(8,128)(2,1)S(1)}, bf16[16,4096]{1,0:T(8,128)(2,1)S(1)}, u32[]{:S(2)}, u32[]{:S(2)}) collective-permute-start(bf16[16,4096]{1,0:T(8,128)(2,1)S(1)} %maximum_select_fusion.9), channel_id=1, source_target_pairs={{0,4},{1,9},{2,6},{3,11},{4,0},{5,13},{6,2},{7,15},{8,12},{9,1},{1... | collective-permute-start | bytes 393224 | tf_op jit(solution)/shard_map/ppermute | solution.py:48
  23.1 8.0 %collective-permute-start.17 = (bf16[32,4096]{1,0:T(8,128)(2,1)S(1)}, bf16[32,4096]{1,0:T(8,128)(2,1)S(1)}, u32[]{:S(2)}, u32[]{:S(2)}) collective-permute-start(bf16[32,4096]{1,0:T(8,128)(2,1)S(1)} %maximum_select_fusion.8), channel_id=1, source_target_pairs={{0,2},{1,3},{2,0},{3,1},{4,6},{5,7},{6,4},{7,5},{8,10},{9,11},{10,... | collective-permute-start | bytes 786440 | tf_op jit(solution)/shard_map/ppermute | solution.py:48
  29.4 9.7 %copy-start.6 = (s32[1,2,896]{2,1,0:T(2,128)S(1)}, s32[1,2,896]{2,1,0:T(2,128)}, u32[]{:S(2)}) copy-start(s32[1,2,896]{2,1,0:T(2,128)} %param.11) | copy-start | bytes 21508
  29.4 6.4 %collective-permute-start.4 = (bf16[32,4096]{1,0:T(8,128)(2,1)S(1)}, bf16[32,4096]{1,0:T(8,128)(2,1)S(1)}, u32[]{:S(2)}, u32[]{:S(2)}) collective-permute-start(bf16[32,4096]{1,0:T(8,128)(2,1)S(1)} %maximum_select_fusion.6), channel_id=1, source_target_pairs={{0,2},{1,5},{2,0},{3,7},{4,6},{5,1},{6,4},{7,3},{8,10},{9,13},{10,... | collective-permute-start | bytes 786440 | tf_op jit(solution)/shard_map/ppermute | solution.py:48
  31.1 8.2 %collective-permute-start.18 = (bf16[64,4096]{1,0:T(8,128)(2,1)S(1)}, bf16[64,4096]{1,0:T(8,128)(2,1)S(1)}, u32[]{:S(2)}, u32[]{:S(2)}) collective-permute-start(bf16[64,4096]{1,0:T(8,128)(2,1)S(1)} %maximum_select_fusion.5), channel_id=1, source_target_pairs={{0,1},{1,0},{2,3},{3,2},{4,5},{5,4},{6,7},{7,6},{8,9},{9,8},{10,11... | collective-permute-start | bytes 1572872 | tf_op jit(solution)/shard_map/ppermute | solution.py:467
  36.0 3.6 %collective-permute-start.5 = (bf16[64,4096]{1,0:T(8,128)(2,1)S(1)}, bf16[64,4096]{1,0:T(8,128)(2,1)}, u32[]{:S(2)}, u32[]{:S(2)}) collective-permute-start(bf16[64,4096]{1,0:T(8,128)(2,1)S(1)} %maximum_select_fusion.3), channel_id=1, source_target_pairs={{0,1},{1,0},{2,3},{3,2},{4,5},{5,4},{6,7},{7,6},{8,9},{9,8},{10,11... | collective-permute-start | bytes 1572872 | tf_op jit(solution)/shard_map/ppermute | solution.py:467
  39.1 1.9 %copy-start.4 = (s32[1,2,4096]{2,1,0:T(2,128)S(1)}, s32[1,2,4096]{2,1,0:T(2,128)}, u32[]{:S(2)}) copy-start(s32[1,2,4096]{2,1,0:T(2,128)} %param.10) | copy-start | bytes 98308
  39.1 99.9 %collective-permute-start.20 = (bf16[480,2048]{1,0:T(8,128)(2,1)}, bf16[480,2048]{1,0:T(8,128)(2,1)}, u32[]{:S(2)}, u32[]{:S(2)}) collective-permute-start(bf16[480,2048]{1,0:T(8,128)(2,1)} %dynamic-slice_bitcast_fusion.1), channel_id=1, source_target_pairs={{0,16},{16,0},{1,17},{17,1},{2,18},{18,2},{3,19},{19,3},{4,20},{20... | collective-permute-start | bytes 5898248 | tf_op jit(solution)/shard_map/ppermute | solution.py:445
  54.6 0.8 copy-start
  55.4 12.5 %copy-start.2 = (f32[896,128]{1,0:T(8,128)}, f32[896,128]{1,0:T(8,128)S(1)}, u32[]{:S(2)}) copy-start(f32[896,128]{1,0:T(8,128)S(1)} %get-tuple-element.45.sd) | copy-start | bytes 1376260
  55.4 2.8 %collective-permute-start.6 = (bf16[128,4096]{1,0:T(8,128)(2,1)S(1)}, bf16[128,4096]{1,0:T(8,128)(2,1)S(1)}, u32[]{:S(2)}, u32[]{:S(2)}) collective-permute-start(bf16[128,4096]{1,0:T(8,128)(2,1)S(1)} %get-tuple-element.41), channel_id=1, source_target_pairs={{0,1},{1,0},{2,3},{3,2},{4,5},{5,4},{6,7},{7,6},{8,9},{9,8},{10,11... | collective-permute-start | bytes 3145736 | tf_op jit(solution)/shard_map/ppermute | solution.py:500
  58.4 9.2 %collective-permute-start.7 = (bf16[64,4096]{1,0:T(8,128)(2,1)S(1)}, bf16[64,4096]{1,0:T(8,128)(2,1)S(1)}, u32[]{:S(2)}, u32[]{:S(2)}) collective-permute-start(bf16[64,4096]{1,0:T(8,128)(2,1)S(1)} %constant_dynamic-slice_fusion.2), channel_id=1, source_target_pairs={{0,2},{1,5},{2,0},{3,7},{4,6},{5,1},{6,4},{7,3},{8,10},{9,13},{10,... | collective-permute-start | bytes 1572872 | tf_op jit(solution)/shard_map/ppermute | solution.py:48
  67.9 9.1 %collective-permute-start.8 = (bf16[32,4096]{1,0:T(8,128)(2,1)S(1)}, bf16[32,4096]{1,0:T(8,128)(2,1)S(1)}, u32[]{:S(2)}, u32[]{:S(2)}) collective-permute-start(bf16[32,4096]{1,0:T(8,128)(2,1)S(1)} %constant_dynamic-slice_fusion.1), channel_id=1, source_target_pairs={{0,4},{1,9},{2,6},{3,11},{4,0},{5,13},{6,2},{7,15},{8,12},{9,1},{1... | collective-permute-start | bytes 786440 | tf_op jit(solution)/shard_map/ppermute | solution.py:48
  77.0 6.3 %collective-permute-start.9 = (bf16[16,4096]{1,0:T(8,128)(2,1)S(1)}, bf16[16,4096]{1,0:T(8,128)(2,1)S(1)}, u32[]{:S(2)}, u32[]{:S(2)}) collective-permute-start(bf16[16,4096]{1,0:T(8,128)(2,1)S(1)} %constant_dynamic-slice_fusion), channel_id=1, source_target_pairs={{0,8},{1,3},{2,10},{3,1},{4,12},{5,7},{6,14},{7,5},{8,0},{9,11},{1... | collective-permute-start | bytes 393224 | tf_op jit(solution)/shard_map/ppermute | solution.py:48
  83.4 10.5 %collective-permute-start.10 = (bf16[16,4096]{1,0:T(8,128)(2,1)S(1)}, bf16[16,4096]{1,0:T(8,128)(2,1)S(1)}, u32[]{:S(2)}, u32[]{:S(2)}) collective-permute-start(bf16[16,4096]{1,0:T(8,128)(2,1)S(1)} %add_convert_fusion.3), channel_id=1, source_target_pairs={{0,8},{1,3},{2,10},{3,1},{4,12},{5,7},{6,14},{7,5},{8,0},{9,11},{1... | collective-permute-start | bytes 393224 | tf_op jit(solution)/shard_map/ppermute | solution.py:48
  93.9 7.9 %collective-permute-start.11 = (bf16[32,4096]{1,0:T(8,128)(2,1)S(1)}, bf16[32,4096]{1,0:T(8,128)(2,1)S(1)}, u32[]{:S(2)}, u32[]{:S(2)}) collective-permute-start(bf16[32,4096]{1,0:T(8,128)(2,1)S(1)} %maximum_select_fusion.7), channel_id=1, source_target_pairs={{0,4},{1,9},{2,6},{3,11},{4,0},{5,13},{6,2},{7,15},{8,12},{9,1},{1... | collective-permute-start | bytes 786440 | tf_op jit(solution)/shard_map/ppermute | solution.py:48
  102.7 9.5 %collective-permute-start.12 = (bf16[64,4096]{1,0:T(8,128)(2,1)}, bf16[64,4096]{1,0:T(8,128)(2,1)}, u32[]{:S(2)}, u32[]{:S(2)}) collective-permute-start(bf16[64,4096]{1,0:T(8,128)(2,1)} %maximum_select_fusion.4), channel_id=1, source_target_pairs={{0,2},{1,5},{2,0},{3,7},{4,6},{5,1},{6,4},{7,3},{8,10},{9,13},{10,... | collective-permute-start | bytes 1572872 | tf_op jit(solution)/shard_map/ppermute | solution.py:48
  104.2 14.5 %copy-start.1 = (f32[896,128]{1,0:T(8,128)S(1)}, f32[896,128]{1,0:T(8,128)}, u32[]{:S(2)}) copy-start(f32[896,128]{1,0:T(8,128)} %copy-done) | copy-start | bytes 1376260
  104.2 14.5 %copy-start.3 = (f32[896,128]{1,0:T(8,128)S(1)}, f32[896,128]{1,0:T(8,128)}, u32[]{:S(2)}) copy-start(f32[896,128]{1,0:T(8,128)} %copy-done.2) | copy-start | bytes 1376260
  114.0 4.7 %collective-permute-start.13 = (bf16[128,4096]{1,0:T(8,128)(2,1)S(1)}, bf16[128,4096]{1,0:T(8,128)(2,1)S(1)}, u32[]{:S(2)}, u32[]{:S(2)}) collective-permute-start(bf16[128,4096]{1,0:T(8,128)(2,1)S(1)} %maximum_select_fusion.1.mine), channel_id=1, source_target_pairs={{0,1},{1,0},{2,3},{3,2},{4,5},{5,4},{6,7},{7,6},{8,9},{9,8},{10,11... | collective-permute-start | bytes 3145736 | tf_op jit(solution)/shard_map/ppermute | solution.py:503
  123.2 15.5 %collective-permute-start.14 = (bf16[896,256]{1,0:T(8,128)(2,1)S(1)}, bf16[896,256]{1,0:T(8,128)(2,1)S(1)}, u32[]{:S(2)}, u32[]{:S(2)}) collective-permute-start(bf16[896,256]{1,0:T(8,128)(2,1)S(1)} %backward.1.grads.refs_2_.refs_3_), channel_id=1, source_target_pairs={{0,16},{16,0},{1,17},{17,1},{2,18},{18,2},{3,19},{19,3},{4,20},{20... | collective-permute-start | bytes 1376264 | tf_op jit(solution)/shard_map/ppermute | solution.py:445
  131.4 32.2 %collective-permute-start.21 = (bf16[96,2048]{1,0:T(8,128)(2,1)S(1)}, bf16[96,2048]{1,0:T(8,128)(2,1)S(1)}, u32[]{:S(2)}, u32[]{:S(2)}) collective-permute-start(bf16[96,2048]{1,0:T(8,128)(2,1)S(1)} %get-tuple-element.53), channel_id=1, source_target_pairs={{0,16},{16,0},{1,17},{17,1},{2,18},{18,2},{3,19},{19,3},{4,20},{20... | collective-permute-start | bytes 1179656 | tf_op jit(solution)/shard_map/ppermute | solution.py:445
  131.5 34.3 %collective-permute-start.22 = (bf16[128,2048]{1,0:T(8,128)(2,1)S(1)}, bf16[128,2048]{1,0:T(8,128)(2,1)S(1)}, u32[]{:S(2)}, u32[]{:S(2)}) collective-permute-start(bf16[128,2048]{1,0:T(8,128)(2,1)S(1)} %get-tuple-element.59), channel_id=1, source_target_pairs={{0,16},{16,0},{1,17},{17,1},{2,18},{18,2},{3,19},{19,3},{4,20},{20... | collective-permute-start | bytes 1572872 | tf_op jit(solution)/shard_map/ppermute | solution.py:445
  138.7 30.9 %collective-permute-start.23 = (bf16[128,2048]{1,0:T(8,128)(2,1)S(1)}, bf16[128,2048]{1,0:T(8,128)(2,1)S(1)}, u32[]{:S(2)}, u32[]{:S(2)}) collective-permute-start(bf16[128,2048]{1,0:T(8,128)(2,1)S(1)} %get-tuple-element.65), channel_id=1, source_target_pairs={{0,16},{16,0},{1,17},{17,1},{2,18},{18,2},{3,19},{19,3},{4,20},{20... | collective-permute-start | bytes 1572872 | tf_op jit(solution)/shard_map/ppermute | solution.py:445
  139.0 35.0 %collective-permute-start.24 = (bf16[64,2048]{1,0:T(8,128)(2,1)S(1)}, bf16[64,2048]{1,0:T(8,128)(2,1)S(1)}, u32[]{:S(2)}, u32[]{:S(2)}) collective-permute-start(bf16[64,2048]{1,0:T(8,128)(2,1)S(1)} %pad_maximum_fusion), channel_id=1, source_target_pairs={{0,16},{16,0},{1,17},{17,1},{2,18},{18,2},{3,19},{19,3},{4,20},{20... | collective-permute-start | bytes 786440 | tf_op jit(solution)/shard_map/ppermute | solution.py:445
